TPU v7x, 128 devices: a whole 4x4x4 slice. The times are simulated.
128 devices in a mesh: dp: 4 (over x), seq: 2 (over y_hi), tensor: 16 (over z, y_lo, core).
Axes of the slice: x: 4, y: 4 (y_hi: 2, y_lo: 2; y = y_hi * 2 + y_lo), z: 4, core: 2. Of those that a mesh axis runs over, the one named last changes fastest.
Arguments:
- captured: bfloat16 [3, 4, 256, 8192], P(None, 'dp', 'seq', 'tensor'), may hold values from -6 to 6
- target_logits: bfloat16 [4, 256, 16384], P('dp', 'seq', 'tensor'), may hold values from -400 to 400
- unite_weight: bfloat16 [3, 8192, 8192], P(None, 'tensor', ('dp', 'seq')), may hold values from -0.0390625 to 0.0390625
- norm_gain: float32 [8192], replicated, may hold values from 0.1 to 1.9
- head_weight: bfloat16 [16384, 8192], P('tensor'), may hold values from -32 to 32
- lengths: int32 [4], P('dp'), may hold values from 1 to 256, 640 in all
- loss_mask: int32 [4, 256], P('dp', 'seq'), may hold values 0 or 1
Outputs:
- seq_kl: float32 [4], P('dp')
- unite_grad: float32 [3, 8192, 8192], P(None, 'tensor', ('dp', 'seq'))
Inputs may be any that keep to these rules, and one draw needn't show every extreme that they name: `lengths`: some sequence has all 256 positions valid.
All inputs are finite; a program needn't handle non-finite values. No bound on the sum of `lengths` or of `loss_mask` on one device may be relied on, other than what follows from the above.
Results may differ from a plain program's by a relative error of at most 0.02.
Values may be sent and summed in bfloat16 or wider, within the bound.
No kernel may reach another device: no remote copies, remote signals or barrier semaphores. Data moves between devices by JAX's collectives and lax.ppermute only.
A program may use at most 128 MiB of HBM per device.

v0:
```python
import jax
import jax.numpy as jnp
from jax import lax
from jax.sharding import PartitionSpec as P

NORM_EPS = 1e-05


def merged_2(part, axis, combine):
    gathered = jax.tree.map(lambda a: lax.all_gather(a, axis), part)

    def take(source):
        return jax.tree.map(lambda a: lax.dynamic_index_in_dim(a, source, 0, False), gathered)

    return lax.fori_loop(
        1, lax.axis_size(axis), lambda source, state: combine(state, take(source)), take(0)
    )


def stat_combine(earlier, latter):
    top_target = jnp.maximum(earlier[0], latter[0])
    left_target = jnp.exp(earlier[0] - top_target)
    right_target = jnp.exp(latter[0] - top_target)
    top_draft = jnp.maximum(earlier[3], latter[3])
    left_draft = jnp.exp(earlier[3] - top_draft)
    right_draft = jnp.exp(latter[3] - top_draft)
    merged = (
        top_target,
        earlier[1] * left_target + latter[1] * right_target,
        earlier[2] * left_target + latter[2] * right_target,
        top_draft,
        earlier[4] * left_draft + latter[4] * right_draft,
    )
    if len(earlier) > 5:
        merged = merged + (earlier[5] + latter[5],)
    return merged


def local_stats(target, draft_logits):
    top_target = jnp.max(target, axis=-1)
    target_powers = jnp.exp(target - top_target[:, None])
    sum_target = jnp.sum(target_powers, axis=-1)
    numerator = jnp.sum(target_powers * (target - draft_logits), axis=-1)
    top_draft = jnp.max(draft_logits, axis=-1)
    sum_draft = jnp.sum(jnp.exp(draft_logits - top_draft[:, None]), axis=-1)
    return (top_target, sum_target, numerator, top_draft, sum_draft)


def row_divergence(stat_tuple):
    return (
        stat_tuple[2] / stat_tuple[1]
        - stat_tuple[0]
        - jnp.log(stat_tuple[1])
        + stat_tuple[3]
        + jnp.log(stat_tuple[4])
    )


def normalize(united_rows, gain_blocks, model_width):
    values = united_rows.astype(jnp.float32)
    row_scale = lax.rsqrt(jnp.sum(values * values, axis=(0, 2)) / model_width + NORM_EPS)
    normed = (values * row_scale[None, :, None] * gain_blocks).astype(jnp.bfloat16)
    return (row_scale, normed)


def norm_backward(united_rows, row_scale, gain_blocks, grad_normed, model_width):
    values = united_rows.astype(jnp.float32)
    scaled = grad_normed * gain_blocks
    row_inner = jnp.sum(values * scaled, axis=(0, 2))
    cubic = row_scale * row_scale * row_scale * row_inner / model_width
    return (row_scale[None, :, None] * scaled - cubic[None, :, None] * values).astype(jnp.bfloat16)


def tensor_total(partial_value):
    return lax.psum(partial_value, "tensor")


def relay_blocks(blocks):
    return lax.all_to_all(blocks, ("dp", "seq"), split_axis=0, concat_axis=0, tiled=True)


def local(captured, target_logits, unite_weight, norm_gain, head_weight, lengths, loss_mask):
    groups = lax.axis_size("dp") * lax.axis_size("seq")
    seq_local = captured.shape[1]
    half_len = captured.shape[2]
    group_rows = seq_local * half_len
    model_width = norm_gain.shape[0]
    block_cols = unite_weight.shape[2]
    vocab_local = head_weight.shape[0]
    gathered = lax.all_gather(captured, ("dp", "seq"), axis=1, tiled=True)
    streams_all = gathered.reshape(3, groups * group_rows, gathered.shape[3])
    gain_blocks = norm_gain.reshape(groups, 1, block_cols)
    head_blocks = head_weight.reshape(vocab_local, groups, block_cols)
    partial_value = jnp.einsum(
        "sgk,skn->gn", streams_all, unite_weight, preferred_element_type=jnp.float32
    )
    united_cols = tensor_total(partial_value).astype(jnp.bfloat16)
    united_rows = relay_blocks(united_cols.reshape(groups, group_rows, block_cols))
    row_scale, normed = normalize(united_rows, gain_blocks, model_width)
    draft_logits = jnp.einsum(
        "crn,vcn->rv", normed, head_blocks, preferred_element_type=jnp.float32
    )
    target = target_logits.reshape(group_rows, vocab_local).astype(jnp.float32)
    seq_half = lax.axis_index("seq")
    dp_index = lax.axis_index("dp")
    positions = seq_half * half_len + lax.broadcasted_iota(jnp.int32, (seq_local, half_len), 1)
    valid_flags = (
        ((positions < lengths[:, None]) & (loss_mask == 1)).astype(jnp.float32).reshape(group_rows)
    )
    stat_tuple = local_stats(target, draft_logits)
    seq_count = lax.axis_size("dp") * seq_local
    own_stats = merged_2(stat_tuple, "tensor", stat_combine)
    kl_rows = row_divergence(own_stats)
    kl_seq = jnp.sum((kl_rows * valid_flags).reshape(seq_local, half_len), axis=1)
    count_seq = jnp.sum(valid_flags.reshape(seq_local, half_len), axis=1)
    slot_match = lax.broadcasted_iota(
        jnp.int32, (seq_count, seq_local), 0
    ) == dp_index * seq_local + lax.broadcasted_iota(jnp.int32, (seq_count, seq_local), 1)
    kl_part = jnp.sum(jnp.where(slot_match, kl_seq[None, :], 0.0), axis=1)
    count_part = jnp.sum(jnp.where(slot_match, count_seq[None, :], 0.0), axis=1)
    kl_all, count_all = lax.psum((kl_part, count_part), ("dp", "seq"))
    seq_length = half_len * lax.axis_size("seq")
    factor = seq_length / jnp.maximum(jnp.sum(count_all), 1.0)
    own_kl = lax.dynamic_slice_in_dim(kl_all, dp_index * seq_local, seq_local)
    own_count = lax.dynamic_slice_in_dim(count_all, dp_index * seq_local, seq_local)
    seq_kl = own_kl / jnp.maximum(own_count, 1.0)
    target_prob = jnp.exp(target - (own_stats[0] + jnp.log(own_stats[1]))[:, None])
    draft_prob = jnp.exp(draft_logits - (own_stats[3] + jnp.log(own_stats[4]))[:, None])
    grad_logits = (valid_flags[:, None] * (draft_prob - target_prob)).astype(jnp.bfloat16)
    grad_partial = jnp.einsum(
        "rv,vcn->crn", grad_logits, head_blocks, preferred_element_type=jnp.float32
    )
    grad_normed = tensor_total(grad_partial)
    grad_united = norm_backward(united_rows, row_scale, gain_blocks, grad_normed, model_width)
    grad_cols = relay_blocks(grad_united)
    grad_flat = grad_cols.reshape(groups * group_rows, block_cols)
    weight_grad = jnp.einsum(
        "sgk,gn->skn", streams_all, grad_flat, preferred_element_type=jnp.float32
    )
    unite_grad = weight_grad * factor
    return (seq_kl, unite_grad)


def solution(mesh):
    placed = (
        P(None, "dp", "seq", "tensor"),
        P("dp", "seq", "tensor"),
        P(None, "tensor", ("dp", "seq")),
        P(),
        P("tensor", None),
        P("dp"),
        P("dp", "seq"),
    )
    return jax.shard_map(
        local,
        mesh=mesh,
        in_specs=placed,
        out_specs=(P("dp"), P(None, "tensor", ("dp", "seq"))),
        check_vma=False,
    )
```

profile of v0, /device:TPU:1, one launch (start us, length us, event | category | flops | bytes accessed | tf_op | source)
XLA Modules:
  0.0 529.2 jit_solution(5826818035555718092)
XLA Ops:
  7.2 0.7 all-gather.12.cloned.1.call-update
  7.9 68.3 %all-gather.12.cloned.1.call-done = bf16[3,8,128,512]{3,2,1,0:T(8,128)(2,1)} async-done(((bf16[3,1,128,512]{3,2,1,0:T(8,128)(2,1)}), bf16[3,8,128,512]{3,2,1,0:T(8,128)(2,1)}) %all-gather.12.cloned.1.call-update) | async-done | bytes 3145744 | tf_op jit(solution)/shard_map/all_gather | solution.py:90
  76.2 6.8 %convolution_bitcast_fusion = f32[1024,1024]{1,0:T(8,128)} fusion(bf16[3,1024,512]{2,1,0:T(8,128)(2,1)} %bitcast.120, bf16[3,512,1024]{2,1,0:T(8,128)(2,1)S(1)} %copy-done), kind=kOutput, calls=%fused_computation.39 | convolution fusion | flops 3221225472 | bytes 10485760 | tf_op jit(solution)/shard_map/sgk,skn->gn/dot_general | solution.py:94
  83.0 95.6 %all-reduce.5 = bf16[1024,1024]{1,0:T(8,128)(2,1)} all-reduce(f32[1024,1024]{1,0:T(8,128)} %convolution_bitcast_fusion), channel_id=1, replica_groups=mesh['dp'=4,'seq'=2,'tensor'=16] {'tensor'}, use_global_device_ids=true, to_apply=%region_2.0 | all-reduce | flops 1048576 | bytes 6291456 | tf_op jit(solution)/shard_map/psum | solution.py:75
  178.6 4.4 all-to-all-start
  183.9 32.6 %all-gather.5 = f32[16,1,128]{2,1,0:T(1,128)S(1)} all-gather(f32[1,1,128]{2,1,0:T(1,128)S(1)} %get-tuple-element.317), channel_id=2, replica_groups=mesh['dp'=4,'seq'=2,'tensor'=16] {'tensor'}, dimensions={0}, use_global_device_ids=true | all-gather | bytes 8704 | tf_op jit(solution)/shard_map/all_gather | solution.py:10
  217.1 2.1 fusion.20
  219.2 12.9 %fusion.58 = (f32[128]{0:T(128)S(1)}, f32[128,1024]{1,0:T(8,128)}) fusion(bf16[128,8,8,1024]{3,2,1,0:T(8,128)(2,1)} %bitcast.118, bf16[8,128,1024]{2,1,0:T(8,128)(2,1)} %all-to-all-done, f32[8,1024]{1,0:T(8,128)S(1)} %mul.154, f32[128]{0:T(128)S(1)} %add_rsqrt_fusion), kind=kOutput, calls=%fused_computation.79 | convolution fusion | flops 2151809024 | bytes 19432448 | tf_op jit(solution)/shard_map/crn,vcn->rv/dot_general | solution.py:100
  232.1 1.4 exponential_reduce_fusion
  233.5 16.1 %all-gather.7 = f32[16,1,128]{2,1,0:T(1,128)S(1)} all-gather(f32[1,1,128]{2,1,0:T(1,128)S(1)} %bitcast.117), channel_id=4, replica_groups=mesh['dp'=4,'seq'=2,'tensor'=16] {'tensor'}, dimensions={0}, use_global_device_ids=true | all-gather | bytes 8704 | tf_op jit(solution)/shard_map/all_gather | solution.py:10
  249.6 17.5 %all-gather.9 = f32[16,1,128]{2,1,0:T(1,128)S(1)} all-gather(f32[1,1,128]{2,1,0:T(1,128)S(1)} %bitcast.116), channel_id=6, replica_groups=mesh['dp'=4,'seq'=2,'tensor'=16] {'tensor'}, dimensions={0}, use_global_device_ids=true | all-gather | bytes 8704 | tf_op jit(solution)/shard_map/all_gather | solution.py:10
  267.2 16.1 %all-gather.6 = f32[16,1,128]{2,1,0:T(1,128)S(1)} all-gather(f32[1,1,128]{2,1,0:T(1,128)S(1)} %bitcast.115), channel_id=3, replica_groups=mesh['dp'=4,'seq'=2,'tensor'=16] {'tensor'}, dimensions={0}, use_global_device_ids=true | all-gather | bytes 8704 | tf_op jit(solution)/shard_map/all_gather | solution.py:10
  283.3 17.7 %all-gather.8 = f32[16,1,128]{2,1,0:T(1,128)S(1)} all-gather(f32[1,1,128]{2,1,0:T(1,128)S(1)} %bitcast.114), channel_id=5, replica_groups=mesh['dp'=4,'seq'=2,'tensor'=16] {'tensor'}, dimensions={0}, use_global_device_ids=true | all-gather | bytes 8704 | tf_op jit(solution)/shard_map/all_gather | solution.py:10
  301.0 1.3 while.23
  302.9 10.5 %fusion.26 = f32[8,128,1024]{2,1,0:T(8,128)} fusion(bf16[128,8,8,1024]{3,2,1,0:T(8,128)(2,1)} %bitcast.119, f32[128,1024]{1,0:T(8,128)} %get-tuple-element.319, bf16[1,128,1024]{2,1,0:T(8,128)(2,1)S(1)} %copy-done.2, f32[128]{0:T(128)S(1)} %get-tuple-element.315, f32[128]{0:T(128)S(1)} %get-tuple-element.313, f32[128]{0:T(128)S(1)} %bitcast.113), kind=kOutput, calls=%fused_computation.38 | convolution fusion | flops 2148270080 | bytes 21759488 | tf_op jit(solution)/shard_map/rv,vcn->crn/dot_general | solution.py:130
  313.4 137.3 %all-reduce.4.cloned.1.call-done = f32[8,128,1024]{2,1,0:T(8,128)} async-done(((f32[8,128,1024]{2,1,0:T(8,128)}), f32[8,128,1024]{2,1,0:T(8,128)}) %all-reduce.4.cloned.1.call-update) | async-done | bytes 4194320 | tf_op jit(solution)/shard_map/psum | solution.py:75
  450.7 3.7 fusion.23
  454.7 4.1 fusion.25
  458.8 6.1 %all-to-all-start.1 = ((bf16[8,128,1024]{2,1,0:T(8,128)(2,1)}), bf16[8,128,1024]{2,1,0:T(8,128)(2,1)}, u32[]{:S(2)}, u32[]{:S(2)}) async-start(bf16[8,128,1024]{2,1,0:T(8,128)(2,1)} %fusion.25), calls=%async_computation.1 | async-start | bytes 4194304 | tf_op jit(solution)/shard_map/all_to_all | solution.py:79
  464.9 1.3 compare_select_fusion
  466.2 35.9 %all-reduce = (f32[4]{0:T(128)S(1)}, f32[4]{0:T(128)S(1)}) all-reduce(f32[4]{0:T(128)S(1)} %get-tuple-element.321, f32[4]{0:T(128)S(1)} %get-tuple-element.320), channel_id=1, replica_groups=mesh['dp'=4,'seq'=2,'tensor'=16] {'dp','seq'}, use_global_device_ids=true, to_apply=%region_10.11 | all-reduce | flops 8 | bytes 64 | tf_op jit(solution)/shard_map/psum | solution.py:121
  502.1 0.7 reduce_sum.87
  506.0 8.7 %fusion.19 = f32[3,512,1024]{1,2,0:T(8,128)} fusion(f32[]{:T(128)S(6)} %div.19, bf16[3,8,128,512]{3,2,1,0:T(8,128)(2,1)} %all-gather.12.cloned.1.call-done, bf16[8,128,1024]{2,1,0:T(8,128)(2,1)} %all-to-all-done.1), kind=kOutput, calls=%fused_computation.31 | convolution fusion | flops 3222798336 | bytes 11534340 | tf_op jit(solution)/shard_map/sgk,gn->skn/dot_general | solution.py:137
  514.7 6.6 %copy.16 = f32[3,512,1024]{2,1,0:T(8,128)} copy(f32[3,512,1024]{1,2,0:T(8,128)} %fusion.19) | data formatting | bytes 12582912
  (74 shorter events, 3.9 us)
Async XLA Ops:
  7.2 69.0 %copy-start = (bf16[3,512,1024]{2,1,0:T(8,128)(2,1)S(1)}, bf16[3,512,1024]{2,1,0:T(8,128)(2,1)}, u32[]{:S(2)}) copy-start(bf16[3,512,1024]{2,1,0:T(8,128)(2,1)} %param.11) | copy-start | bytes 9437188
  7.2 69.0 %all-gather.12.cloned.1.call-start = ((), (), s32[]{:S(2)}) async-start(), calls=%async_computation.2 | async-start | bytes 3538944 | tf_op jit(solution)/shard_map/all_gather | solution.py:90
  83.0 100.7 %copy-start.3 = (f32[8192]{0:T(1024)S(1)}, f32[8192]{0:T(1024)}, u32[]{:S(2)}) copy-start(f32[8192]{0:T(1024)} %param.12) | copy-start | bytes 98308
  83.0 100.7 %copy-start.2 = (bf16[1,128,1024]{2,1,0:T(8,128)(2,1)S(1)}, bf16[1,128,1024]{2,1,0:T(8,128)(2,1)}, u32[]{:S(2)}) copy-start(bf16[1,128,1024]{2,1,0:T(8,128)(2,1)} %param.10) | copy-start | bytes 786436
  83.0 133.4 %copy-start.4 = (s32[1,128]{1,0:T(1,128)S(1)}, s32[1,128]{1,0:T(1,128)}, u32[]{:S(2)}) copy-start(s32[1,128]{1,0:T(1,128)} %param.15) | copy-start | bytes 1540
  178.6 38.4 %all-to-all-start = ((bf16[8,128,1024]{2,1,0:T(8,128)(2,1)}), bf16[8,128,1024]{2,1,0:T(8,128)(2,1)}, u32[]{:S(2)}, u32[]{:S(2)}) async-start(bf16[8,128,1024]{2,1,0:T(8,128)(2,1)} %bitcast.107), calls=%async_computation | async-start | bytes 4194304 | tf_op jit(solution)/shard_map/all_to_all | solution.py:79
  183.0 267.7 %all-reduce.4.cloned.1.call-start = ((), (), s32[]{:S(2)}) async-start(), calls=%async_computation.3 | async-start | bytes 8388608 | tf_op jit(solution)/shard_map/psum | solution.py:75
  450.7 4.0 copy-start.1
  458.8 47.2 %all-to-all-start.1 = ((bf16[8,128,1024]{2,1,0:T(8,128)(2,1)}), bf16[8,128,1024]{2,1,0:T(8,128)(2,1)}, u32[]{:S(2)}, u32[]{:S(2)}) async-start(bf16[8,128,1024]{2,1,0:T(8,128)(2,1)} %fusion.25), calls=%async_computation.1 | async-start | bytes 4194304 | tf_op jit(solution)/shard_map/all_to_all | solution.py:79
Sparse Core Ops, SparseCore 0:
  10.4 65.7 all-gather.11
  313.5 137.1 all-reduce.3
where the time goes:
time: 533 us; the launch traced here: 529 us
  blocking collectives  232 us (44%)
  waiting for transfers between devices  206 us (39%)
  matrix products  38.9 us (7%)
  between operations  17.9 us (3%)
  other arithmetic  15.5 us (3%)
  starting transfers between devices  10.6 us (2%)
  local copies, waits for them, and re-layouts  8.1 us (2%)
    psum x1, waiting for transfers between devices, tensor_total(): return lax.psum(partial_value, 'tensor')  137 us
    all_gather x5, blocking collectives, merged_2(): gathered = jax.tree.map(lambda a: lax.all_gather(a, axis), part)  100 us
    psum x1, blocking collectives, tensor_total(): return lax.psum(partial_value, 'tensor')  95.6 us
    all_gather x1, waiting for transfers between devices, local(): gathered = lax.all_gather(captured, ('dp', 'seq'), axis=1, tiled=True)  68.3 us
    psum x1, blocking collectives, local(): kl_all, count_all = lax.psum((kl_part, count_part), ('dp', 'seq'))  35.9 us
    dot_general x1, matrix products, local(): jnp.einsum('crn,vcn->rv', normed, head_blocks, preferred_element_type=jnp...  12.9 us
  transfers between devices with their start and end apart: 4, of which 2 were waited for; matrix products, arithmetic and copies ran while one was open for 1% of the time, Pallas kernels for 0%

commit v1 on v0

v1 whole, which is shorter than its diff:
```python
import jax
import jax.numpy as jnp
from jax import lax
from jax.sharding import Mesh, PartitionSpec as P

NORM_EPS = 1e-05
GROUP = ("x", "yh")
RING = ("z", "yl")
ALL = ("x", "yh", "z", "yl", "c")


def spread(value, axes, count):
    return lax.all_to_all(
        jnp.broadcast_to(value[None], (count,) + value.shape), axes, 0, 0, tiled=True
    )


def swap_core(value):
    return lax.ppermute(value, "c", [(0, 1), (1, 0)])


def gather_tensor(piece):
    ring = spread(piece, RING, 8)
    other = swap_core(ring)
    first = lax.axis_index("c") == 0
    return jnp.stack([jnp.where(first, ring, other), jnp.where(first, other, ring)], 1)


def local(captured, target_logits, unite_weight, norm_gain, head_weight, lengths, loss_mask):
    f32, bf16 = jnp.float32, jnp.bfloat16
    half_len = captured.shape[2]
    width = norm_gain.shape[0]
    vocab = head_weight.shape[0]
    t_index = lax.axis_index(("z", "yl", "c"))
    streams = spread(captured.reshape(3, half_len, 512), GROUP, 8)

    positions = lax.axis_index("yh") * half_len + lax.iota(jnp.int32, half_len)
    valid = ((positions < lengths[0]) & (loss_mask[0] == 1)).astype(f32)
    count_part = jnp.sum(valid)
    count_all = spread(jnp.full((8, 128), count_part, f32), GROUP, 8)[:, 0, 0]
    factor = (2 * half_len) / jnp.maximum(jnp.sum(count_all), 1.0)
    count_seq = jnp.sum(
        lax.dynamic_slice_in_dim(count_all, lax.axis_index("x") * 2, 2)
    )

    partial = jnp.einsum("gsrk,skn->grn", streams, unite_weight, preferred_element_type=f32)
    pieces = lax.all_to_all(
        partial.astype(bf16).reshape(128, 8, 1024), ALL, 0, 0, tiled=True
    )
    united = jnp.sum(pieces.reshape(8, 16, 8, 1024).astype(f32), axis=1).astype(bf16)
    rows = gather_tensor(united)
    united_rows = rows.reshape(16, 8, 8, 1024).transpose(0, 2, 1, 3).reshape(128, width)

    values = united_rows.astype(f32)
    row_scale = lax.rsqrt(jnp.sum(values * values, axis=1) / width + NORM_EPS)
    normed = (values * row_scale[:, None] * norm_gain[None, :]).astype(bf16)
    logits = lax.dot_general(
        normed, head_weight, (((1,), (1,)), ((), ())), preferred_element_type=f32
    )
    target = target_logits.reshape(half_len, vocab).astype(f32)
    top_t = jnp.max(target, axis=1)
    pow_t = jnp.exp(target - top_t[:, None])
    top_d = jnp.max(logits, axis=1)
    pow_d = jnp.exp(logits - top_d[:, None])
    stats = jnp.stack(
        [
            top_t,
            jnp.sum(pow_t, axis=1),
            jnp.sum(pow_t * target, axis=1),
            jnp.sum(pow_t * logits, axis=1),
            top_d,
            jnp.sum(pow_d, axis=1),
            jnp.sum(pow_d * logits, axis=1),
            jnp.zeros_like(top_d),
        ]
    )
    every = spread(stats, ("z", "yl", "c"), 16)
    max_t = jnp.max(every[:, 0], axis=0)
    scale_t = jnp.exp(every[:, 0] - max_t)
    sum_t = jnp.sum(every[:, 1] * scale_t, axis=0)
    mean_tt = jnp.sum(every[:, 2] * scale_t, axis=0) / sum_t
    mean_tl = jnp.sum(every[:, 3] * scale_t, axis=0) / sum_t
    max_d = jnp.max(every[:, 4], axis=0)
    scale_d = jnp.exp(every[:, 4] - max_d)
    sum_d = jnp.sum(every[:, 5] * scale_d, axis=0)
    mean_dl = jnp.sum(every[:, 6] * scale_d, axis=0) / sum_d
    log_t = max_t + jnp.log(sum_t)
    log_d = max_d + jnp.log(sum_d)
    kl = mean_tt - mean_tl - log_t + log_d
    inner = valid * (mean_dl - mean_tl) / row_scale

    grad_logits = (
        valid[:, None] * (jnp.exp(logits - log_d[:, None]) - jnp.exp(target - log_t[:, None]))
    ).astype(bf16)
    grad_normed = lax.dot_general(
        grad_logits, head_weight, (((1,), (0,)), ((), ())), preferred_element_type=f32
    )
    mine = (lax.iota(jnp.int32, half_len) // 8) == t_index
    cubic = jnp.where(mine, row_scale * row_scale * row_scale * inner / width, 0.0)
    grad_part = (
        grad_normed * row_scale[:, None] * norm_gain[None, :] - cubic[:, None] * values
    ).astype(bf16)
    grad_pieces = lax.all_to_all(
        grad_part.reshape(128, 8, 1024).transpose(1, 0, 2).reshape(128, 8, 1024),
        ALL, 0, 0, tiled=True,
    )
    grad_sum = jnp.sum(grad_pieces.reshape(8, 16, 8, 1024).astype(f32), axis=1).astype(bf16)
    grad_all = gather_tensor(grad_sum).reshape(16, 8, 8, 1024).transpose(1, 0, 2, 3)
    grad_all = grad_all.reshape(8, 128, 1024)
    weight_grad = jnp.einsum("gsrk,grn->skn", streams, grad_all, preferred_element_type=f32)
    unite_grad = weight_grad * factor

    kl_part = jnp.sum(kl * valid)
    kl_all = spread(jnp.full((8, 128), kl_part, f32), ("yh",), 2)[:, 0, 0]
    seq_kl = (jnp.sum(kl_all) / jnp.maximum(count_seq, 1.0)).reshape(1)
    return (seq_kl, unite_grad)


def solution(mesh):
    fine = Mesh(mesh.devices.reshape(4, 2, 4, 2, 2), ALL)
    tensor = ("z", "yl", "c")
    placed = (
        P(None, "x", "yh", tensor),
        P("x", "yh", tensor),
        P(None, tensor, GROUP),
        P(),
        P(tensor, None),
        P("x"),
        P("x", "yh"),
    )
    return jax.shard_map(
        local,
        mesh=fine,
        in_specs=placed,
        out_specs=(P("x"), P(None, tensor, GROUP)),
        check_vma=False,
    )
```

time: 533 us -> 244 us (0.46)
  waiting for transfers between devices: 206 us -> 17.5 us
  blocking collectives: 232 us -> 152 us
  between operations: 17.9 us -> 4.63 us
  other arithmetic: 15.5 us -> 8.31 us
  matrix products: 38.9 us -> 32 us
  local copies, waits for them, and re-layouts: 8.1 us -> 13.7 us
    all_to_all x0 -> x5, blocking collectives: none -> 152 us  [the longest x3 78.5 us: spread(): lax.all_to_all(jnp.broadcast_to(value[None], (count,) + value.shape), axe...]
    psum x1 -> x0, waiting for transfers between devices: 137 us -> none  [tensor_total(): return lax.psum(partial_value, 'tensor')]
    psum x2 -> x0, blocking collectives: 132 us -> none  [the longest x1 95.6 us: tensor_total(): return lax.psum(partial_value, 'tensor')]
    all_gather x5 -> x0, blocking collectives: 100 us -> none  [merged_2(): gathered = jax.tree.map(lambda a: lax.all_gather(a, axis), part)]
    all_gather x1 -> x0, waiting for transfers between devices: 68.3 us -> none  [local(): gathered = lax.all_gather(captured, ('dp', 'seq'), axis=1, tiled=True)]
    all_to_all x2 -> x3, waiting for transfers between devices: 0.01 us -> 15.9 us  [spread(): lax.all_to_all(jnp.broadcast_to(value[None], (count,) + value.shape), axe...]
    dot_general x4, matrix products: 38.9 us -> 32 us  [the longest x1 12.8 us: local(): lax.dot_general(normed, head_weight, (((1,), (1,)), ((), ())), preferred_...]
  transfers between devices with their start and end apart: 4 -> 5, of which waited for: 2 -> 4; matrix products, arithmetic and copies ran while one was open for 1% -> 2% of each run, Pallas kernels for 0% -> 0%
where the time goes in v1:
time: 244 us; the launch traced here: 243 us
  blocking collectives  152 us (62%)
  matrix products  32 us (13%)
  waiting for transfers between devices  17.5 us (7%)
  starting transfers between devices  15 us (6%)
  local copies, waits for them, and re-layouts  13.7 us (6%)
  other arithmetic  8.31 us (3%)
  between operations  4.63 us (2%)
    all_to_all x3, blocking collectives, spread(): lax.all_to_all(jnp.broadcast_to(value[None], (count,) + value.shape), axe...  78.5 us
    all_to_all x1, blocking collectives, local(): lax.all_to_all(partial.astype(bf16).reshape(128, 8, 1024), ALL, 0, 0, til...  38.8 us
    all_to_all x1, blocking collectives, local(): lax.all_to_all(grad_part.reshape(128, 8, 1024).transpose(1, 0, 2).reshape...  34.2 us
    all_to_all x3, waiting for transfers between devices, spread(): lax.all_to_all(jnp.broadcast_to(value[None], (count,) + value.shape), axe...  15.9 us
    dot_general x1, matrix products, local(): lax.dot_general(normed, head_weight, (((1,), (1,)), ((), ())), preferred_...  12.8 us
    all_to_all x3, starting transfers between devices, spread(): lax.all_to_all(jnp.broadcast_to(value[None], (count,) + value.shape), axe...  10.2 us
    dot_general x1, matrix products, local(): lax.dot_general(grad_logits, head_weight, (((1,), (0,)), ((), ())), prefe...  10.2 us
    unnamed x15, local copies, waits for them, and re-layouts  8.41 us
  transfers between devices with their start and end apart: 5, of which 4 were waited for; matrix products, arithmetic and copies ran while one was open for 2% of the time, Pallas kernels for 0%

profile of v1, /device:TPU:1, one launch (start us, length us, event | category | flops | bytes accessed | tf_op | source)
XLA Modules:
  0.0 242.8 jit_solution(11186661143317831072)
XLA Ops:
  0.6 1.5 broadcast_in_dim.12
  2.1 45.2 %all_to_all.40 = bf16[8,3,128,512]{3,2,1,0:T(8,128)(2,1)S(1)} all-to-all(bf16[8,3,128,512]{3,2,1,0:T(8,128)(2,1)S(1)} %broadcast_in_dim.12), channel_id=1, replica_groups=mesh['x'=4,'yh'=2,'z'=4,'yl'=2,'c'=2] {'x','yh'}, dimensions={0} | all-to-all | bytes 6291456 | tf_op jit(solution)/shard_map/all_to_all | solution.py:13
  47.3 3.6 %bitcast_convert_fusion = bf16[8,128,1024]{2,1,0:T(8,128)(2,1)S(1)} fusion(bf16[8,3,128,512]{3,2,1,0:T(8,128)(2,1)S(1)} %all_to_all.40, bf16[3,512,1024]{2,1,0:T(8,128)(2,1)S(1)} %copy-done), kind=kOutput, calls=%fused_computation.6 | convolution fusion | flops 3222274048 | bytes 8388608 | tf_op jit(solution)/shard_map/gsrk,skn->grn/dot_general | solution.py:46
  51.0 38.8 %all_to_all.41 = bf16[128,8,1024]{2,1,0:T(8,128)(2,1)S(1)} all-to-all(bf16[128,8,1024]{2,1,0:T(8,128)(2,1)S(1)} %bitcast.104), channel_id=1, replica_groups=mesh['x'=4,'yh'=2,'z'=4,'yl'=2,'c'=2] {'x','yh','z','yl','c'}, dimensions={0} | all-to-all | bytes 4194304 | tf_op jit(solution)/shard_map/all_to_all | solution.py:47
  90.2 16.7 %all_to_all.42 = bf16[8,8,8,1024]{3,2,1,0:T(8,128)(2,1)S(1)} all-to-all(bf16[8,8,8,1024]{3,2,1,0:T(8,128)(2,1)S(1)} %broadcast_in_dim.13), channel_id=1, replica_groups=mesh['x'=4,'yh'=2,'z'=4,'yl'=2,'c'=2] {'z','yl'}, dimensions={0} | all-to-all | bytes 2097152 | tf_op jit(solution)/shard_map/all_to_all | solution.py:13
  106.9 2.4 collective-permute-start
  110.1 1.6 collective-permute-done
  111.7 1.4 select_bitcast_fusion.3
  113.6 2.3 maximum_convert_fusion
  116.0 12.8 %fusion.34 = (f32[128]{0:T(128)S(1)}, f32[128,1024]{1,0:T(8,128)S(1)}) fusion(bf16[1024,8192]{1,0:T(8,128)(2,1)} %param.11, f32[128,8192]{1,0:T(8,128)} %bitcast.99, f32[8192]{0:T(1024)S(1)} %copy-done.5, f32[128]{0:T(128)S(1)} %rsqrt.14), kind=kOutput, calls=%fused_computation.73 | convolution fusion | flops 2150760448 | bytes 21529600 | tf_op jit(solution)/shard_map/dot_general | solution.py:57
  130.0 3.7 %all-to-all-start.3 = ((f32[16,8,128]{2,1,0:T(8,128)}), f32[16,8,128]{2,1,0:T(8,128)S(1)}, u32[]{:S(2)}, u32[]{:S(2)}) async-start(f32[16,8,128]{2,1,0:T(8,128)} %broadcast_in_dim.14), calls=%async_computation.3 | async-start | bytes 131072 | tf_op jit(solution)/shard_map/all_to_all | solution.py:13
  133.7 5.8 %all-to-all-done.3 = f32[16,8,128]{2,1,0:T(8,128)S(1)} async-done(((f32[16,8,128]{2,1,0:T(8,128)}), f32[16,8,128]{2,1,0:T(8,128)S(1)}, u32[]{:S(2)}, u32[]{:S(2)}) %all-to-all-start.3) | async-done | bytes 65568 | tf_op jit(solution)/shard_map/all_to_all | solution.py:13
  140.3 10.2 %fusion.2 = bf16[128,8192]{1,0:T(8,128)(2,1)S(1)} fusion(bf16[1024,8192]{1,0:T(8,128)(2,1)} %param.11, f32[128,8192]{1,0:T(8,128)} %bitcast.100, f32[128]{0:T(128)S(1)} %get-tuple-element.30, f32[8192]{0:T(1024)S(1)} %copy-done.5, f32[128]{0:T(128)S(1)} %rsqrt.14, f32[128,1024]{1,0:T(8,128)S(1)} %get-tuple-element.50, ...), kind=kOutput, calls=%fused_computation.3 | convolution fusion | flops 2153512960 | bytes 23890432 | tf_op jit(solution)/shard_map/dot_general | solution.py:95
  150.7 34.2 %all_to_all.43 = bf16[128,8,1024]{2,1,0:T(8,128)(2,1)S(1)} all-to-all(bf16[128,8,1024]{2,1,0:T(8,128)(2,1)S(1)} %bitcast.102), channel_id=1, replica_groups=mesh['x'=4,'yh'=2,'z'=4,'yl'=2,'c'=2] {'x','yh','z','yl','c'}, dimensions={0} | all-to-all | bytes 4194304 | tf_op jit(solution)/shard_map/all_to_all | solution.py:103
  185.4 16.7 %all_to_all.44 = bf16[8,8,8,1024]{3,2,1,0:T(8,128)(2,1)S(1)} all-to-all(bf16[8,8,8,1024]{3,2,1,0:T(8,128)(2,1)S(1)} %broadcast_in_dim.15), channel_id=1, replica_groups=mesh['x'=4,'yh'=2,'z'=4,'yl'=2,'c'=2] {'z','yl'}, dimensions={0} | all-to-all | bytes 2097152 | tf_op jit(solution)/shard_map/all_to_all | solution.py:13
  202.1 2.4 collective-permute-start.1
  205.6 3.2 %all-to-all-start.4 = ((f32[2,8,128]{2,1,0:T(8,128)}), f32[2,8,128]{2,1,0:T(8,128)S(1)}, u32[]{:S(2)}, u32[]{:S(2)}) async-start(f32[2,8,128]{2,1,0:T(8,128)} %broadcast_in_dim_broadcast_in_dim_broadcast_in_dim.6), calls=%async_computation.4 | async-start | bytes 16384 | tf_op jit(solution)/shard_map/all_to_all | solution.py:13
  208.9 4.1 %all-to-all-done.4 = f32[2,8,128]{2,1,0:T(8,128)S(1)} async-done(((f32[2,8,128]{2,1,0:T(8,128)}), f32[2,8,128]{2,1,0:T(8,128)S(1)}, u32[]{:S(2)}, u32[]{:S(2)}) %all-to-all-start.4) | async-done | bytes 8224 | tf_op jit(solution)/shard_map/all_to_all | solution.py:13
  213.0 1.3 broadcast_in_dim_broadcast_in_dim_broadcast_in_dim.7
  214.3 3.3 %all-to-all-start.5 = ((f32[8,8,128]{2,1,0:T(8,128)}), f32[8,8,128]{2,1,0:T(8,128)S(1)}, u32[]{:S(2)}, u32[]{:S(2)}) async-start(f32[8,8,128]{2,1,0:T(8,128)} %broadcast_in_dim_broadcast_in_dim_broadcast_in_dim.7), calls=%async_computation.5 | async-start | bytes 65536 | tf_op jit(solution)/shard_map/all_to_all | solution.py:13
  218.2 5.9 %all-to-all-done.5 = f32[8,8,128]{2,1,0:T(8,128)S(1)} async-done(((f32[8,8,128]{2,1,0:T(8,128)}), f32[8,8,128]{2,1,0:T(8,128)S(1)}, u32[]{:S(2)}, u32[]{:S(2)}) %all-to-all-start.5) | async-done | bytes 32800 | tf_op jit(solution)/shard_map/all_to_all | solution.py:13
  227.9 1.7 copy-done.3
  229.6 5.4 %fusion.3 = f32[3,512,1024]{1,2,0:T(8,128)} fusion(f32[]{:T(128)S(6)} %div.53, bf16[8,3,128,512]{3,2,1,0:T(8,128)(2,1)S(1)} %copy-done.3, bf16[8,16,8,1024]{3,2,0,1:T(8,128)(2,1)S(1)} %bitcast.103), kind=kOutput, calls=%fused_computation.5 | convolution fusion | flops 3222798336 | bytes 11534340 | tf_op jit(solution)/shard_map/gsrk,grn->skn/dot_general | solution.py:110
  235.0 6.7 %copy.92 = f32[3,512,1024]{2,1,0:T(8,128)} copy(f32[3,512,1024]{1,2,0:T(8,128)} %fusion.3) | data formatting | bytes 12582912
  (43 shorter events, 7.3 us)
Async XLA Ops:
  0.6 46.7 %copy-start = (bf16[3,512,1024]{2,1,0:T(8,128)(2,1)S(1)}, bf16[3,512,1024]{2,1,0:T(8,128)(2,1)}, u32[]{:S(2)}) copy-start(bf16[3,512,1024]{2,1,0:T(8,128)(2,1)} %param.9) | copy-start | bytes 9437188
  47.3 3.6 %copy-start.2 = (bf16[8,3,128,512]{3,2,1,0:T(8,128)(2,1)}, bf16[8,3,128,512]{3,2,1,0:T(8,128)(2,1)S(1)}, u32[]{:S(2)}) copy-start(bf16[8,3,128,512]{3,2,1,0:T(8,128)(2,1)S(1)} %all_to_all.40) | copy-start | bytes 9437188
  89.8 20.2 %copy-start.4 = (bf16[1,128,1024]{2,1,0:T(8,128)(2,1)S(1)}, bf16[1,128,1024]{2,1,0:T(8,128)(2,1)}, u32[]{:S(2)}) copy-start(bf16[1,128,1024]{2,1,0:T(8,128)(2,1)} %param.8) | copy-start | bytes 786436
  106.9 4.8 %collective-permute-start = (bf16[8,8,8,1024]{3,2,1,0:T(8,128)(2,1)S(1)}, bf16[8,8,8,1024]{3,2,1,0:T(8,128)(2,1)}, u32[]{:S(2)}, u32[]{:S(2)}) collective-permute-start(bf16[8,8,8,1024]{3,2,1,0:T(8,128)(2,1)S(1)} %all_to_all.42), channel_id=1, source_target_pairs={{0,1},{1,0},{2,3},{3,2},{4,5},{5,4},{6,7},{7,6},{8,9},{9,8},{10,11... | collective-permute-start | bytes 3145736 | tf_op jit(solution)/shard_map/ppermute | solution.py:19
  113.6 2.4 copy-start.5
  116.0 17.7 %copy-start.6 = (s32[1,128]{1,0:T(1,128)S(1)}, s32[1,128]{1,0:T(1,128)}, u32[]{:S(2)}) copy-start(s32[1,128]{1,0:T(1,128)} %param.13) | copy-start | bytes 1540
  130.0 9.5 %all-to-all-start.3 = ((f32[16,8,128]{2,1,0:T(8,128)}), f32[16,8,128]{2,1,0:T(8,128)S(1)}, u32[]{:S(2)}, u32[]{:S(2)}) async-start(f32[16,8,128]{2,1,0:T(8,128)} %broadcast_in_dim.14), calls=%async_computation.3 | async-start | bytes 131072 | tf_op jit(solution)/shard_map/all_to_all | solution.py:13
  202.1 25.3 %collective-permute-start.1 = (bf16[8,8,8,1024]{3,2,1,0:T(8,128)(2,1)S(1)}, bf16[8,8,8,1024]{3,2,1,0:T(8,128)(2,1)S(1)}, u32[]{:S(2)}, u32[]{:S(2)}) collective-permute-start(bf16[8,8,8,1024]{3,2,1,0:T(8,128)(2,1)S(1)} %all_to_all.44), channel_id=1, source_target_pairs={{0,1},{1,0},{2,3},{3,2},{4,5},{5,4},{6,7},{7,6},{8,9},{9,8},{10,11... | collective-permute-start | bytes 3145736 | tf_op jit(solution)/shard_map/ppermute | solution.py:19
  205.6 7.4 %all-to-all-start.4 = ((f32[2,8,128]{2,1,0:T(8,128)}), f32[2,8,128]{2,1,0:T(8,128)S(1)}, u32[]{:S(2)}, u32[]{:S(2)}) async-start(f32[2,8,128]{2,1,0:T(8,128)} %broadcast_in_dim_broadcast_in_dim_broadcast_in_dim.6), calls=%async_computation.4 | async-start | bytes 16384 | tf_op jit(solution)/shard_map/all_to_all | solution.py:13
  214.3 9.8 %all-to-all-start.5 = ((f32[8,8,128]{2,1,0:T(8,128)}), f32[8,8,128]{2,1,0:T(8,128)S(1)}, u32[]{:S(2)}, u32[]{:S(2)}) async-start(f32[8,8,128]{2,1,0:T(8,128)} %broadcast_in_dim_broadcast_in_dim_broadcast_in_dim.7), calls=%async_computation.5 | async-start | bytes 65536 | tf_op jit(solution)/shard_map/all_to_all | solution.py:13
  227.7 1.9 copy-start.3
  235.0 6.7 %copy-start.1 = (bf16[3,512,1024]{2,1,0:T(8,128)(2,1)S(1)}, bf16[3,512,1024]{2,1,0:T(8,128)(2,1)}, u32[]{:S(2)}) copy-start(bf16[3,512,1024]{2,1,0:T(8,128)(2,1)} %param.9) | copy-start | bytes 9437188

commit v2 on v1

v2 whole, which is shorter than its diff:
```python
import functools

import jax
import jax.numpy as jnp
from jax import lax
from jax.experimental import pallas as pl
from jax.experimental.pallas import tpu as pltpu
from jax.sharding import Mesh, PartitionSpec as P

NORM_EPS = 1e-05
GROUP = ("x", "yh")
RING = ("z", "yl")
ALL = ("x", "yh", "z", "yl", "c")
GROUPS = 8
HALF = 128
ROWS = 80
SPARE = HALF - ROWS
PIECE = ROWS // 2
MIB = 1 << 20
f32, bf16 = jnp.float32, jnp.bfloat16
SCALARS = pl.BlockSpec(memory_space=pltpu.SMEM)
VECTORS = pl.BlockSpec(memory_space=pltpu.VMEM)
ANYWHERE = pl.BlockSpec(memory_space=pl.ANY)
OWN, X, YH, CORE, TENSOR, HAVE, BLOCKS, SPARES = 0, 1, 2, 3, 4, 5, 8, 16


def spread(value, axes, count):
    return lax.all_to_all(
        jnp.broadcast_to(value[None], (count,) + value.shape), axes, 0, 0, tiled=True
    )


def swap(value, axis, bit, count):
    return lax.ppermute(value, axis, [(i, i ^ bit) for i in range(count)])


def pack_kernel(info_ref, cap_ref, mask_ref, out_ref):
    out_ref[0 : 3 * HALF, :] = cap_ref[...].reshape(3 * HALF, 512)
    lane = lax.broadcasted_iota(jnp.int32, (1, 512), 1)
    masked = (mask_ref[...] == 1).astype(f32)
    near = lax.broadcasted_iota(jnp.int32, (1, HALF), 1) < info_ref[HAVE]
    count = jnp.sum(jnp.where(near, masked, 0.0), axis=1, keepdims=True)
    place = lax.broadcasted_iota(jnp.int32, (HALF, 512), 0) - ROWS
    column = lax.broadcasted_iota(jnp.int32, (HALF, 512), 1)
    tiled = jnp.zeros((HALF, 512), f32)
    for g in range(GROUPS):
        tiled = jnp.where((column - SPARE * g == place) & (place >= 0), 1.0, tiled)
    repeated = jnp.dot(
        jnp.broadcast_to(masked, (8, HALF)).astype(bf16),
        tiled.astype(bf16),
        preferred_element_type=f32,
    )[0:1]
    have = jnp.zeros((1, 512), f32) + info_ref[HAVE].astype(f32)
    row = lax.broadcasted_iota(jnp.int32, (16, 512), 0)
    facts = jnp.where(row == 0, have, jnp.where(row == 1, repeated, 0.0))
    facts = jnp.where(row == 2, count + lane.astype(f32) * 0.0, facts)
    out_ref[3 * HALF : 3 * HALF + 16, :] = facts.astype(bf16)


def pack(info, captured, loss_mask):
    return pl.pallas_call(
        pack_kernel,
        in_specs=[SCALARS, VECTORS, VECTORS],
        out_specs=VECTORS,
        out_shape=jax.ShapeDtypeStruct((3 * HALF + 16, 512), bf16),
        compiler_params=pltpu.CompilerParams(vmem_limit_bytes=8 * MIB),
        name="pack",
    )(info, captured, loss_mask)


def unite_kernel(info_ref, *refs):
    blocks = refs[:GROUPS]
    weight_ref, rows_ref, part_ref, slot_ref, fact_ref, cap_ref, sems = refs[GROUPS:]
    copies = [
        pltpu.make_async_copy(blocks[k], cap_ref.at[info_ref[BLOCKS + k]], sems.at[k])
        for k in range(GROUPS)
    ]
    for copy in copies:
        copy.start()
    for copy in copies:
        copy.wait()
    lane = lax.broadcasted_iota(jnp.int32, (1, 512), 1).astype(f32)
    have, before_more, before_less, facts = [], [], [], []
    more = less = total_count = jnp.zeros((1, 512), f32)
    for g in range(GROUPS):
        fact = cap_ref[g, 3 * HALF : 3 * HALF + 16, :].astype(f32)
        facts.append(fact[1:2])
        have.append(fact[0:1])
        before_more.append(more)
        before_less.append(less)
        more = more + jnp.maximum(have[g] - ROWS, 0.0)
        less = less + jnp.maximum(ROWS - have[g], 0.0)
        total_count = total_count + fact[2:3]
        fact_ref[g : g + 1, :] = fact[2:3, 0:128]
    order = jnp.full((1, 512), -1.0, f32)
    mask_pool = jnp.zeros((1, 512), f32)
    seq_pool = jnp.zeros((1, 512), f32)
    for g in range(GROUPS):
        place = lane - SPARE * g
        mine = (place >= 0) & (place < SPARE)
        order = jnp.where(mine & (place < have[g] - ROWS), before_more[g] + place, order)
        mask_pool = jnp.where(mine, facts[g], mask_pool)
        seq_pool = jnp.where(mine, float(g // 2), seq_pool)
    slot = jnp.full((1, 512), -1.0, f32)
    for g in range(GROUPS):
        offset = order - before_less[g]
        mine = (order >= 0) & (offset >= 0) & (offset < ROWS - have[g])
        slot = jnp.where(mine, ROWS * g + have[g] + offset, slot)
    slot_ref[...] = jnp.concatenate(
        [slot, mask_pool, seq_pool] + [jnp.zeros((1, 512), f32)] * 5, axis=0
    )
    for block in range(2):
        row = lax.broadcasted_iota(jnp.int32, (4 * ROWS, 384), 0) + block * 4 * ROWS
        pick = (row.astype(f32) == slot[:, :384]).astype(bf16)
        total = None
        for s in range(3):
            pool = cap_ref[:, s * HALF + ROWS : (s + 1) * HALF, :].reshape(384, 512)
            moved = jnp.dot(pick, pool, preferred_element_type=f32)
            kept = []
            for g in range(4 * block, 4 * block + 4):
                own = cap_ref[g, s * HALF : s * HALF + ROWS, :].astype(f32)
                within = lax.broadcasted_iota(jnp.int32, (ROWS, 512), 0).astype(f32) < have[g]
                base = (g - 4 * block) * ROWS
                kept.append(jnp.where(within, own, moved[base : base + ROWS]))
            rows = jnp.concatenate(kept, axis=0).astype(bf16)
            rows_ref[s, pl.ds(block * 4 * ROWS, 4 * ROWS), :] = rows
            term = jnp.dot(rows, weight_ref[s], preferred_element_type=f32)
            total = term if total is None else total + term
        for g in range(4):
            for j in range(8):
                for c in range(2):
                    base = g * ROWS + c * PIECE
                    part_ref[4 * block + g, j, c] = total[
                        base : base + PIECE, j * 128 : (j + 1) * 128
                    ].astype(bf16)


def unite(info, blocks, weight):
    return pl.pallas_call(
        unite_kernel,
        in_specs=[SCALARS] + [ANYWHERE] * GROUPS + [VECTORS],
        out_specs=[VECTORS] * 4,
        out_shape=(
            jax.ShapeDtypeStruct((3, GROUPS * ROWS, 512), bf16),
            jax.ShapeDtypeStruct((GROUPS, 8, 2, PIECE, 128), bf16),
            jax.ShapeDtypeStruct((8, 512), f32),
            jax.ShapeDtypeStruct((GROUPS, 128), f32),
        ),
        scratch_shapes=[
            pltpu.VMEM((GROUPS, 3 * HALF + 16, 512), bf16),
            pltpu.SemaphoreType.DMA((GROUPS,)),
        ],
        compiler_params=pltpu.CompilerParams(vmem_limit_bytes=40 * MIB),
        name="unite",
    )(info, *blocks, weight)


def head_kernel(info_ref, own_ref, other_ref, gain_ref, target_ref, mask_ref, slot_ref, *refs):
    spares = refs[:GROUPS]
    head_ref, logit_ref, chosen_ref, stat_ref, side_ref, united_ref = refs[GROUPS : GROUPS + 6]
    wide, normed, held, pool, sems, pool_sems = refs[GROUPS + 6 :]
    width = wide.shape[1]
    tile = head_ref.shape[0] // 4
    loads = [
        pltpu.make_async_copy(
            head_ref.at[pl.ds(i * tile, tile)], held.at[pl.ds(i * tile, tile)], sems.at[i]
        )
        for i in range(4)
    ]
    moves = [
        pltpu.make_async_copy(spares[k], pool.at[info_ref[SPARES + k]], pool_sems.at[k])
        for k in range(GROUPS)
    ]
    for copy in moves + loads:
        copy.start()

    first = info_ref[CORE] == 0
    wide[ROWS:HALF, :] = jnp.zeros((HALF - ROWS, width), f32)
    for g in range(GROUPS):
        for j in range(8):
            column = (g * 8 + j) * 128
            a = own_ref[j, g].astype(f32)
            b = other_ref[j, g].astype(f32)
            wide[0:PIECE, column : column + 128] = jnp.where(first, a, b)
            wide[PIECE:ROWS, column : column + 128] = jnp.where(first, b, a)
    square = jnp.zeros((HALF, 1), f32)
    for g in range(GROUPS):
        values = wide[:, g * 1024 : (g + 1) * 1024]
        square = square + jnp.sum(values * values, axis=1, keepdims=True)
    scale = lax.rsqrt(square / width + NORM_EPS)
    for g in range(GROUPS):
        part = slice(g * 1024, (g + 1) * 1024)
        values = wide[:, part]
        united_ref[:, part] = values[0:ROWS].astype(bf16)
        normed[part, :] = jnp.transpose(values * scale * gain_ref[:, part]).astype(bf16)

    for copy in moves:
        copy.wait()
    have = info_ref[HAVE]
    row = lax.broadcasted_iota(jnp.int32, (HALF, 384), 0) + info_ref[OWN] * ROWS
    pick = (row.astype(f32) == slot_ref[0:1, 0:384]).astype(bf16)
    moved = jnp.dot(pick, pool[...].reshape(384, pool.shape[2]), preferred_element_type=f32)
    kept = lax.broadcasted_iota(jnp.int32, moved.shape, 0) < have
    chosen = jnp.transpose(jnp.where(kept, target_ref[...].astype(f32), moved))
    chosen_ref[...] = chosen
    traits = lax.dot_general(
        slot_ref[:, 0:384].astype(bf16), pick, (((1,), (1,)), ((), ())), preferred_element_type=f32
    )
    lane = lax.broadcasted_iota(jnp.int32, (1, HALF), 1)
    masked = (mask_ref[...] == 1).astype(f32)
    valid = jnp.where(lane < have, masked, traits[1:2])
    valid = jnp.where(lane < ROWS, valid, 0.0)
    sequence = jnp.where(lane < have, info_ref[X].astype(f32), traits[2:3])
    scale_lane = jnp.transpose(jnp.broadcast_to(scale, (HALF, HALF)))[0:1]
    nothing = jnp.zeros((1, HALF), f32)
    side_ref[...] = jnp.concatenate([scale_lane, valid, sequence] + [nothing] * 5, axis=0)

    top_t = jnp.max(chosen, axis=0, keepdims=True)
    pow_t = jnp.exp(chosen - top_t)
    sum_t = jnp.sum(pow_t, axis=0, keepdims=True)
    dot_t = jnp.sum(pow_t * chosen, axis=0, keepdims=True)
    for i in range(4):
        loads[i].wait()
        part = slice(i * tile, (i + 1) * tile)
        logit_ref[part, :] = jnp.dot(held[part, :], normed[...], preferred_element_type=f32)
    logits = logit_ref[...]
    top_d = jnp.max(logits, axis=0, keepdims=True)
    pow_d = jnp.exp(logits - top_d)
    stat_ref[...] = jnp.concatenate(
        [
            top_t,
            sum_t,
            dot_t,
            jnp.sum(pow_t * logits, axis=0, keepdims=True),
            top_d,
            jnp.sum(pow_d, axis=0, keepdims=True),
            jnp.sum(pow_d * logits, axis=0, keepdims=True),
            nothing,
        ],
        axis=0,
    )


def head_forward(info, own, other, gain, target, loss_mask, slots, spares, head):
    vocab, width = head.shape
    return pl.pallas_call(
        head_kernel,
        in_specs=[SCALARS] + [VECTORS] * 6 + [ANYWHERE] * (GROUPS + 1),
        out_specs=[VECTORS] * 5,
        out_shape=(
            jax.ShapeDtypeStruct((vocab, HALF), f32),
            jax.ShapeDtypeStruct((vocab, HALF), f32),
            jax.ShapeDtypeStruct((8, HALF), f32),
            jax.ShapeDtypeStruct((8, HALF), f32),
            jax.ShapeDtypeStruct((ROWS, width), bf16),
        ),
        scratch_shapes=[
            pltpu.VMEM((HALF, width), f32),
            pltpu.VMEM((width, HALF), bf16),
            pltpu.VMEM((vocab, width), bf16),
            pltpu.VMEM((GROUPS, SPARE, vocab), bf16),
            pltpu.SemaphoreType.DMA((4,)),
            pltpu.SemaphoreType.DMA((GROUPS,)),
        ],
        compiler_params=pltpu.CompilerParams(vmem_limit_bytes=44 * MIB),
        name="head_forward",
    )(info, own, other, gain, target, loss_mask, slots, *spares, head)


def back_kernel(
    info_ref, every_ref, logit_ref, chosen_ref, side_ref, gain_ref, united_ref, head_ref,
    out_ref, sum_ref, held, sems,
):
    width = gain_ref.shape[1]
    loads = [
        pltpu.make_async_copy(
            head_ref.at[:, pl.ds(g * 1024, 1024)], held.at[g], sems.at[g]
        )
        for g in range(GROUPS)
    ]
    for copy in loads:
        copy.start()
    every = every_ref[...]
    max_t = jnp.max(every[:, 0:1], axis=0)
    scale_t = jnp.exp(every[:, 0:1] - max_t[None])
    sum_t = jnp.sum(every[:, 1:2] * scale_t, axis=0)
    mean_tt = jnp.sum(every[:, 2:3] * scale_t, axis=0) / sum_t
    mean_tl = jnp.sum(every[:, 3:4] * scale_t, axis=0) / sum_t
    max_d = jnp.max(every[:, 4:5], axis=0)
    scale_d = jnp.exp(every[:, 4:5] - max_d[None])
    sum_d = jnp.sum(every[:, 5:6] * scale_d, axis=0)
    mean_dl = jnp.sum(every[:, 6:7] * scale_d, axis=0) / sum_d
    log_t = max_t + jnp.log(sum_t)
    log_d = max_d + jnp.log(sum_d)
    row_scale, valid, sequence = side_ref[0:1], side_ref[1:2], side_ref[2:3]
    kl = (mean_tt - mean_tl - log_t + log_d) * valid
    row = lax.broadcasted_iota(jnp.int32, (8, HALF), 0)
    sum_ref[...] = jnp.broadcast_to(
        jnp.sum(jnp.where(row.astype(f32) == sequence, kl, 0.0), axis=1, keepdims=True), (8, HALF)
    )

    weight = valid * row_scale
    grad = weight * (jnp.exp(logit_ref[...] - log_d) - jnp.exp(chosen_ref[...] - log_t))
    grad = jnp.transpose(grad)[0:ROWS].astype(bf16)
    lane = lax.broadcasted_iota(jnp.int32, (1, HALF), 1)
    share = ROWS // 16
    mine = (lane >= info_ref[TENSOR] * share) & (lane < (info_ref[TENSOR] + 1) * share)
    cubic = jnp.where(mine, weight * row_scale * (mean_dl - mean_tl) / width, 0.0)
    cubic = jnp.transpose(jnp.broadcast_to(cubic, (HALF, HALF)))[0:ROWS, 0:1]
    for g in range(GROUPS):
        part = slice(g * 1024, (g + 1) * 1024)
        loads[g].wait()
        block = jnp.dot(grad, held[g], preferred_element_type=f32)
        block = block * gain_ref[:, part] - cubic * united_ref[:, part].astype(f32)
        for j in range(8):
            for c in range(2):
                out_ref[g, j, c] = block[
                    c * PIECE : (c + 1) * PIECE, j * 128 : (j + 1) * 128
                ].astype(bf16)


def head_backward(info, every, logits, chosen, side, gain, united, head):
    vocab = head.shape[0]
    return pl.pallas_call(
        back_kernel,
        in_specs=[SCALARS] + [VECTORS] * 6 + [ANYWHERE],
        out_specs=[VECTORS] * 2,
        out_shape=(
            jax.ShapeDtypeStruct((GROUPS, 8, 2, PIECE, 128), bf16),
            jax.ShapeDtypeStruct((8, HALF), f32),
        ),
        scratch_shapes=[
            pltpu.VMEM((GROUPS, vocab, 1024), bf16),
            pltpu.SemaphoreType.DMA((GROUPS,)),
        ],
        compiler_params=pltpu.CompilerParams(vmem_limit_bytes=44 * MIB),
        name="head_backward",
    )(info, every, logits, chosen, side, gain, united, head)


def grad_kernel(core_ref, factor_ref, own_ref, other_ref, rows_ref, out_ref, wide, grads):
    @pl.when((pl.program_id(0) == 0) & (pl.program_id(1) == 0))
    def _():
        first = core_ref[0] == 0
        for g in range(GROUPS):
            for j in range(8):
                a = own_ref[j, g].astype(f32)
                b = other_ref[j, g].astype(f32)
                base = g * ROWS
                wide[base : base + PIECE, j * 128 : (j + 1) * 128] = jnp.where(first, a, b)
                wide[base + PIECE : base + ROWS, j * 128 : (j + 1) * 128] = jnp.where(first, b, a)
        grads[...] = wide[...].astype(bf16)

    out_ref[0] = factor_ref[0] * lax.dot_general(
        rows_ref[0], grads[...], (((0,), (0,)), ((), ())), preferred_element_type=f32
    )


def weight_gradient(core, factor, own, other, rows):
    total = GROUPS * ROWS
    whole = lambda shape: pl.BlockSpec(shape, lambda s, i: (0,) * len(shape))
    return pl.pallas_call(
        grad_kernel,
        grid=(3, 2),
        in_specs=[
            pl.BlockSpec(memory_space=pltpu.SMEM),
            pl.BlockSpec(memory_space=pltpu.SMEM),
            whole((8, GROUPS, PIECE, 128)),
            whole((8, GROUPS, PIECE, 128)),
            pl.BlockSpec((1, total, 256), lambda s, i: (s, 0, i)),
        ],
        out_specs=pl.BlockSpec((1, 256, 1024), lambda s, i: (s, i, 0)),
        out_shape=jax.ShapeDtypeStruct((3, 512, 1024), f32),
        scratch_shapes=[pltpu.VMEM((total, 1024), f32), pltpu.VMEM((total, 1024), bf16)],
        compiler_params=pltpu.CompilerParams(vmem_limit_bytes=40 * MIB),
        name="weight_gradient",
    )(core, factor, own, other, rows)


def sum_over_tensor(pieces):
    received = lax.all_to_all(pieces.reshape(128, PIECE, 128), ALL, 0, 0, tiled=True)
    return jnp.sum(received.reshape(GROUPS, 16, PIECE, 128).astype(f32), axis=1).astype(bf16)


def route(value, first, second):
    moves = {"y": (0, 1), "right": (1, 0), "left": (3, 0), "far": (2, 0)}
    pairs = []
    for x in range(4):
        for y in range(2):
            for c, step in enumerate((first, second)):
                dx, dy = moves[step]
                target = ((x + dx) % 4 * 2 + (y ^ dy)) * 2 + c
                pairs.append(((x * 2 + y) * 2 + c, target))
    return lax.ppermute(value, ("x", "yh", "c"), pairs)


def gather_blocks(own):
    first = lax.axis_index("c") == 0
    r1 = route(own, "y", "right")
    r2 = route(own, "right", "left")
    r3 = route(own, "left", "far")
    r4 = route(own, "far", "y")
    r5 = route(r1, "right", "y")
    r6 = route(jnp.where(first, r1, r2), "left", "y")
    r7 = route(jnp.where(first, r1, r3), "far", "y")
    return [own, r1, r2, r3, r4, r5, r6, r7]


def local(captured, target_logits, unite_weight, norm_gain, head_weight, lengths, loss_mask):
    width = norm_gain.shape[0]
    x, yh, core = lax.axis_index("x"), lax.axis_index("yh"), lax.axis_index("c")
    have = jnp.clip(lengths[0] - yh * HALF, 0, HALF)

    def group_of(dx, dy):
        return (x + dx) % 4 * 2 + (yh ^ dy)

    early = [group_of(0, 1), group_of(3, 0), group_of(1, 0), group_of(2, 0)]
    late = [early[1], early[2], early[3], early[0]]
    offsets = [(dx, dy) for dx in range(4) for dy in range(2)]
    info = jnp.stack(
        [group_of(0, 0), x, yh, core, lax.axis_index(("z", "yl", "c")), have, have, have]
        + [group_of(0, 0)]
        + [jnp.where(core == 0, a, b) for a, b in zip(early, late)]
        + [group_of(3, 1), group_of(1, 1), group_of(2, 1)]
        + [group_of(-dx % 4, dy) for dx, dy in offsets]
    ).astype(jnp.int32)

    blocks = gather_blocks(pack(info, captured.reshape(3, HALF, 512), loss_mask))
    rows, partial, slots, counts = unite(info, blocks, unite_weight)

    target = target_logits.reshape(HALF, -1)
    partial, spare = lax.optimization_barrier((partial, target[ROWS:]))
    spares = [spare]
    for dx, dy in offsets[1:]:
        pairs = [
            (p * 2 + q, (p + dx) % 4 * 2 + (q ^ dy)) for p in range(4) for q in range(2)
        ]
        spares.append(lax.ppermute(spare, GROUP, pairs))

    own_united = spread(sum_over_tensor(partial), RING, 8)
    other_united = swap(own_united, "c", 1, 2)
    gain = norm_gain.reshape(1, width)
    logits, chosen, stats, side, united = head_forward(
        info, own_united, other_united, gain, target, loss_mask, slots, spares, head_weight
    )
    every = spread(stats, ("z", "yl", "c"), 16)
    grad_pieces, seq_sums = head_backward(
        info, every, logits, chosen, side, gain, united, head_weight
    )
    grad_sum = sum_over_tensor(grad_pieces)
    seq_sums = seq_sums + swap(seq_sums, "yh", 1, 2)
    grad_sum, seq_sums = lax.optimization_barrier((grad_sum, seq_sums))
    own_grad = spread(grad_sum, RING, 8)
    seq_sums = seq_sums + swap(seq_sums, "x", 1, 4)
    own_grad, seq_sums = lax.optimization_barrier((own_grad, seq_sums))
    other_grad = swap(own_grad, "c", 1, 2)
    seq_sums = seq_sums + swap(seq_sums, "x", 2, 4)

    counts = counts[:, 0]
    factor = (2 * HALF) / jnp.maximum(jnp.sum(counts), 1.0)
    unite_grad = weight_gradient(core.reshape(1), factor.reshape(1), own_grad, other_grad, rows)
    here = lax.iota(jnp.int32, GROUPS)
    count_seq = jnp.sum(jnp.where(here // 2 == x, counts, 0.0))
    seq_sum = jnp.sum(jnp.where(here == x, seq_sums[:, 0], 0.0))
    seq_kl = (seq_sum / jnp.maximum(count_seq, 1.0)).reshape(1)
    return (seq_kl, unite_grad)


def solution(mesh):
    fine = Mesh(mesh.devices.reshape(4, 2, 4, 2, 2), ALL)
    tensor = ("z", "yl", "c")
    placed = (
        P(None, "x", "yh", tensor),
        P("x", "yh", tensor),
        P(None, tensor, GROUP),
        P(),
        P(tensor, None),
        P("x"),
        P("x", "yh"),
    )
    return jax.shard_map(
        local,
        mesh=fine,
        in_specs=placed,
        out_specs=(P("x"), P(None, tensor, GROUP)),
        check_vma=False,
    )
```

time: 244 us -> 200 us (0.82)
  blocking collectives: 152 us -> 55.2 us
  waiting for transfers between devices: 17.5 us -> 59.4 us
  matrix products: 32 us -> 0 us
  Pallas kernels: 0 us -> 30 us
  starting transfers between devices: 15 us -> 44.1 us
  local copies, waits for them, and re-layouts: 13.7 us -> 3.84 us
  other arithmetic: 8.31 us -> 2.38 us
    all_to_all x3 -> x2, blocking collectives: 78.5 us -> 23.3 us  [spread(): lax.all_to_all(jnp.broadcast_to(value[None], (count,) + value.shape), axe...]
    all_to_all x2 -> x1, blocking collectives: 73 us -> 31.9 us  [sum_over_tensor(): lax.all_to_all(pieces.reshape(128, PIECE, 128), ALL, 0, 0, tiled=True)]
    ppermute x2 -> x19, waiting for transfers between devices: 1.63 us -> 38.6 us  [the longest x7 24.8 us: route(): return lax.ppermute(value, ('x', 'yh', 'c'), pairs)]
    dot_general x4 -> x0, matrix products: 32 us -> none  [the longest x1 12.8 us: local(): lax.dot_general(normed, head_weight, (((1,), (1,)), ((), ())), preferred_...]
    pallas_call x0 -> x5, Pallas kernels: none -> 30 us  [the longest x1 9.26 us: head_forward(): pl.pallas_call(head_kernel, in_specs=[SCALARS] + [VECTORS] * 6 + [ANYWHER...]
    ppermute x2 -> x19, starting transfers between devices: 4.82 us -> 33.7 us  [the longest x7 14.2 us: route(): return lax.ppermute(value, ('x', 'yh', 'c'), pairs)]
    all_to_all x0 -> x1, waiting for transfers between devices: none -> 13 us  [sum_over_tensor(): lax.all_to_all(pieces.reshape(128, PIECE, 128), ALL, 0, 0, tiled=True)]
    all_to_all x3 -> x1, waiting for transfers between devices: 15.9 us -> 7.85 us  [spread(): lax.all_to_all(jnp.broadcast_to(value[None], (count,) + value.shape), axe...]
  transfers between devices with their start and end apart: 5 -> 21, of which waited for: 4 -> 14; matrix products, arithmetic and copies ran while one was open for 2% -> 2% of each run, Pallas kernels for 0% -> 0%
where the time goes in v2:
time: 200 us
  waiting for transfers between devices  59.4 us (30%)
  blocking collectives  55.2 us (28%)
  starting transfers between devices  44.1 us (22%)
  Pallas kernels  30 us (15%)
  between operations  4.76 us (2%)
  local copies, waits for them, and re-layouts  3.84 us (2%)
  other arithmetic  2.38 us (1%)
    all_to_all x1, blocking collectives, sum_over_tensor(): lax.all_to_all(pieces.reshape(128, PIECE, 128), ALL, 0, 0, tiled=True)  31.9 us
    ppermute x7, waiting for transfers between devices, route(): return lax.ppermute(value, ('x', 'yh', 'c'), pairs)  24.8 us
    all_to_all x2, blocking collectives, spread(): lax.all_to_all(jnp.broadcast_to(value[None], (count,) + value.shape), axe...  23.3 us
    ppermute x7, starting transfers between devices, route(): return lax.ppermute(value, ('x', 'yh', 'c'), pairs)  14.2 us
    all_to_all x1, waiting for transfers between devices, sum_over_tensor(): lax.all_to_all(pieces.reshape(128, PIECE, 128), ALL, 0, 0, tiled=True)  13 us
    ppermute x7, starting transfers between devices, local(): spares.append(lax.ppermute(spare, GROUP, pairs))  11 us
    pallas_call x1, Pallas kernels, head_forward(): pl.pallas_call(head_kernel, in_specs=[SCALARS] + [VECTORS] * 6 + [ANYWHER...  9.26 us
    ppermute x5, waiting for transfers between devices, swap(): return lax.ppermute(value, axis, [(i, i ^ bit) for i in range(count)])  9.07 us
  transfers between devices with their start and end apart: 21, of which 14 were waited for; matrix products, arithmetic and copies ran while one was open for 2% of the time, Pallas kernels for 0%

profile of v2, /device:TPU:1, one launch (start us, length us, event | category | flops | bytes accessed | tf_op | source)
XLA Modules:
  0.0 199.6 jit_solution(5712105818374530397)
XLA Ops:
  4.0 3.6 %collective-permute-start.2 = (bf16[400,512]{1,0:T(8,128)(2,1)S(1)}, bf16[400,512]{1,0:T(8,128)(2,1)S(1)}, u32[]{:S(2)}, u32[]{:S(2)}) collective-permute-start(bf16[400,512]{1,0:T(8,128)(2,1)S(1)} %pack.1.refs_0_), channel_id=1, source_target_pairs={{0,96},{1,65},{16,112},{17,81},{32,0},{33,97},{48,16},{49,113},{64... | collective-permute-start | bytes 1228808 | tf_op jit(solution)/shard_map/ppermute | solution.py:394
  9.0 2.9 %collective-permute-start.3 = (bf16[400,512]{1,0:T(8,128)(2,1)S(1)}, bf16[400,512]{1,0:T(8,128)(2,1)S(1)}, u32[]{:S(2)}, u32[]{:S(2)}) collective-permute-start(bf16[400,512]{1,0:T(8,128)(2,1)S(1)} %pack.1.refs_0_), channel_id=1, source_target_pairs={{0,64},{1,17},{16,80},{17,1},{32,96},{33,49},{48,112},{49,33},{64,... | collective-permute-start | bytes 1228808 | tf_op jit(solution)/shard_map/ppermute | solution.py:394
  11.9 4.0 %collective-permute-done.2.refs_3_ = bf16[400,512]{1,0:T(8,128)(2,1)S(1)} collective-permute-done((bf16[400,512]{1,0:T(8,128)(2,1)S(1)}, bf16[400,512]{1,0:T(8,128)(2,1)S(1)}, u32[]{:S(2)}, u32[]{:S(2)}) %collective-permute-start.2) | collective-permute-done | bytes 409632 | tf_op jit(solution)/shard_map/ppermute | solution.py:394
  16.0 10.2 %collective-permute-done.1.refs_2_ = bf16[400,512]{1,0:T(8,128)(2,1)S(1)} collective-permute-done((bf16[400,512]{1,0:T(8,128)(2,1)S(1)}, bf16[400,512]{1,0:T(8,128)(2,1)S(1)}, u32[]{:S(2)}, u32[]{:S(2)}) %collective-permute-start.1) | collective-permute-done | bytes 409632 | tf_op jit(solution)/shard_map/ppermute | solution.py:394
  26.6 3.2 %collective-permute-start.6 = (bf16[400,512]{1,0:T(8,128)(2,1)S(1)}, bf16[400,512]{1,0:T(8,128)(2,1)S(1)}, u32[]{:S(2)}, u32[]{:S(2)}) collective-permute-start(bf16[400,512]{1,0:T(8,128)(2,1)S(1)} %get-tuple-element.38), channel_id=1, source_target_pairs={{0,64},{1,17},{16,80},{17,1},{32,96},{33,49},{48,112},{49,33},{64,... | collective-permute-start | bytes 1228808 | tf_op jit(solution)/shard_map/ppermute | solution.py:394
  29.9 2.9 %collective-permute-start.5 = (bf16[400,512]{1,0:T(8,128)(2,1)S(1)}, bf16[400,512]{1,0:T(8,128)(2,1)S(1)}, u32[]{:S(2)}, u32[]{:S(2)}) collective-permute-start(bf16[400,512]{1,0:T(8,128)(2,1)S(1)} %get-tuple-element.39), channel_id=1, source_target_pairs={{0,96},{1,17},{16,112},{17,1},{32,0},{33,49},{48,16},{49,33},{64,3... | collective-permute-start | bytes 1228808 | tf_op jit(solution)/shard_map/ppermute | solution.py:394
  33.7 5.9 %collective-permute-done.4.refs_5_ = bf16[400,512]{1,0:T(8,128)(2,1)S(1)} collective-permute-done((bf16[400,512]{1,0:T(8,128)(2,1)S(1)}, bf16[400,512]{1,0:T(8,128)(2,1)S(1)}, u32[]{:S(2)}, u32[]{:S(2)}) %collective-permute-start.4) | collective-permute-done | bytes 409632 | tf_op jit(solution)/shard_map/ppermute | solution.py:394
  39.5 4.4 %collective-permute-done.5.refs_6_ = bf16[400,512]{1,0:T(8,128)(2,1)S(1)} collective-permute-done((bf16[400,512]{1,0:T(8,128)(2,1)S(1)}, bf16[400,512]{1,0:T(8,128)(2,1)S(1)}, u32[]{:S(2)}, u32[]{:S(2)}) %collective-permute-start.5) | collective-permute-done | bytes 409632 | tf_op jit(solution)/shard_map/ppermute | solution.py:394
  43.9 6.0 %unite.1 = (bf16[3,640,512]{2,1,0:T(8,128)(2,1)S(1)}, bf16[8,8,2,40,128]{4,3,2,1,0:T(8,128)(2,1)S(1)}, f32[8,512]{1,0:T(8,128)S(1)}, f32[8,128]{1,0:T(8,128)S(1)}) custom-call(s32[24]{0:T(128)S(1)} %stack.78.info_ref, bf16[400,512]{1,0:T(8,128)(2,1)S(1)} %pack.1.refs_0_, bf16[400,512]{1,0:T(8,128)(2,1)S(1)} %collective-permute-done.refs_1_, ...), custom_call_target="tpu_custom_call" | custom-call | tf_op jit(solution)/shard_map/unite/pallas_call | solution.py:139
  49.9 31.9 %all_to_all.25 = bf16[128,40,128]{2,1,0:T(8,128)(2,1)S(1)} all-to-all(bf16[128,40,128]{2,1,0:T(8,128)(2,1)S(1)} %bitcast.32), channel_id=1, replica_groups=mesh['x'=4,'yh'=2,'z'=4,'yl'=2,'c'=2] {'x','yh','z','yl','c'}, dimensions={0} | all-to-all | bytes 2621440 | tf_op jit(solution)/shard_map/all_to_all | solution.py:381
  82.1 12.9 %all_to_all.26.own_ref = bf16[8,8,40,128]{3,2,1,0:T(8,128)(2,1)S(1)} all-to-all(bf16[8,8,40,128]{3,2,1,0:T(8,128)(2,1)S(1)} %broadcast_in_dim.10), channel_id=1, replica_groups=mesh['x'=4,'yh'=2,'z'=4,'yl'=2,'c'=2] {'z','yl'}, dimensions={0} | all-to-all | bytes 1310720 | tf_op jit(solution)/shard_map/all_to_all | solution.py:28
  99.3 3.4 %collective-permute-start.12 = (bf16[48,1024]{1,0:T(8,128)(2,1)S(1)}, bf16[48,1024]{1,0:T(8,128)(2,1)S(1)}, u32[]{:S(2)}, u32[]{:S(2)}) collective-permute-start(bf16[48,1024]{1,0:T(8,128)(2,1)S(1)} %slice_bitcast_fusion.refs_0_), channel_id=1, source_target_pairs={{0,80},{16,64},{32,112},{48,96},{64,16},{80,0},{96,48},{112,32},{1... | collective-permute-start | bytes 294920 | tf_op jit(solution)/shard_map/ppermute | solution.py:438
  108.9 2.1 %collective-permute-done.10.refs_3_ = bf16[48,1024]{1,0:T(8,128)(2,1)S(1)} collective-permute-done((bf16[48,1024]{1,0:T(8,128)(2,1)S(1)}, bf16[48,1024]{1,0:T(8,128)(2,1)S(1)}, u32[]{:S(2)}, u32[]{:S(2)}) %collective-permute-start.10) | collective-permute-done | bytes 98336 | tf_op jit(solution)/shard_map/ppermute | solution.py:438
  112.7 9.3 %head_forward.1 = (f32[1024,128]{1,0:T(8,128)S(1)}, f32[1024,128]{1,0:T(8,128)S(1)}, f32[8,128]{1,0:T(8,128)S(1)}, f32[8,128]{1,0:T(8,128)S(1)}, bf16[80,8192]{1,0:T(8,128)(2,1)S(1)}) custom-call(s32[24]{0:T(128)S(1)} %stack.78.info_ref, bf16[8,8,40,128]{3,2,1,0:T(8,128)(2,1)S(1)} %all_to_all.26.own_ref, ...), custom_call_target="tpu_custom_call" | custom-call | tf_op jit(solution)/shard_map/head_forward/pallas_call | solution.py:246
  122.0 10.4 %all_to_all.27.every_ref = f32[16,8,128]{2,1,0:T(8,128)S(1)} all-to-all(f32[16,8,128]{2,1,0:T(8,128)S(1)} %broadcast_in_dim.11), channel_id=1, replica_groups=mesh['x'=4,'yh'=2,'z'=4,'yl'=2,'c'=2] {'z','yl','c'}, dimensions={0} | all-to-all | bytes 131072 | tf_op jit(solution)/shard_map/all_to_all | solution.py:28
  132.4 8.3 %head_backward.1 = (bf16[8,8,2,40,128]{4,3,2,1,0:T(8,128)(2,1)}, f32[8,128]{1,0:T(8,128)S(1)}) custom-call(s32[24]{0:T(128)S(1)} %stack.78.info_ref, f32[16,8,128]{2,1,0:T(8,128)S(1)} %all_to_all.27.every_ref, f32[1024,128]{1,0:T(8,128)S(1)} %get-tuple-element.24.logit_ref, f32[1024,128]{1,0:T(8,128)S(1)} %get-tuple-element.25.chosen_ref, ...), custom_call_target="tpu_custom_call" | custom-call | tf_op jit(solution)/shard_map/head_backward/pallas_call | solution.py:324
  140.8 6.9 %all-to-all-start.3 = ((bf16[128,40,128]{2,1,0:T(8,128)(2,1)}), bf16[128,40,128]{2,1,0:T(8,128)(2,1)S(1)}, u32[]{:S(2)}, u32[]{:S(2)}) async-start(bf16[128,40,128]{2,1,0:T(8,128)(2,1)} %bitcast.24), calls=%async_computation.3 | async-start | bytes 2621440 | tf_op jit(solution)/shard_map/all_to_all | solution.py:381
  147.7 3.0 %collective-permute-start.15 = (f32[8,128]{1,0:T(8,128)S(1)}, f32[8,128]{1,0:T(8,128)S(1)}, u32[]{:S(2)}, u32[]{:S(2)}) collective-permute-start(f32[8,128]{1,0:T(8,128)S(1)} %get-tuple-element.29), channel_id=1, source_target_pairs={{0,16},{16,0},{1,17},{17,1},{2,18},{18,2},{3,19},{19,3},{4,20},{20... | collective-permute-start | bytes 12296 | tf_op jit(solution)/shard_map/ppermute | solution.py:34
  150.6 6.0 %collective-permute-done.15 = f32[8,128]{1,0:T(8,128)S(1)} collective-permute-done((f32[8,128]{1,0:T(8,128)S(1)}, f32[8,128]{1,0:T(8,128)S(1)}, u32[]{:S(2)}, u32[]{:S(2)}) %collective-permute-start.15) | collective-permute-done | bytes 4128 | tf_op jit(solution)/shard_map/ppermute | solution.py:34
  156.7 13.0 %all-to-all-done.3 = bf16[128,40,128]{2,1,0:T(8,128)(2,1)S(1)} async-done(((bf16[128,40,128]{2,1,0:T(8,128)(2,1)}), bf16[128,40,128]{2,1,0:T(8,128)(2,1)S(1)}, u32[]{:S(2)}, u32[]{:S(2)}) %all-to-all-start.3) | async-done | bytes 1310752 | tf_op jit(solution)/shard_map/all_to_all | solution.py:381
  170.7 3.5 %all-to-all-start.4 = ((bf16[8,8,40,128]{3,2,1,0:T(8,128)(2,1)}), bf16[8,8,40,128]{3,2,1,0:T(8,128)(2,1)S(1)}, u32[]{:S(2)}, u32[]{:S(2)}) async-start(bf16[8,8,40,128]{3,2,1,0:T(8,128)(2,1)} %broadcast_in_dim.12), calls=%async_computation.4 | async-start | bytes 1310720 | tf_op jit(solution)/shard_map/all_to_all | solution.py:28
  174.7 2.2 %collective-permute-done.16 = f32[8,128]{1,0:T(8,128)S(1)} collective-permute-done((f32[8,128]{1,0:T(8,128)S(1)}, f32[8,128]{1,0:T(8,128)S(1)}, u32[]{:S(2)}, u32[]{:S(2)}) %collective-permute-start.16) | collective-permute-done | bytes 4128 | tf_op jit(solution)/shard_map/ppermute | solution.py:34
  176.8 7.9 %all-to-all-done.4.own_ref = bf16[8,8,40,128]{3,2,1,0:T(8,128)(2,1)S(1)} async-done(((bf16[8,8,40,128]{3,2,1,0:T(8,128)(2,1)}), bf16[8,8,40,128]{3,2,1,0:T(8,128)(2,1)S(1)}, u32[]{:S(2)}, u32[]{:S(2)}) %all-to-all-start.4) | async-done | bytes 655392 | tf_op jit(solution)/shard_map/all_to_all | solution.py:28
  192.8 5.8 %weight_gradient.1 = f32[3,512,1024]{2,1,0:T(8,128)} custom-call(s32[1]{0:T(128)} %bitcast.3.core_ref, f32[1]{0:T(128)} %bitcast.27.factor_ref, bf16[8,8,40,128]{3,2,1,0:T(8,128)(2,1)S(1)} %all-to-all-done.4.own_ref, bf16[8,8,40,128]{3,2,1,0:T(8,128)(2,1)S(1)} %collective-permute-done.18.other_ref, bf16[3,640,512]{2,1,0:T(8,128)(2,1)S(1)} %copy-done.2), custom_call_target="tpu_custom_call" | custom-call | tf_op jit(solution)/shard_map/weight_gradient/pallas_call | solution.py:362
  (57 shorter events, 25.5 us)
Async XLA Ops:
  0.7 43.3 %copy-start = (bf16[3,512,1024]{2,1,0:T(8,128)(2,1)S(1)}, bf16[3,512,1024]{2,1,0:T(8,128)(2,1)}, u32[]{:S(2)}) copy-start(bf16[3,512,1024]{2,1,0:T(8,128)(2,1)} %refs_8_.2) | copy-start | bytes 9437188
  4.0 12.0 %collective-permute-start.2 = (bf16[400,512]{1,0:T(8,128)(2,1)S(1)}, bf16[400,512]{1,0:T(8,128)(2,1)S(1)}, u32[]{:S(2)}, u32[]{:S(2)}) collective-permute-start(bf16[400,512]{1,0:T(8,128)(2,1)S(1)} %pack.1.refs_0_), channel_id=1, source_target_pairs={{0,96},{1,65},{16,112},{17,81},{32,0},{33,97},{48,16},{49,113},{64... | collective-permute-start | bytes 1228808 | tf_op jit(solution)/shard_map/ppermute | solution.py:394
  7.6 18.6 %collective-permute-start.1 = (bf16[400,512]{1,0:T(8,128)(2,1)S(1)}, bf16[400,512]{1,0:T(8,128)(2,1)S(1)}, u32[]{:S(2)}, u32[]{:S(2)}) collective-permute-start(bf16[400,512]{1,0:T(8,128)(2,1)S(1)} %pack.1.refs_0_), channel_id=1, source_target_pairs={{0,32},{1,97},{16,48},{17,113},{32,64},{33,1},{48,80},{49,17},{64,... | collective-permute-start | bytes 1228808 | tf_op jit(solution)/shard_map/ppermute | solution.py:394
  8.4 18.1 %collective-permute-start = (bf16[400,512]{1,0:T(8,128)(2,1)S(1)}, bf16[400,512]{1,0:T(8,128)(2,1)S(1)}, u32[]{:S(2)}, u32[]{:S(2)}) collective-permute-start(bf16[400,512]{1,0:T(8,128)(2,1)S(1)} %pack.1.refs_0_), channel_id=1, source_target_pairs={{0,16},{1,33},{16,0},{17,49},{32,48},{33,65},{48,32},{49,81},{64,8... | collective-permute-start | bytes 1228808 | tf_op jit(solution)/shard_map/ppermute | solution.py:394
  9.0 24.6 %collective-permute-start.3 = (bf16[400,512]{1,0:T(8,128)(2,1)S(1)}, bf16[400,512]{1,0:T(8,128)(2,1)S(1)}, u32[]{:S(2)}, u32[]{:S(2)}) collective-permute-start(bf16[400,512]{1,0:T(8,128)(2,1)S(1)} %pack.1.refs_0_), channel_id=1, source_target_pairs={{0,64},{1,17},{16,80},{17,1},{32,96},{33,49},{48,112},{49,33},{64,... | collective-permute-start | bytes 1228808 | tf_op jit(solution)/shard_map/ppermute | solution.py:394
  26.6 12.9 %collective-permute-start.6 = (bf16[400,512]{1,0:T(8,128)(2,1)S(1)}, bf16[400,512]{1,0:T(8,128)(2,1)S(1)}, u32[]{:S(2)}, u32[]{:S(2)}) collective-permute-start(bf16[400,512]{1,0:T(8,128)(2,1)S(1)} %get-tuple-element.38), channel_id=1, source_target_pairs={{0,64},{1,17},{16,80},{17,1},{32,96},{33,49},{48,112},{49,33},{64,... | collective-permute-start | bytes 1228808 | tf_op jit(solution)/shard_map/ppermute | solution.py:394
  29.8 9.7 %collective-permute-start.4 = (bf16[400,512]{1,0:T(8,128)(2,1)S(1)}, bf16[400,512]{1,0:T(8,128)(2,1)S(1)}, u32[]{:S(2)}, u32[]{:S(2)}) collective-permute-start(bf16[400,512]{1,0:T(8,128)(2,1)S(1)} %collective-permute-done.refs_1_), channel_id=1, source_target_pairs={{0,32},{1,17},{16,48},{17,1},{32,64},{33,49},{48,80},{49,33},{64,9... | collective-permute-start | bytes 1228808 | tf_op jit(solution)/shard_map/ppermute | solution.py:394
  29.9 14.0 %collective-permute-start.5 = (bf16[400,512]{1,0:T(8,128)(2,1)S(1)}, bf16[400,512]{1,0:T(8,128)(2,1)S(1)}, u32[]{:S(2)}, u32[]{:S(2)}) collective-permute-start(bf16[400,512]{1,0:T(8,128)(2,1)S(1)} %get-tuple-element.39), channel_id=1, source_target_pairs={{0,96},{1,17},{16,112},{17,1},{32,0},{33,49},{48,16},{49,33},{64,3... | collective-permute-start | bytes 1228808 | tf_op jit(solution)/shard_map/ppermute | solution.py:394
  49.9 31.9 %copy-start.1 = (bf16[3,640,512]{2,1,0:T(8,128)(2,1)}, bf16[3,640,512]{2,1,0:T(8,128)(2,1)S(1)}, u32[]{:S(2)}) copy-start(bf16[3,640,512]{2,1,0:T(8,128)(2,1)S(1)} %get-tuple-element.35.rows_ref) | copy-start | bytes 5898244
  82.0 30.8 %copy-start.3 = (bf16[1,128,1024]{2,1,0:T(8,128)(2,1)S(1)}, bf16[1,128,1024]{2,1,0:T(8,128)(2,1)}, u32[]{:S(2)}) copy-start(bf16[1,128,1024]{2,1,0:T(8,128)(2,1)} %param.8) | copy-start | bytes 786436
  95.0 17.8 %collective-permute-start.7 = (bf16[8,8,40,128]{3,2,1,0:T(8,128)(2,1)S(1)}, bf16[8,8,40,128]{3,2,1,0:T(8,128)(2,1)S(1)}, u32[]{:S(2)}, u32[]{:S(2)}) collective-permute-start(bf16[8,8,40,128]{3,2,1,0:T(8,128)(2,1)S(1)} %all_to_all.26.own_ref), channel_id=1, source_target_pairs={{0,1},{1,0},{2,3},{3,2},{4,5},{5,4},{6,7},{7,6},{8,9},{9,8},{10,11... | collective-permute-start | bytes 1966088 | tf_op jit(solution)/shard_map/ppermute | solution.py:34
  97.0 6.8 %collective-permute-start.14 = (bf16[48,1024]{1,0:T(8,128)(2,1)S(1)}, bf16[48,1024]{1,0:T(8,128)(2,1)S(1)}, u32[]{:S(2)}, u32[]{:S(2)}) collective-permute-start(bf16[48,1024]{1,0:T(8,128)(2,1)S(1)} %slice_bitcast_fusion.refs_0_), channel_id=1, source_target_pairs={{0,112},{16,96},{32,16},{48,0},{64,48},{80,32},{96,80},{112,64},{1... | collective-permute-start | bytes 294920 | tf_op jit(solution)/shard_map/ppermute | solution.py:438
  98.5 6.8 %collective-permute-start.13 = (bf16[48,1024]{1,0:T(8,128)(2,1)S(1)}, bf16[48,1024]{1,0:T(8,128)(2,1)S(1)}, u32[]{:S(2)}, u32[]{:S(2)}) collective-permute-start(bf16[48,1024]{1,0:T(8,128)(2,1)S(1)} %slice_bitcast_fusion.refs_0_), channel_id=1, source_target_pairs={{0,96},{16,112},{32,0},{48,16},{64,32},{80,48},{96,64},{112,80},{1... | collective-permute-start | bytes 294920 | tf_op jit(solution)/shard_map/ppermute | solution.py:438
  99.3 7.7 %collective-permute-start.12 = (bf16[48,1024]{1,0:T(8,128)(2,1)S(1)}, bf16[48,1024]{1,0:T(8,128)(2,1)S(1)}, u32[]{:S(2)}, u32[]{:S(2)}) collective-permute-start(bf16[48,1024]{1,0:T(8,128)(2,1)S(1)} %slice_bitcast_fusion.refs_0_), channel_id=1, source_target_pairs={{0,80},{16,64},{32,112},{48,96},{64,16},{80,0},{96,48},{112,32},{1... | collective-permute-start | bytes 294920 | tf_op jit(solution)/shard_map/ppermute | solution.py:438
  102.7 6.2 %collective-permute-start.11 = (bf16[48,1024]{1,0:T(8,128)(2,1)S(1)}, bf16[48,1024]{1,0:T(8,128)(2,1)S(1)}, u32[]{:S(2)}, u32[]{:S(2)}) collective-permute-start(bf16[48,1024]{1,0:T(8,128)(2,1)S(1)} %slice_bitcast_fusion.refs_0_), channel_id=1, source_target_pairs={{0,64},{16,80},{32,96},{48,112},{64,0},{80,16},{96,32},{112,48},{1... | collective-permute-start | bytes 294920 | tf_op jit(solution)/shard_map/ppermute | solution.py:438
  103.9 7.1 %collective-permute-start.10 = (bf16[48,1024]{1,0:T(8,128)(2,1)S(1)}, bf16[48,1024]{1,0:T(8,128)(2,1)S(1)}, u32[]{:S(2)}, u32[]{:S(2)}) collective-permute-start(bf16[48,1024]{1,0:T(8,128)(2,1)S(1)} %slice_bitcast_fusion.refs_0_), channel_id=1, source_target_pairs={{0,48},{16,32},{32,80},{48,64},{64,112},{80,96},{96,16},{112,0},{1... | collective-permute-start | bytes 294920 | tf_op jit(solution)/shard_map/ppermute | solution.py:438
  105.4 7.1 %collective-permute-start.9 = (bf16[48,1024]{1,0:T(8,128)(2,1)S(1)}, bf16[48,1024]{1,0:T(8,128)(2,1)S(1)}, u32[]{:S(2)}, u32[]{:S(2)}) collective-permute-start(bf16[48,1024]{1,0:T(8,128)(2,1)S(1)} %slice_bitcast_fusion.refs_0_), channel_id=1, source_target_pairs={{0,32},{16,48},{32,64},{48,80},{64,96},{80,112},{96,0},{112,16},{1... | collective-permute-start | bytes 294920 | tf_op jit(solution)/shard_map/ppermute | solution.py:438
  107.0 5.7 %collective-permute-start.8 = (bf16[48,1024]{1,0:T(8,128)(2,1)S(1)}, bf16[48,1024]{1,0:T(8,128)(2,1)S(1)}, u32[]{:S(2)}, u32[]{:S(2)}) collective-permute-start(bf16[48,1024]{1,0:T(8,128)(2,1)S(1)} %slice_bitcast_fusion.refs_0_), channel_id=1, source_target_pairs={{0,16},{16,0},{32,48},{48,32},{64,80},{80,64},{96,112},{112,96},{1... | collective-permute-start | bytes 294920 | tf_op jit(solution)/shard_map/ppermute | solution.py:438
  140.8 28.9 %all-to-all-start.3 = ((bf16[128,40,128]{2,1,0:T(8,128)(2,1)}), bf16[128,40,128]{2,1,0:T(8,128)(2,1)S(1)}, u32[]{:S(2)}, u32[]{:S(2)}) async-start(bf16[128,40,128]{2,1,0:T(8,128)(2,1)} %bitcast.24), calls=%async_computation.3 | async-start | bytes 2621440 | tf_op jit(solution)/shard_map/all_to_all | solution.py:381
  147.7 9.0 %collective-permute-start.15 = (f32[8,128]{1,0:T(8,128)S(1)}, f32[8,128]{1,0:T(8,128)S(1)}, u32[]{:S(2)}, u32[]{:S(2)}) collective-permute-start(f32[8,128]{1,0:T(8,128)S(1)} %get-tuple-element.29), channel_id=1, source_target_pairs={{0,16},{16,0},{1,17},{17,1},{2,18},{18,2},{3,19},{19,3},{4,20},{20... | collective-permute-start | bytes 12296 | tf_op jit(solution)/shard_map/ppermute | solution.py:34
  170.7 13.9 %all-to-all-start.4 = ((bf16[8,8,40,128]{3,2,1,0:T(8,128)(2,1)}), bf16[8,8,40,128]{3,2,1,0:T(8,128)(2,1)S(1)}, u32[]{:S(2)}, u32[]{:S(2)}) async-start(bf16[8,8,40,128]{3,2,1,0:T(8,128)(2,1)} %broadcast_in_dim.12), calls=%async_computation.4 | async-start | bytes 1310720 | tf_op jit(solution)/shard_map/all_to_all | solution.py:28
  174.3 2.5 %collective-permute-start.16 = (f32[8,128]{1,0:T(8,128)S(1)}, f32[8,128]{1,0:T(8,128)S(1)}, u32[]{:S(2)}, u32[]{:S(2)}) collective-permute-start(f32[8,128]{1,0:T(8,128)S(1)} %add.110), channel_id=1, source_target_pairs={{0,32},{32,0},{64,96},{96,64},{1,33},{33,1},{65,97},{97,65},{2,34}... | collective-permute-start | bytes 12296 | tf_op jit(solution)/shard_map/ppermute | solution.py:34
  184.7 8.1 %collective-permute-start.18 = (bf16[8,8,40,128]{3,2,1,0:T(8,128)(2,1)S(1)}, bf16[8,8,40,128]{3,2,1,0:T(8,128)(2,1)S(1)}, u32[]{:S(2)}, u32[]{:S(2)}) collective-permute-start(bf16[8,8,40,128]{3,2,1,0:T(8,128)(2,1)S(1)} %all-to-all-done.4.own_ref), channel_id=1, source_target_pairs={{0,1},{1,0},{2,3},{3,2},{4,5},{5,4},{6,7},{7,6},{8,9},{9,8},{10,11... | collective-permute-start | bytes 1966088 | tf_op jit(solution)/shard_map/ppermute | solution.py:34
  187.4 4.0 %collective-permute-start.17 = (f32[8,128]{1,0:T(8,128)S(1)}, f32[8,128]{1,0:T(8,128)S(1)}, u32[]{:S(2)}, u32[]{:S(2)}) collective-permute-start(f32[8,128]{1,0:T(8,128)S(1)} %add.111), channel_id=1, source_target_pairs={{0,64},{32,96},{64,0},{96,32},{1,65},{33,97},{65,1},{97,33},{2,66}... | collective-permute-start | bytes 12296 | tf_op jit(solution)/shard_map/ppermute | solution.py:34
  (5 other events, 86.1 us)

commit v3 on v2

v3 whole, which is shorter than its diff:
```python
import functools

import jax
import jax.numpy as jnp
from jax import lax
from jax.experimental import pallas as pl
from jax.experimental.pallas import tpu as pltpu
from jax.sharding import Mesh, PartitionSpec as P

NORM_EPS = 1e-05
GROUP = ("x", "yh")
RING = ("z", "yl")
CHIPS = ("x", "yh", "z", "yl")
ALL = CHIPS + ("c",)
OFFSETS = [(dx, dy) for dx in range(4) for dy in range(2)]
GROUPS = 8
HALF = 128
ROWS = 80
SPARE = HALF - ROWS
PIECE = ROWS // 2
MIB = 1 << 20
f32, bf16 = jnp.float32, jnp.bfloat16
SCALARS = pl.BlockSpec(memory_space=pltpu.SMEM)
VECTORS = pl.BlockSpec(memory_space=pltpu.VMEM)
ANYWHERE = pl.BlockSpec(memory_space=pl.ANY)


def group_at(dx, dy):
    return lax.rem(lax.axis_index("x") + dx, 4) * 2 + lax.rem(lax.axis_index("yh") + dy, 2)


def have_here(length):
    return jnp.clip(length - lax.axis_index("yh") * HALF, 0, HALF)


def spread(value, axes, count):
    return lax.all_to_all(
        jnp.broadcast_to(value[None], (count,) + value.shape), axes, 0, 0, tiled=True
    )


def swap(value, axis, bit, count):
    return lax.ppermute(value, axis, [(i, i ^ bit) for i in range(count)])


def pack_kernel(length_ref, cap_ref, mask_ref, out_ref):
    out_ref[0 : 3 * HALF, :] = cap_ref[...].reshape(3 * HALF, 512)
    lane = lax.broadcasted_iota(jnp.int32, (1, 512), 1)
    masked = (mask_ref[...] == 1).astype(f32)
    here = have_here(length_ref[0])
    near = lax.broadcasted_iota(jnp.int32, (1, HALF), 1) < here
    count = jnp.sum(jnp.where(near, masked, 0.0), axis=1, keepdims=True)
    place = lax.broadcasted_iota(jnp.int32, (HALF, 512), 0) - ROWS
    column = lax.broadcasted_iota(jnp.int32, (HALF, 512), 1)
    tiled = jnp.zeros((HALF, 512), f32)
    for g in range(GROUPS):
        tiled = jnp.where((column - SPARE * g == place) & (place >= 0), 1.0, tiled)
    repeated = jnp.dot(
        jnp.broadcast_to(masked, (8, HALF)).astype(bf16),
        tiled.astype(bf16),
        preferred_element_type=f32,
    )[0:1]
    have = jnp.zeros((1, 512), f32) + here.astype(f32)
    row = lax.broadcasted_iota(jnp.int32, (16, 512), 0)
    facts = jnp.where(row == 0, have, jnp.where(row == 1, repeated, 0.0))
    facts = jnp.where(row == 2, count + lane.astype(f32) * 0.0, facts)
    out_ref[3 * HALF : 3 * HALF + 16, :] = facts.astype(bf16)


def pack(lengths, captured, loss_mask):
    return pl.pallas_call(
        pack_kernel,
        in_specs=[SCALARS, VECTORS, VECTORS],
        out_specs=VECTORS,
        out_shape=jax.ShapeDtypeStruct((3 * HALF + 16, 512), bf16),
        compiler_params=pltpu.CompilerParams(vmem_limit_bytes=8 * MIB),
        name="pack",
    )(lengths, captured, loss_mask)


def split_by_core(block, first, mine_ref, other_ref, extra=None):
    for j in range(8):
        upper = block[0:PIECE, j * 128 : (j + 1) * 128]
        lower = block[PIECE:ROWS, j * 128 : (j + 1) * 128]
        mine = jnp.where(first, upper, lower)
        other = jnp.where(first, lower, upper)
        if extra is not None:
            mine = jnp.concatenate([mine, extra], axis=0)
            other = jnp.concatenate([other, jnp.zeros_like(extra)], axis=0)
        mine_ref[j] = mine.astype(bf16)
        other_ref[j] = other.astype(bf16)


def unite_kernel(*refs):
    blocks = refs[:GROUPS]
    hbm_weight, rows_ref, mine_ref, other_ref, slot_ref, fact_ref, cap_ref, weight_ref, sems = refs[
        GROUPS:
    ]
    core = lax.axis_index("c")
    places = [(0, 0), (0, 1), (3, 0), (1, 0), (2, 0), (3, 1), (1, 1), (2, 1)]
    copies = [
        pltpu.make_async_copy(block, cap_ref.at[group_at(*place)], sems.at[k])
        for k, (block, place) in enumerate(zip(blocks, places))
    ]
    loads = [
        pltpu.make_async_copy(hbm_weight.at[k], weight_ref.at[k], sems.at[GROUPS + k])
        for k in range(3)
    ]
    for copy in copies + loads:
        copy.start()
    for copy in copies:
        copy.wait()
    lane = lax.broadcasted_iota(jnp.int32, (1, 512), 1).astype(f32)
    have, before_more, before_less, facts = [], [], [], []
    more = less = total_count = jnp.zeros((1, 512), f32)
    for g in range(GROUPS):
        fact = cap_ref[g, 3 * HALF : 3 * HALF + 16, :].astype(f32)
        facts.append(fact[1:2])
        have.append(fact[0:1])
        before_more.append(more)
        before_less.append(less)
        more = more + jnp.maximum(have[g] - ROWS, 0.0)
        less = less + jnp.maximum(ROWS - have[g], 0.0)
        total_count = total_count + fact[2:3]
        fact_ref[g : g + 1, :] = fact[2:3, 0:128]
    order = jnp.full((1, 512), -1.0, f32)
    mask_pool = jnp.zeros((1, 512), f32)
    seq_pool = jnp.zeros((1, 512), f32)
    for g in range(GROUPS):
        place = lane - SPARE * g
        mine = (place >= 0) & (place < SPARE)
        order = jnp.where(mine & (place < have[g] - ROWS), before_more[g] + place, order)
        mask_pool = jnp.where(mine, facts[g], mask_pool)
        seq_pool = jnp.where(mine, float(g // 2), seq_pool)
    slot = jnp.full((1, 512), -1.0, f32)
    for g in range(GROUPS):
        offset = order - before_less[g]
        mine = (order >= 0) & (offset >= 0) & (offset < ROWS - have[g])
        slot = jnp.where(mine, ROWS * g + have[g] + offset, slot)
    slot_ref[...] = jnp.concatenate(
        [slot, mask_pool, seq_pool] + [jnp.zeros((1, 512), f32)] * 5, axis=0
    )
    for block in range(2):
        row = lax.broadcasted_iota(jnp.int32, (4 * ROWS, 384), 0) + block * 4 * ROWS
        pick = (row.astype(f32) == slot[:, :384]).astype(bf16)
        total = None
        for s in range(3):
            pool = cap_ref[:, s * HALF + ROWS : (s + 1) * HALF, :].reshape(384, 512)
            moved = jnp.dot(pick, pool, preferred_element_type=f32)
            kept = []
            for g in range(4 * block, 4 * block + 4):
                own = cap_ref[g, s * HALF : s * HALF + ROWS, :].astype(f32)
                within = lax.broadcasted_iota(jnp.int32, (ROWS, 512), 0).astype(f32) < have[g]
                base = (g - 4 * block) * ROWS
                kept.append(jnp.where(within, own, moved[base : base + ROWS]))
            rows = jnp.concatenate(kept, axis=0).astype(bf16)
            rows_ref[s, pl.ds(block * 4 * ROWS, 4 * ROWS), :] = rows
            if block == 0:
                loads[s].wait()
            term = jnp.dot(rows, weight_ref[s], preferred_element_type=f32)
            total = term if total is None else total + term
        for g in range(4):
            base = g * ROWS
            split_by_core(
                total[base : base + ROWS], core == 0, mine_ref.at[4 * block + g], other_ref.at[4 * block + g]
            )


def unite(blocks, weight):
    return pl.pallas_call(
        unite_kernel,
        in_specs=[ANYWHERE] * (GROUPS + 1),
        out_specs=[VECTORS] * 5,
        out_shape=(
            jax.ShapeDtypeStruct((3, GROUPS * ROWS, 512), bf16),
            jax.ShapeDtypeStruct((GROUPS, 8, PIECE, 128), bf16),
            jax.ShapeDtypeStruct((GROUPS, 8, PIECE, 128), bf16),
            jax.ShapeDtypeStruct((8, 512), f32),
            jax.ShapeDtypeStruct((GROUPS, 128), f32),
        ),
        scratch_shapes=[
            pltpu.VMEM((GROUPS, 3 * HALF + 16, 512), bf16),
            pltpu.VMEM(weight.shape, bf16),
            pltpu.SemaphoreType.DMA((GROUPS + 3,)),
        ],
        compiler_params=pltpu.CompilerParams(vmem_limit_bytes=52 * MIB),
        name="unite",
    )(*blocks, weight)


def head_kernel(length_ref, own_ref, other_ref, gain_ref, target_ref, mask_ref, slot_ref, *refs):
    spares = refs[:4]
    head_ref, logit_ref, chosen_ref, stat_ref, side_ref, united_ref = refs[4:10]
    wide, normed, held, pool, sems, pool_sems = refs[10:]
    width = wide.shape[1]
    tile = head_ref.shape[0] // 8
    loads = [
        pltpu.make_async_copy(
            head_ref.at[pl.ds(i * tile, tile)], held.at[pl.ds(i * tile, tile)], sems.at[i]
        )
        for i in range(8)
    ]
    moves = [
        pltpu.make_async_copy(spares[dx].at[dy], pool.at[group_at(-dx % 4, dy)], pool_sems.at[k])
        for k, (dx, dy) in enumerate(OFFSETS)
    ]
    for copy in moves + loads[:3]:
        copy.start()

    first = lax.axis_index("c") == 0
    wide[ROWS:HALF, :] = jnp.zeros((HALF - ROWS, width), f32)
    for g in range(GROUPS):
        for j in range(8):
            column = (g * 8 + j) * 128
            a = own_ref[j, g].astype(f32)
            b = other_ref[j, g].astype(f32)
            wide[0:PIECE, column : column + 128] = jnp.where(first, a, b)
            wide[PIECE:ROWS, column : column + 128] = jnp.where(first, b, a)
    square = jnp.zeros((HALF, 1), f32)
    for g in range(GROUPS):
        values = wide[:, g * 1024 : (g + 1) * 1024]
        square = square + jnp.sum(values * values, axis=1, keepdims=True)
    scale = lax.rsqrt(square / width + NORM_EPS)
    for g in range(GROUPS):
        part = slice(g * 1024, (g + 1) * 1024)
        values = wide[:, part]
        united_ref[:, part] = values[0:ROWS].astype(bf16)
        normed[part, :] = jnp.transpose(values * scale * gain_ref[:, part]).astype(bf16)

    for copy in moves:
        copy.wait()
    have = have_here(length_ref[0])
    row = lax.broadcasted_iota(jnp.int32, (HALF, 384), 0) + group_at(0, 0) * ROWS
    pick = (row.astype(f32) == slot_ref[0:1, 0:384]).astype(bf16)
    moved = jnp.dot(pick, pool[...].reshape(384, pool.shape[2]), preferred_element_type=f32)
    kept = lax.broadcasted_iota(jnp.int32, moved.shape, 0) < have
    chosen = jnp.transpose(jnp.where(kept, target_ref[...].astype(f32), moved))
    chosen_ref[...] = chosen
    traits = lax.dot_general(
        slot_ref[:, 0:384].astype(bf16), pick, (((1,), (1,)), ((), ())), preferred_element_type=f32
    )
    lane = lax.broadcasted_iota(jnp.int32, (1, HALF), 1)
    masked = (mask_ref[...] == 1).astype(f32)
    valid = jnp.where(lane < have, masked, traits[1:2])
    valid = jnp.where(lane < ROWS, valid, 0.0)
    sequence = jnp.where(lane < have, lax.axis_index("x").astype(f32), traits[2:3])
    scale_lane = jnp.transpose(jnp.broadcast_to(scale, (HALF, HALF)))[0:1]
    nothing = jnp.zeros((1, HALF), f32)
    side_ref[...] = jnp.concatenate([scale_lane, valid, sequence] + [nothing] * 5, axis=0)

    top_t = jnp.max(chosen, axis=0, keepdims=True)
    pow_t = jnp.exp(chosen - top_t)
    sum_t = jnp.sum(pow_t, axis=0, keepdims=True)
    dot_t = jnp.sum(pow_t * chosen, axis=0, keepdims=True)
    for i in range(0, 8, 2):
        for k in (i, i + 1):
            loads[k].wait()
            if k + 3 < 8:
                loads[k + 3].start()
        part = slice(i * tile, (i + 2) * tile)
        logit_ref[part, :] = jnp.dot(held[part, :], normed[...], preferred_element_type=f32)
    logits = logit_ref[...]
    top_d = jnp.max(logits, axis=0, keepdims=True)
    pow_d = jnp.exp(logits - top_d)
    stat_ref[...] = jnp.concatenate(
        [
            top_t,
            sum_t,
            dot_t,
            jnp.sum(pow_t * logits, axis=0, keepdims=True),
            top_d,
            jnp.sum(pow_d, axis=0, keepdims=True),
            jnp.sum(pow_d * logits, axis=0, keepdims=True),
            nothing,
        ],
        axis=0,
    )


def head_forward(lengths, own, other, gain, target, loss_mask, slots, spares, head):
    vocab, width = head.shape
    return pl.pallas_call(
        head_kernel,
        in_specs=[SCALARS] + [VECTORS] * 6 + [ANYWHERE] * 5,
        out_specs=[VECTORS] * 5,
        out_shape=(
            jax.ShapeDtypeStruct((vocab, HALF), f32),
            jax.ShapeDtypeStruct((vocab, HALF), f32),
            jax.ShapeDtypeStruct((8, HALF), f32),
            jax.ShapeDtypeStruct((8, HALF), f32),
            jax.ShapeDtypeStruct((ROWS, width), bf16),
        ),
        scratch_shapes=[
            pltpu.VMEM((HALF, width), f32),
            pltpu.VMEM((width, HALF), bf16),
            pltpu.VMEM((vocab, width), bf16),
            pltpu.VMEM((GROUPS, SPARE, vocab), bf16),
            pltpu.SemaphoreType.DMA((8,)),
            pltpu.SemaphoreType.DMA((GROUPS,)),
        ],
        compiler_params=pltpu.CompilerParams(vmem_limit_bytes=44 * MIB),
        name="head_forward",
    )(lengths, own, other, gain, target, loss_mask, slots, *spares, head)


def back_kernel(
    every_ref, logit_ref, chosen_ref, side_ref, gain_ref, united_ref, head_ref,
    mine_ref, other_ref, held, sems,
):
    width = gain_ref.shape[1]
    loads = [
        pltpu.make_async_copy(
            head_ref.at[:, pl.ds(g * 1024, 1024)], held.at[g], sems.at[g]
        )
        for g in range(GROUPS)
    ]
    for copy in loads[:3]:
        copy.start()
    every = every_ref[...]
    max_t = jnp.max(every[:, 0:1], axis=0)
    scale_t = jnp.exp(every[:, 0:1] - max_t[None])
    sum_t = jnp.sum(every[:, 1:2] * scale_t, axis=0)
    mean_tt = jnp.sum(every[:, 2:3] * scale_t, axis=0) / sum_t
    mean_tl = jnp.sum(every[:, 3:4] * scale_t, axis=0) / sum_t
    max_d = jnp.max(every[:, 4:5], axis=0)
    scale_d = jnp.exp(every[:, 4:5] - max_d[None])
    sum_d = jnp.sum(every[:, 5:6] * scale_d, axis=0)
    mean_dl = jnp.sum(every[:, 6:7] * scale_d, axis=0) / sum_d
    log_t = max_t + jnp.log(sum_t)
    log_d = max_d + jnp.log(sum_d)
    row_scale, valid, sequence = side_ref[0:1], side_ref[1:2], side_ref[2:3]
    kl = (mean_tt - mean_tl - log_t + log_d) * valid
    row = lax.broadcasted_iota(jnp.int32, (8, HALF), 0)
    sums = jnp.sum(jnp.where(row.astype(f32) == sequence, kl, 0.0), axis=1, keepdims=True)
    sums = jnp.broadcast_to(sums, (8, HALF))
    high = sums.astype(bf16).astype(f32)
    middle = (sums - high).astype(bf16).astype(f32)
    column = lax.broadcasted_iota(jnp.int32, (8, HALF), 1)
    third = jnp.where(column < 96, sums - high - middle, 0.0)
    sums = jnp.where(column < 32, high, jnp.where(column < 64, middle, third))

    weight = valid * row_scale
    grad = weight * (jnp.exp(logit_ref[...] - log_d) - jnp.exp(chosen_ref[...] - log_t))
    grad = jnp.transpose(grad)[0:ROWS].astype(bf16)
    lane = lax.broadcasted_iota(jnp.int32, (1, HALF), 1)
    share = ROWS // 16
    index = lax.axis_index(("z", "yl", "c"))
    mine = (lane >= index * share) & (lane < (index + 1) * share)
    cubic = jnp.where(mine, weight * row_scale * (mean_dl - mean_tl) / width, 0.0)
    cubic = jnp.transpose(jnp.broadcast_to(cubic, (HALF, HALF)))[0:ROWS, 0:1]
    for g in range(GROUPS):
        part = slice(g * 1024, (g + 1) * 1024)
        loads[g].wait()
        if g + 3 < GROUPS:
            loads[g + 3].start()
        block = jnp.dot(grad, held[g], preferred_element_type=f32)
        block = block * gain_ref[:, part] - cubic * united_ref[:, part].astype(f32)
        split_by_core(
            block, lax.axis_index("c") == 0, mine_ref.at[g], other_ref.at[g], sums
        )


def head_backward(every, logits, chosen, side, gain, united, head):
    vocab = head.shape[0]
    return pl.pallas_call(
        back_kernel,
        in_specs=[VECTORS] * 6 + [ANYWHERE],
        out_specs=[VECTORS] * 2,
        out_shape=(
            jax.ShapeDtypeStruct((GROUPS, 8, PIECE + 8, 128), bf16),
            jax.ShapeDtypeStruct((GROUPS, 8, PIECE + 8, 128), bf16),
        ),
        scratch_shapes=[
            pltpu.VMEM((GROUPS, vocab, 1024), bf16),
            pltpu.SemaphoreType.DMA((GROUPS,)),
        ],
        compiler_params=pltpu.CompilerParams(vmem_limit_bytes=44 * MIB),
        name="head_backward",
    )(every, logits, chosen, side, gain, united, head)


def grad_kernel(factor_ref, own_ref, other_ref, rows_ref, out_ref, wide, grads):
    @pl.when((pl.program_id(0) == 0) & (pl.program_id(1) == 0))
    def _():
        first = lax.axis_index("c") == 0
        for g in range(GROUPS):
            for j in range(8):
                a = own_ref[j, g].astype(f32)
                b = other_ref[j, g].astype(f32)
                base = g * ROWS
                wide[base : base + PIECE, j * 128 : (j + 1) * 128] = jnp.where(first, a, b)
                wide[base + PIECE : base + ROWS, j * 128 : (j + 1) * 128] = jnp.where(first, b, a)
        grads[...] = wide[...].astype(bf16)

    out_ref[0] = factor_ref[0] * lax.dot_general(
        rows_ref[0], grads[...], (((0,), (0,)), ((), ())), preferred_element_type=f32
    )


def weight_gradient(factor, own, other, rows):
    total = GROUPS * ROWS
    whole = lambda shape: pl.BlockSpec(shape, lambda s, i: (0,) * len(shape))
    return pl.pallas_call(
        grad_kernel,
        grid=(3, 2),
        in_specs=[
            SCALARS,
            whole((8, GROUPS, PIECE, 128)),
            whole((8, GROUPS, PIECE, 128)),
            pl.BlockSpec((1, total, 256), lambda s, i: (s, 0, i)),
        ],
        out_specs=pl.BlockSpec((1, 256, 1024), lambda s, i: (s, i, 0)),
        out_shape=jax.ShapeDtypeStruct((3, 512, 1024), f32),
        scratch_shapes=[pltpu.VMEM((total, 1024), f32), pltpu.VMEM((total, 1024), bf16)],
        compiler_params=pltpu.CompilerParams(vmem_limit_bytes=40 * MIB),
        name="weight_gradient",
    )(factor, own, other, rows)


def sum_kernel(piece_ref, out_ref, extra_ref):
    extra = jnp.zeros((8, 128), f32)
    for g in range(GROUPS):
        total = jnp.zeros((PIECE, 128), f32)
        for j in range(8):
            total = total + piece_ref[g * 8 + j, 0:PIECE, :].astype(f32)
        for k in range(8):
            out_ref[k, g] = total.astype(bf16)
        if piece_ref.shape[1] > PIECE:
            extra = extra + piece_ref[g * 8].astype(f32)[PIECE : PIECE + 8]
    extra_ref[...] = extra


def gather_sum(mine, other):
    pair = (mine.astype(f32) + swap(other, "c", 1, 2).astype(f32)).astype(bf16)
    received = lax.all_to_all(pair.reshape((64,) + pair.shape[2:]), CHIPS, 0, 0, tiled=True)
    copies, extra = pl.pallas_call(
        sum_kernel,
        in_specs=[VECTORS],
        out_specs=[VECTORS] * 2,
        out_shape=(
            jax.ShapeDtypeStruct((8, GROUPS, PIECE, 128), bf16),
            jax.ShapeDtypeStruct((8, 128), f32),
        ),
        compiler_params=pltpu.CompilerParams(vmem_limit_bytes=8 * MIB),
        name="sum_pieces",
    )(received)
    return copies, extra


def route(value, dx, dy):
    pairs = [(p * 2 + q, (p + dx) % 4 * 2 + (q ^ dy)) for p in range(4) for q in range(2)]
    return lax.ppermute(value, GROUP, pairs)


def gather_blocks(own):
    far = route(own, 2, 0)
    over = route(own, 0, 1)
    right = route(own, 3, 0)
    left = route(own, 1, 0)
    over_far = route(far, 0, 1)
    over_right = route(over, 3, 0)
    over_left = route(over, 1, 0)
    return [own, over, left, right, far, over_left, over_right, over_far]


def local(captured, target_logits, unite_weight, norm_gain, head_weight, lengths, loss_mask):
    width = norm_gain.shape[0]
    blocks = gather_blocks(pack(lengths, captured.reshape(3, HALF, 512), loss_mask))
    rows, mine, other, slots, counts = unite(blocks, unite_weight)

    target = target_logits.reshape(HALF, -1)
    spare = target[ROWS:]
    pair = jnp.stack([spare, route(spare, 0, 1)])
    mine, pair = lax.optimization_barrier((mine, pair))
    spares = [pair] + [route(pair, dx, 0) for dx in range(1, 4)]
    copies, _ = gather_sum(mine, other)
    copies, *spares = lax.optimization_barrier((copies, *spares))
    own_united = lax.all_to_all(copies, RING, 0, 0, tiled=True)
    other_united = swap(own_united, "c", 1, 2)
    gain = norm_gain.reshape(1, width)
    logits, chosen, stats, side, united = head_forward(
        lengths, own_united, other_united, gain, target, loss_mask, slots, spares, head_weight
    )
    every = spread(stats, ("z", "yl", "c"), 16)
    mine, other = head_backward(every, logits, chosen, side, gain, united, head_weight)
    copies, sums = gather_sum(mine, other)
    own_grad = lax.all_to_all(copies, RING, 0, 0, tiled=True)
    x = lax.axis_index("x")
    counts = counts[:, 0]
    factor = (2 * HALF) / jnp.maximum(jnp.sum(counts), 1.0)
    here = lax.iota(jnp.int32, GROUPS)
    count_seq = jnp.sum(jnp.where(here // 2 == x, counts, 0.0))
    seq_sum = jnp.sum(jnp.where(here[:, None] == x, sums, 0.0)) / 32.0
    seq_kl = (seq_sum / jnp.maximum(count_seq, 1.0)).reshape(1)
    own_grad, seq_kl, factor = lax.optimization_barrier((own_grad, seq_kl, factor))
    other_grad = swap(own_grad, "c", 1, 2)
    unite_grad = weight_gradient(factor.reshape(1), own_grad, other_grad, rows)
    return (seq_kl, unite_grad)


def solution(mesh):
    fine = Mesh(mesh.devices.reshape(4, 2, 4, 2, 2), ALL)
    tensor = ("z", "yl", "c")
    placed = (
        P(None, "x", "yh", tensor),
        P("x", "yh", tensor),
        P(None, tensor, GROUP),
        P(),
        P(tensor, None),
        P("x"),
        P("x", "yh"),
    )
    return jax.shard_map(
        local,
        mesh=fine,
        in_specs=placed,
        out_specs=(P("x"), P(None, tensor, GROUP)),
        check_vma=False,
    )
```

time: 200 us -> 175 us (0.88)
  waiting for transfers between devices: 59.4 us -> 44.7 us
  blocking collectives: 55.2 us -> 43.9 us
    all_to_all x2 -> x1, blocking collectives: 23.3 us -> 8.66 us  [spread(): lax.all_to_all(jnp.broadcast_to(value[None], (count,) + value.shape), axe...]
    ppermute x14 -> x11, waiting for transfers between devices: 29.5 us -> 23.8 us  [route(): return lax.ppermute(value, GROUP, pairs)]
    all_to_all x2, waiting for transfers between devices: 20.8 us -> 15.5 us  [the longest x1 9.73 us: gather_sum(): lax.all_to_all(pair.reshape((64,) + pair.shape[2:]), CHIPS, 0, 0, tiled=T...]
    ppermute x14 -> x11, starting transfers between devices: 25.1 us -> 20.4 us  [route(): return lax.ppermute(value, GROUP, pairs)]
    all_to_all x2, starting transfers between devices: 10.4 us -> 14.4 us  [the longest x1 10.9 us: gather_sum(): lax.all_to_all(pair.reshape((64,) + pair.shape[2:]), CHIPS, 0, 0, tiled=T...]
    ppermute x5 -> x4, waiting for transfers between devices: 9.07 us -> 5.36 us  [swap(): return lax.ppermute(value, axis, [(i, i ^ bit) for i in range(count)])]
    all_to_all x1 -> x2, blocking collectives: 31.9 us -> 35.2 us  [the longest x1 21 us: gather_sum(): lax.all_to_all(pair.reshape((64,) + pair.shape[2:]), CHIPS, 0, 0, tiled=T...]
    convert_element_type x0 -> x2, other arithmetic: none -> 2.32 us  [gather_sum(): pair = (mine.astype(f32) + swap(other, 'c', 1, 2).astype(f32)).astype(bf16)]
  transfers between devices with their start and end apart: 21 -> 17, of which waited for: 14 -> 12; matrix products, arithmetic and copies ran while one was open for 2% -> 1% of each run, Pallas kernels for 0% -> 0%
where the time goes in v3:
time: 175 us; the launch traced here: 174 us
  waiting for transfers between devices  44.7 us (26%)
  blocking collectives  43.9 us (25%)
  starting transfers between devices  42.3 us (24%)
  Pallas kernels  31.5 us (18%)
  between operations  4.58 us (3%)
  other arithmetic  4.27 us (2%)
  local copies, waits for them, and re-layouts  3.17 us (2%)
    ppermute x11, waiting for transfers between devices, route(): return lax.ppermute(value, GROUP, pairs)  23.8 us
    all_to_all x1, blocking collectives, gather_sum(): lax.all_to_all(pair.reshape((64,) + pair.shape[2:]), CHIPS, 0, 0, tiled=T...  21 us
    ppermute x11, starting transfers between devices, route(): return lax.ppermute(value, GROUP, pairs)  20.4 us
    all_to_all x1, blocking collectives, local(): own_united = lax.all_to_all(copies, RING, 0, 0, tiled=True)  14.2 us
    all_to_all x1, starting transfers between devices, gather_sum(): lax.all_to_all(pair.reshape((64,) + pair.shape[2:]), CHIPS, 0, 0, tiled=T...  10.9 us
    all_to_all x1, waiting for transfers between devices, gather_sum(): lax.all_to_all(pair.reshape((64,) + pair.shape[2:]), CHIPS, 0, 0, tiled=T...  9.73 us
    pallas_call x1, Pallas kernels, head_forward(): pl.pallas_call(head_kernel, in_specs=[SCALARS] + [VECTORS] * 6 + [ANYWHER...  9.44 us
    all_to_all x1, blocking collectives, spread(): lax.all_to_all(jnp.broadcast_to(value[None], (count,) + value.shape), axe...  8.66 us
  transfers between devices with their start and end apart: 17, of which 12 were waited for; matrix products, arithmetic and copies ran while one was open for 1% of the time, Pallas kernels for 0%

profile of v3, /device:TPU:1, one launch (start us, length us, event | category | flops | bytes accessed | tf_op | source)
XLA Modules:
  0.0 174.4 jit_solution(16186636858111675193)
XLA Ops:
  3.1 3.6 %collective-permute-start.3 = (bf16[400,512]{1,0:T(8,128)(2,1)S(1)}, bf16[400,512]{1,0:T(8,128)(2,1)S(1)}, u32[]{:S(2)}, u32[]{:S(2)}) collective-permute-start(bf16[400,512]{1,0:T(8,128)(2,1)S(1)} %pack.1.refs_0_), channel_id=1, source_target_pairs={{0,64},{16,80},{32,96},{48,112},{64,0},{80,16},{96,32},{112,48},{1... | collective-permute-start | bytes 1228808 | tf_op jit(solution)/shard_map/ppermute | solution.py:452
  6.7 2.9 %collective-permute-start = (bf16[400,512]{1,0:T(8,128)(2,1)S(1)}, bf16[400,512]{1,0:T(8,128)(2,1)S(1)}, u32[]{:S(2)}, u32[]{:S(2)}) collective-permute-start(bf16[400,512]{1,0:T(8,128)(2,1)S(1)} %pack.1.refs_0_), channel_id=1, source_target_pairs={{0,16},{16,0},{32,48},{48,32},{64,80},{80,64},{96,112},{112,96},{1... | collective-permute-start | bytes 1228808 | tf_op jit(solution)/shard_map/ppermute | solution.py:452
  11.1 4.3 %collective-permute-done.3.refs_4_ = bf16[400,512]{1,0:T(8,128)(2,1)S(1)} collective-permute-done((bf16[400,512]{1,0:T(8,128)(2,1)S(1)}, bf16[400,512]{1,0:T(8,128)(2,1)S(1)}, u32[]{:S(2)}, u32[]{:S(2)}) %collective-permute-start.3) | collective-permute-done | bytes 409632 | tf_op jit(solution)/shard_map/ppermute | solution.py:452
  15.4 3.3 %collective-permute-start.6 = (bf16[400,512]{1,0:T(8,128)(2,1)S(1)}, bf16[400,512]{1,0:T(8,128)(2,1)S(1)}, u32[]{:S(2)}, u32[]{:S(2)}) collective-permute-start(bf16[400,512]{1,0:T(8,128)(2,1)S(1)} %collective-permute-done.3.refs_4_), channel_id=1, source_target_pairs={{0,16},{16,0},{32,48},{48,32},{64,80},{80,64},{96,112},{112,96},{1... | collective-permute-start | bytes 1228808 | tf_op jit(solution)/shard_map/ppermute | solution.py:452
  18.8 2.5 %collective-permute-start.5 = (bf16[400,512]{1,0:T(8,128)(2,1)S(1)}, bf16[400,512]{1,0:T(8,128)(2,1)S(1)}, u32[]{:S(2)}, u32[]{:S(2)}) collective-permute-start(bf16[400,512]{1,0:T(8,128)(2,1)S(1)} %collective-permute-done.refs_1_), channel_id=1, source_target_pairs={{0,96},{16,112},{32,0},{48,16},{64,32},{80,48},{96,64},{112,80},{1... | collective-permute-start | bytes 1228808 | tf_op jit(solution)/shard_map/ppermute | solution.py:452
  21.2 3.5 %collective-permute-done.2.refs_3_ = bf16[400,512]{1,0:T(8,128)(2,1)S(1)} collective-permute-done((bf16[400,512]{1,0:T(8,128)(2,1)S(1)}, bf16[400,512]{1,0:T(8,128)(2,1)S(1)}, u32[]{:S(2)}, u32[]{:S(2)}) %collective-permute-start.2) | collective-permute-done | bytes 409632 | tf_op jit(solution)/shard_map/ppermute | solution.py:452
  25.6 7.9 %collective-permute-done.5.refs_6_ = bf16[400,512]{1,0:T(8,128)(2,1)S(1)} collective-permute-done((bf16[400,512]{1,0:T(8,128)(2,1)S(1)}, bf16[400,512]{1,0:T(8,128)(2,1)S(1)}, u32[]{:S(2)}, u32[]{:S(2)}) %collective-permute-start.5) | collective-permute-done | bytes 409632 | tf_op jit(solution)/shard_map/ppermute | solution.py:452
  35.0 7.7 %unite.1 = (bf16[3,640,512]{2,1,0:T(8,128)(2,1)}, bf16[8,8,40,128]{3,2,1,0:T(8,128)(2,1)}, bf16[8,8,40,128]{3,2,1,0:T(8,128)(2,1)}, f32[8,512]{1,0:T(8,128)S(1)}, f32[8,128]{1,0:T(8,128)S(1)}) custom-call(bf16[400,512]{1,0:T(8,128)(2,1)S(1)} %pack.1.refs_0_, bf16[400,512]{1,0:T(8,128)(2,1)S(1)} %collective-permute-done.refs_1_, ...), custom_call_target="tpu_custom_call" | custom-call | tf_op jit(solution)/shard_map/unite/pallas_call | solution.py:170
  44.3 3.0 %collective-permute-start.7 = (bf16[48,1024]{1,0:T(8,128)(2,1)S(1)}, bf16[48,1024]{1,0:T(8,128)(2,1)S(1)}, u32[]{:S(2)}, u32[]{:S(2)}) collective-permute-start(bf16[48,1024]{1,0:T(8,128)(2,1)S(1)} %get-tuple-element.55), channel_id=1, source_target_pairs={{0,16},{16,0},{32,48},{48,32},{64,80},{80,64},{96,112},{112,96},{1... | collective-permute-start | bytes 294920 | tf_op jit(solution)/shard_map/ppermute | solution.py:452
  47.3 3.0 %collective-permute-done.7 = bf16[48,1024]{1,0:T(8,128)(2,1)S(1)} collective-permute-done((bf16[48,1024]{1,0:T(8,128)(2,1)S(1)}, bf16[48,1024]{1,0:T(8,128)(2,1)S(1)}, u32[]{:S(2)}, u32[]{:S(2)}) %collective-permute-start.7) | collective-permute-done | bytes 98336 | tf_op jit(solution)/shard_map/ppermute | solution.py:452
  52.4 10.9 %all-to-all-start = ((bf16[64,40,128]{2,1,0:T(8,128)(2,1)}), bf16[64,40,128]{2,1,0:T(8,128)(2,1)S(1)}, u32[]{:S(2)}, u32[]{:S(2)}) async-start(bf16[64,40,128]{2,1,0:T(8,128)(2,1)} %bitcast.3), calls=%async_computation | async-start | bytes 1310720 | tf_op jit(solution)/shard_map/all_to_all | solution.py:435
  63.3 2.5 %collective-permute-start.11 = (bf16[2,48,1024]{2,1,0:T(8,128)(2,1)S(1)}, bf16[2,48,1024]{2,1,0:T(8,128)(2,1)S(1)}, u32[]{:S(2)}, u32[]{:S(2)}) collective-permute-start(bf16[2,48,1024]{2,1,0:T(8,128)(2,1)S(1)} %pad_maximum_fusion.refs_0_), channel_id=1, source_target_pairs={{0,96},{16,112},{32,0},{48,16},{64,32},{80,48},{96,64},{112,80},{1... | collective-permute-start | bytes 589832 | tf_op jit(solution)/shard_map/ppermute | solution.py:452
  66.8 9.7 %all-to-all-done.piece_ref = bf16[64,40,128]{2,1,0:T(8,128)(2,1)S(1)} async-done(((bf16[64,40,128]{2,1,0:T(8,128)(2,1)}), bf16[64,40,128]{2,1,0:T(8,128)(2,1)S(1)}, u32[]{:S(2)}, u32[]{:S(2)}) %all-to-all-start) | async-done | bytes 655392 | tf_op jit(solution)/shard_map/all_to_all | solution.py:435
  77.2 4.3 %collective-permute-done.9.refs_1_ = bf16[2,48,1024]{2,1,0:T(8,128)(2,1)S(1)} collective-permute-done((bf16[2,48,1024]{2,1,0:T(8,128)(2,1)S(1)}, bf16[2,48,1024]{2,1,0:T(8,128)(2,1)S(1)}, u32[]{:S(2)}, u32[]{:S(2)}) %collective-permute-start.9) | collective-permute-done | bytes 196640 | tf_op jit(solution)/shard_map/ppermute | solution.py:452
  81.5 14.2 %all_to_all.25.own_ref = bf16[8,8,40,128]{3,2,1,0:T(8,128)(2,1)S(1)} all-to-all(bf16[8,8,40,128]{3,2,1,0:T(8,128)(2,1)S(1)} %get-tuple-element.32), channel_id=1, replica_groups=mesh['x'=4,'yh'=2,'z'=4,'yl'=2,'c'=2] {'z','yl'}, dimensions={0} | all-to-all | bytes 1310720 | tf_op jit(solution)/shard_map/all_to_all | solution.py:478
  95.7 2.8 %collective-permute-start.12 = (bf16[8,8,40,128]{3,2,1,0:T(8,128)(2,1)S(1)}, bf16[8,8,40,128]{3,2,1,0:T(8,128)(2,1)S(1)}, u32[]{:S(2)}, u32[]{:S(2)}) collective-permute-start(bf16[8,8,40,128]{3,2,1,0:T(8,128)(2,1)S(1)} %all_to_all.25.own_ref), channel_id=1, source_target_pairs={{0,1},{1,0},{2,3},{3,2},{4,5},{5,4},{6,7},{7,6},{8,9},{9,8},{10,11... | collective-permute-start | bytes 1966088 | tf_op jit(solution)/shard_map/ppermute | solution.py:43
  100.2 9.4 %head_forward.1 = (f32[1024,128]{1,0:T(8,128)S(1)}, f32[1024,128]{1,0:T(8,128)S(1)}, f32[8,128]{1,0:T(8,128)S(1)}, f32[8,128]{1,0:T(8,128)S(1)}, bf16[80,8192]{1,0:T(8,128)(2,1)S(1)}) custom-call(s32[1]{0:T(128)S(6)} %copy.9.length_ref, bf16[8,8,40,128]{3,2,1,0:T(8,128)(2,1)S(1)} %all_to_all.25.own_ref, ...), custom_call_target="tpu_custom_call" | custom-call | tf_op jit(solution)/shard_map/head_forward/pallas_call | solution.py:282
  109.6 8.7 %all_to_all.26.every_ref = f32[16,8,128]{2,1,0:T(8,128)S(1)} all-to-all(f32[16,8,128]{2,1,0:T(8,128)S(1)} %broadcast_in_dim.23), channel_id=1, replica_groups=mesh['x'=4,'yh'=2,'z'=4,'yl'=2,'c'=2] {'z','yl','c'}, dimensions={0} | all-to-all | bytes 131072 | tf_op jit(solution)/shard_map/all_to_all | solution.py:37
  118.3 7.0 %head_backward.1 = (bf16[8,8,48,128]{3,2,1,0:T(8,128)(2,1)S(1)}, bf16[8,8,48,128]{3,2,1,0:T(8,128)(2,1)S(1)}) custom-call(f32[16,8,128]{2,1,0:T(8,128)S(1)} %all_to_all.26.every_ref, f32[1024,128]{1,0:T(8,128)S(1)} %get-tuple-element.39.logit_ref, f32[1024,128]{1,0:T(8,128)S(1)} %get-tuple-element.40.chosen_ref, f32[8,128]{1,0:T(8,128)S(1)} %get-tuple-element.41.side_ref, ...), custom_call_target="tpu_custom_call" | custom-call | tf_op jit(solution)/shard_map/head_backward/pallas_call | solution.py:365
  127.9 21.0 %all_to_all.27.piece_ref = bf16[64,48,128]{2,1,0:T(8,128)(2,1)S(1)} all-to-all(bf16[64,48,128]{2,1,0:T(8,128)(2,1)S(1)} %bitcast.14), channel_id=1, replica_groups=mesh['x'=4,'yh'=2,'z'=4,'yl'=2,'c'=2] {'x','yh','z','yl'}, dimensions={0} | all-to-all | bytes 1572864 | tf_op jit(solution)/shard_map/all_to_all | solution.py:435
  149.9 3.5 %all-to-all-start.4 = ((bf16[8,8,40,128]{3,2,1,0:T(8,128)(2,1)}), bf16[8,8,40,128]{3,2,1,0:T(8,128)(2,1)S(1)}, u32[]{:S(2)}, u32[]{:S(2)}) async-start(bf16[8,8,40,128]{3,2,1,0:T(8,128)(2,1)} %get-tuple-element.45), calls=%async_computation.4 | async-start | bytes 1310720 | tf_op jit(solution)/shard_map/all_to_all | solution.py:487
  157.4 5.8 %all-to-all-done.4.own_ref = bf16[8,8,40,128]{3,2,1,0:T(8,128)(2,1)S(1)} async-done(((bf16[8,8,40,128]{3,2,1,0:T(8,128)(2,1)}), bf16[8,8,40,128]{3,2,1,0:T(8,128)(2,1)S(1)}, u32[]{:S(2)}, u32[]{:S(2)}) %all-to-all-start.4) | async-done | bytes 655392 | tf_op jit(solution)/shard_map/all_to_all | solution.py:487
  163.2 2.6 %collective-permute-start.14 = (bf16[8,8,40,128]{3,2,1,0:T(8,128)(2,1)S(1)}, bf16[8,8,40,128]{3,2,1,0:T(8,128)(2,1)S(1)}, u32[]{:S(2)}, u32[]{:S(2)}) collective-permute-start(bf16[8,8,40,128]{3,2,1,0:T(8,128)(2,1)S(1)} %all-to-all-done.4.own_ref), channel_id=1, source_target_pairs={{0,1},{1,0},{2,3},{3,2},{4,5},{5,4},{6,7},{7,6},{8,9},{9,8},{10,11... | collective-permute-start | bytes 1966088 | tf_op jit(solution)/shard_map/ppermute | solution.py:43
  167.6 5.7 %weight_gradient.1 = f32[3,512,1024]{2,1,0:T(8,128)} custom-call(f32[1]{0:T(128)} %bitcast.8.factor_ref, bf16[8,8,40,128]{3,2,1,0:T(8,128)(2,1)S(1)} %all-to-all-done.4.own_ref, bf16[8,8,40,128]{3,2,1,0:T(8,128)(2,1)S(1)} %collective-permute-done.14.other_ref, bf16[3,640,512]{2,1,0:T(8,128)(2,1)S(1)} %copy-done), custom_call_target="tpu_custom_call" | custom-call | tf_op jit(solution)/shard_map/weight_gradient/pallas_call | solution.py:403
  (49 shorter events, 20.1 us)
Async XLA Ops:
  1.3 1.0 copy-start.2
  3.1 41.2 %copy-start.1 = (bf16[1,128,1024]{2,1,0:T(8,128)(2,1)S(1)}, bf16[1,128,1024]{2,1,0:T(8,128)(2,1)}, u32[]{:S(2)}) copy-start(bf16[1,128,1024]{2,1,0:T(8,128)(2,1)} %param.8) | copy-start | bytes 786436
  3.1 12.3 %collective-permute-start.3 = (bf16[400,512]{1,0:T(8,128)(2,1)S(1)}, bf16[400,512]{1,0:T(8,128)(2,1)S(1)}, u32[]{:S(2)}, u32[]{:S(2)}) collective-permute-start(bf16[400,512]{1,0:T(8,128)(2,1)S(1)} %pack.1.refs_0_), channel_id=1, source_target_pairs={{0,64},{16,80},{32,96},{48,112},{64,0},{80,16},{96,32},{112,48},{1... | collective-permute-start | bytes 1228808 | tf_op jit(solution)/shard_map/ppermute | solution.py:452
  6.7 12.1 %collective-permute-start = (bf16[400,512]{1,0:T(8,128)(2,1)S(1)}, bf16[400,512]{1,0:T(8,128)(2,1)S(1)}, u32[]{:S(2)}, u32[]{:S(2)}) collective-permute-start(bf16[400,512]{1,0:T(8,128)(2,1)S(1)} %pack.1.refs_0_), channel_id=1, source_target_pairs={{0,16},{16,0},{32,48},{48,32},{64,80},{80,64},{96,112},{112,96},{1... | collective-permute-start | bytes 1228808 | tf_op jit(solution)/shard_map/ppermute | solution.py:452
  9.6 15.1 %collective-permute-start.2 = (bf16[400,512]{1,0:T(8,128)(2,1)S(1)}, bf16[400,512]{1,0:T(8,128)(2,1)S(1)}, u32[]{:S(2)}, u32[]{:S(2)}) collective-permute-start(bf16[400,512]{1,0:T(8,128)(2,1)S(1)} %pack.1.refs_0_), channel_id=1, source_target_pairs={{0,96},{16,112},{32,0},{48,16},{64,32},{80,48},{96,64},{112,80},{1... | collective-permute-start | bytes 1228808 | tf_op jit(solution)/shard_map/ppermute | solution.py:452
  10.5 14.5 %collective-permute-start.1 = (bf16[400,512]{1,0:T(8,128)(2,1)S(1)}, bf16[400,512]{1,0:T(8,128)(2,1)S(1)}, u32[]{:S(2)}, u32[]{:S(2)}) collective-permute-start(bf16[400,512]{1,0:T(8,128)(2,1)S(1)} %pack.1.refs_0_), channel_id=1, source_target_pairs={{0,32},{16,48},{32,64},{48,80},{64,96},{80,112},{96,0},{112,16},{1... | collective-permute-start | bytes 1228808 | tf_op jit(solution)/shard_map/ppermute | solution.py:452
  15.4 18.1 %copy-start.6 = (bf16[400,512]{1,0:T(8,128)(2,1)}, bf16[400,512]{1,0:T(8,128)(2,1)S(1)}, u32[]{:S(2)}) copy-start(bf16[400,512]{1,0:T(8,128)(2,1)S(1)} %collective-permute-done.3.refs_4_) | copy-start | bytes 1228804
  15.4 10.2 %collective-permute-start.6 = (bf16[400,512]{1,0:T(8,128)(2,1)S(1)}, bf16[400,512]{1,0:T(8,128)(2,1)S(1)}, u32[]{:S(2)}, u32[]{:S(2)}) collective-permute-start(bf16[400,512]{1,0:T(8,128)(2,1)S(1)} %collective-permute-done.3.refs_4_), channel_id=1, source_target_pairs={{0,16},{16,0},{32,48},{48,32},{64,80},{80,64},{96,112},{112,96},{1... | collective-permute-start | bytes 1228808 | tf_op jit(solution)/shard_map/ppermute | solution.py:452
  18.8 14.7 %collective-permute-start.5 = (bf16[400,512]{1,0:T(8,128)(2,1)S(1)}, bf16[400,512]{1,0:T(8,128)(2,1)S(1)}, u32[]{:S(2)}, u32[]{:S(2)}) collective-permute-start(bf16[400,512]{1,0:T(8,128)(2,1)S(1)} %collective-permute-done.refs_1_), channel_id=1, source_target_pairs={{0,96},{16,112},{32,0},{48,16},{64,32},{80,48},{96,64},{112,80},{1... | collective-permute-start | bytes 1228808 | tf_op jit(solution)/shard_map/ppermute | solution.py:452
  21.2 12.2 %collective-permute-start.4 = (bf16[400,512]{1,0:T(8,128)(2,1)S(1)}, bf16[400,512]{1,0:T(8,128)(2,1)S(1)}, u32[]{:S(2)}, u32[]{:S(2)}) collective-permute-start(bf16[400,512]{1,0:T(8,128)(2,1)S(1)} %collective-permute-done.refs_1_), channel_id=1, source_target_pairs={{0,32},{16,48},{32,64},{48,80},{64,96},{80,112},{96,0},{112,16},{1... | collective-permute-start | bytes 1228808 | tf_op jit(solution)/shard_map/ppermute | solution.py:452
  25.6 7.9 %copy-start.7 = (bf16[400,512]{1,0:T(8,128)(2,1)}, bf16[400,512]{1,0:T(8,128)(2,1)S(1)}, u32[]{:S(2)}) copy-start(bf16[400,512]{1,0:T(8,128)(2,1)S(1)} %collective-permute-done.6.refs_7_) | copy-start | bytes 1228804
  42.6 7.7 %collective-permute-start.8 = (bf16[8,8,40,128]{3,2,1,0:T(8,128)(2,1)}, bf16[8,8,40,128]{3,2,1,0:T(8,128)(2,1)S(1)}, u32[]{:S(2)}, u32[]{:S(2)}) collective-permute-start(bf16[8,8,40,128]{3,2,1,0:T(8,128)(2,1)} %get-tuple-element.29), channel_id=1, source_target_pairs={{0,1},{1,0},{2,3},{3,2},{4,5},{5,4},{6,7},{7,6},{8,9},{9,8},{10,11... | collective-permute-start | bytes 1966088 | tf_op jit(solution)/shard_map/ppermute | solution.py:43
  44.3 6.0 %collective-permute-start.7 = (bf16[48,1024]{1,0:T(8,128)(2,1)S(1)}, bf16[48,1024]{1,0:T(8,128)(2,1)S(1)}, u32[]{:S(2)}, u32[]{:S(2)}) collective-permute-start(bf16[48,1024]{1,0:T(8,128)(2,1)S(1)} %get-tuple-element.55), channel_id=1, source_target_pairs={{0,16},{16,0},{32,48},{48,32},{64,80},{80,64},{96,112},{112,96},{1... | collective-permute-start | bytes 294920 | tf_op jit(solution)/shard_map/ppermute | solution.py:452
  52.4 47.8 %copy-start.3 = (f32[8192]{0:T(1024)S(1)}, f32[8192]{0:T(1024)}, u32[]{:S(2)}) copy-start(f32[8192]{0:T(1024)} %param.10) | copy-start | bytes 98308
  52.4 47.8 %copy-start.5 = (s32[1,128]{1,0:T(1,128)S(1)}, s32[1,128]{1,0:T(1,128)}, u32[]{:S(2)}) copy-start(s32[1,128]{1,0:T(1,128)} %mask_ref.3) | copy-start | bytes 1540
  52.4 24.2 %all-to-all-start = ((bf16[64,40,128]{2,1,0:T(8,128)(2,1)}), bf16[64,40,128]{2,1,0:T(8,128)(2,1)S(1)}, u32[]{:S(2)}, u32[]{:S(2)}) async-start(bf16[64,40,128]{2,1,0:T(8,128)(2,1)} %bitcast.3), calls=%async_computation | async-start | bytes 1310720 | tf_op jit(solution)/shard_map/all_to_all | solution.py:435
  63.3 13.9 %collective-permute-start.11 = (bf16[2,48,1024]{2,1,0:T(8,128)(2,1)S(1)}, bf16[2,48,1024]{2,1,0:T(8,128)(2,1)S(1)}, u32[]{:S(2)}, u32[]{:S(2)}) collective-permute-start(bf16[2,48,1024]{2,1,0:T(8,128)(2,1)S(1)} %pad_maximum_fusion.refs_0_), channel_id=1, source_target_pairs={{0,96},{16,112},{32,0},{48,16},{64,32},{80,48},{96,64},{112,80},{1... | collective-permute-start | bytes 589832 | tf_op jit(solution)/shard_map/ppermute | solution.py:452
  65.8 11.4 %collective-permute-start.10 = (bf16[2,48,1024]{2,1,0:T(8,128)(2,1)S(1)}, bf16[2,48,1024]{2,1,0:T(8,128)(2,1)S(1)}, u32[]{:S(2)}, u32[]{:S(2)}) collective-permute-start(bf16[2,48,1024]{2,1,0:T(8,128)(2,1)S(1)} %pad_maximum_fusion.refs_0_), channel_id=1, source_target_pairs={{0,64},{16,80},{32,96},{48,112},{64,0},{80,16},{96,32},{112,48},{1... | collective-permute-start | bytes 589832 | tf_op jit(solution)/shard_map/ppermute | solution.py:452
  66.2 15.3 %collective-permute-start.9 = (bf16[2,48,1024]{2,1,0:T(8,128)(2,1)S(1)}, bf16[2,48,1024]{2,1,0:T(8,128)(2,1)S(1)}, u32[]{:S(2)}, u32[]{:S(2)}) collective-permute-start(bf16[2,48,1024]{2,1,0:T(8,128)(2,1)S(1)} %pad_maximum_fusion.refs_0_), channel_id=1, source_target_pairs={{0,32},{16,48},{32,64},{48,80},{64,96},{80,112},{96,0},{112,16},{1... | collective-permute-start | bytes 589832 | tf_op jit(solution)/shard_map/ppermute | solution.py:452
  95.7 4.5 %collective-permute-start.12 = (bf16[8,8,40,128]{3,2,1,0:T(8,128)(2,1)S(1)}, bf16[8,8,40,128]{3,2,1,0:T(8,128)(2,1)S(1)}, u32[]{:S(2)}, u32[]{:S(2)}) collective-permute-start(bf16[8,8,40,128]{3,2,1,0:T(8,128)(2,1)S(1)} %all_to_all.25.own_ref), channel_id=1, source_target_pairs={{0,1},{1,0},{2,3},{3,2},{4,5},{5,4},{6,7},{7,6},{8,9},{9,8},{10,11... | collective-permute-start | bytes 1966088 | tf_op jit(solution)/shard_map/ppermute | solution.py:43
  125.3 2.4 %collective-permute-start.13 = (bf16[8,8,48,128]{3,2,1,0:T(8,128)(2,1)S(1)}, bf16[8,8,48,128]{3,2,1,0:T(8,128)(2,1)S(1)}, u32[]{:S(2)}, u32[]{:S(2)}) collective-permute-start(bf16[8,8,48,128]{3,2,1,0:T(8,128)(2,1)S(1)} %get-tuple-element.44), channel_id=1, source_target_pairs={{0,1},{1,0},{2,3},{3,2},{4,5},{5,4},{6,7},{7,6},{8,9},{9,8},{10,11... | collective-permute-start | bytes 2359304 | tf_op jit(solution)/shard_map/ppermute | solution.py:43
  127.9 39.7 %copy-start = (bf16[3,640,512]{2,1,0:T(8,128)(2,1)S(1)}, bf16[3,640,512]{2,1,0:T(8,128)(2,1)}, u32[]{:S(2)}) copy-start(bf16[3,640,512]{2,1,0:T(8,128)(2,1)} %get-tuple-element.51.rows_ref) | copy-start | bytes 5898244
  149.9 13.3 %all-to-all-start.4 = ((bf16[8,8,40,128]{3,2,1,0:T(8,128)(2,1)}), bf16[8,8,40,128]{3,2,1,0:T(8,128)(2,1)S(1)}, u32[]{:S(2)}, u32[]{:S(2)}) async-start(bf16[8,8,40,128]{3,2,1,0:T(8,128)(2,1)} %get-tuple-element.45), calls=%async_computation.4 | async-start | bytes 1310720 | tf_op jit(solution)/shard_map/all_to_all | solution.py:487
  163.2 4.3 %collective-permute-start.14 = (bf16[8,8,40,128]{3,2,1,0:T(8,128)(2,1)S(1)}, bf16[8,8,40,128]{3,2,1,0:T(8,128)(2,1)S(1)}, u32[]{:S(2)}, u32[]{:S(2)}) collective-permute-start(bf16[8,8,40,128]{3,2,1,0:T(8,128)(2,1)S(1)} %all-to-all-done.4.own_ref), channel_id=1, source_target_pairs={{0,1},{1,0},{2,3},{3,2},{4,5},{5,4},{6,7},{7,6},{8,9},{9,8},{10,11... | collective-permute-start | bytes 1966088 | tf_op jit(solution)/shard_map/ppermute | solution.py:43
  (3 other events, 2.2 us)

commit v4 on v3

v4 whole, which is shorter than its diff:
```python
import functools

import jax
import jax.numpy as jnp
from jax import lax
from jax.experimental import pallas as pl
from jax.experimental.pallas import tpu as pltpu
from jax.sharding import Mesh, PartitionSpec as P

NORM_EPS = 1e-05
GROUP = ("x", "yh")
RING = ("z", "yl")
CHIPS = ("x", "yh", "z", "yl")
ALL = CHIPS + ("c",)
PLACES = [(0, 0), (0, 1), (3, 0), (1, 0), (2, 0), (3, 1), (1, 1), (2, 1)]
GROUPS = 8
HALF = 128
ROWS = 80
SPARE = HALF - ROWS
PIECE = ROWS // 2
MIB = 1 << 20
f32, bf16 = jnp.float32, jnp.bfloat16
SCALARS = pl.BlockSpec(memory_space=pltpu.SMEM)
VECTORS = pl.BlockSpec(memory_space=pltpu.VMEM)
FAR = pl.BlockSpec(memory_space=pltpu.HBM)


def group_at(dx, dy):
    return lax.rem(lax.axis_index("x") + dx, 4) * 2 + lax.rem(lax.axis_index("yh") + dy, 2)


def have_here(length):
    return jnp.clip(length - lax.axis_index("yh") * HALF, 0, HALF)


def spread(value, axes, count):
    return lax.all_to_all(
        jnp.broadcast_to(value[None], (count,) + value.shape), axes, 0, 0, tiled=True
    )


def swap(value, axis, bit, count):
    return lax.ppermute(value, axis, [(i, i ^ bit) for i in range(count)])


def spare_kernel(length_ref, mask_ref, target_ref, spare_ref):
    vocab = target_ref.shape[1]
    masked = (mask_ref[...] == 1).astype(f32)
    near = lax.broadcasted_iota(jnp.int32, (1, HALF), 1) < have_here(length_ref[0])
    count = jnp.sum(jnp.where(near, masked, 0.0), axis=1, keepdims=True)
    place = lax.broadcasted_iota(jnp.int32, (HALF, vocab), 0) - ROWS
    column = lax.broadcasted_iota(jnp.int32, (HALF, vocab), 1)
    tiled = jnp.zeros((HALF, vocab), f32)
    for k in range(GROUPS):
        tiled = jnp.where((column - SPARE * k == place) & (place >= 0), 1.0, tiled)
    repeated = jnp.dot(
        jnp.broadcast_to(masked, (8, HALF)).astype(bf16),
        tiled.astype(bf16),
        preferred_element_type=f32,
    )[0:1]
    row = lax.broadcasted_iota(jnp.int32, (16, vocab), 0)
    facts = jnp.where(row == 0, repeated, jnp.where(row == 1, count, 0.0))
    spare_ref[0:SPARE, :] = target_ref[ROWS:HALF, :]
    spare_ref[SPARE : SPARE + 16, :] = facts.astype(bf16)


def spare_facts(lengths, loss_mask, target):
    return pl.pallas_call(
        spare_kernel,
        in_specs=[SCALARS, VECTORS, VECTORS],
        out_specs=VECTORS,
        out_shape=jax.ShapeDtypeStruct((SPARE + 16, target.shape[1]), bf16),
        compiler_params=pltpu.CompilerParams(vmem_limit_bytes=8 * MIB),
        name="spare_facts",
    )(lengths, loss_mask, target)


def stage_kernel(hbm_weight, hbm_cap, weight_ref, cap_ref, sems):
    copies = [
        pltpu.make_async_copy(hbm_weight, weight_ref, sems.at[0]),
        pltpu.make_async_copy(hbm_cap, cap_ref, sems.at[1]),
    ]
    for copy in copies:
        copy.start()
    for copy in copies:
        copy.wait()


def stage(weight, captured):
    return pl.pallas_call(
        stage_kernel,
        in_specs=[FAR, FAR],
        out_specs=[VECTORS] * 2,
        out_shape=(
            jax.ShapeDtypeStruct(weight.shape, bf16),
            jax.ShapeDtypeStruct(captured.shape, bf16),
        ),
        scratch_shapes=[pltpu.SemaphoreType.DMA((2,))],
        compiler_params=pltpu.CompilerParams(vmem_limit_bytes=8 * MIB),
        name="stage",
    )(weight, captured)


def split_by_core(block, first, mine_ref, other_ref, extra=None):
    for j in range(8):
        upper = block[0:PIECE, j * 128 : (j + 1) * 128]
        lower = block[PIECE:ROWS, j * 128 : (j + 1) * 128]
        mine = jnp.where(first, upper, lower)
        other = jnp.where(first, lower, upper)
        if extra is not None:
            mine = jnp.concatenate([mine, extra], axis=0)
            other = jnp.concatenate([other, jnp.zeros_like(extra)], axis=0)
        mine_ref[j] = mine.astype(bf16)
        other_ref[j] = other.astype(bf16)


def unite_kernel(*refs):
    blocks, length_refs = refs[:GROUPS], refs[GROUPS : GROUPS + 4]
    weight_ref, rows_ref, mine_ref, other_ref, slot_ref = refs[GROUPS + 4 :]
    first = lax.axis_index("c") == 0
    groups = [group_at(*place) for place in PLACES]
    lane = lax.broadcasted_iota(jnp.int32, (1, 512), 1).astype(f32)
    have = [
        jnp.clip(
            jnp.broadcast_to(length_refs[-dx % 4][0:1, 0:1], (1, 512))
            - lax.rem(lax.axis_index("yh") + dy, 2).astype(f32) * HALF,
            0.0,
            float(HALF),
        )
        for dx, dy in PLACES
    ]
    more = [jnp.maximum(h - ROWS, 0.0) for h in have]
    less = [jnp.maximum(ROWS - h, 0.0) for h in have]

    def before(amounts, k):
        total = jnp.zeros((1, 512), f32)
        for m in range(GROUPS):
            if m != k:
                total = total + amounts[m] * (groups[m] < groups[k]).astype(f32)
        return total

    order = jnp.full((1, 512), -1.0, f32)
    for k in range(GROUPS):
        place = lane - SPARE * k
        mine = (place >= 0) & (place < SPARE)
        order = jnp.where(mine & (place < have[k] - ROWS), before(more, k) + place, order)
    slot = jnp.full((1, 512), -1.0, f32)
    for k in range(GROUPS):
        offset = order - before(less, k)
        mine = (order >= 0) & (offset >= 0) & (offset < ROWS - have[k])
        slot = jnp.where(mine, ROWS * k + have[k] + offset, slot)
    slot_ref[...] = jnp.broadcast_to(slot, (8, 512))
    for half in range(2):
        row = lax.broadcasted_iota(jnp.int32, (4 * ROWS, 384), 0) + half * 4 * ROWS
        pick = (row.astype(f32) == slot[:, :384]).astype(bf16)
        total = None
        for s in range(3):
            pool = jnp.concatenate([block[s, ROWS:HALF, :] for block in blocks], axis=0)
            moved = jnp.dot(pick, pool, preferred_element_type=f32)
            kept = []
            for k in range(4 * half, 4 * half + 4):
                own = blocks[k][s, 0:ROWS, :].astype(f32)
                within = lax.broadcasted_iota(jnp.int32, (ROWS, 512), 0).astype(f32) < have[k]
                base = (k - 4 * half) * ROWS
                kept.append(jnp.where(within, own, moved[base : base + ROWS]))
            rows = jnp.concatenate(kept, axis=0).astype(bf16)
            rows_ref[s, pl.ds(half * 4 * ROWS, 4 * ROWS), :] = rows
            term = jnp.dot(rows, weight_ref[s], preferred_element_type=f32)
            total = term if total is None else total + term
        for k in range(4):
            group = groups[4 * half + k]
            split_by_core(
                total[k * ROWS : (k + 1) * ROWS], first, mine_ref.at[group], other_ref.at[group]
            )


def unite(blocks, lengths, weight):
    return pl.pallas_call(
        unite_kernel,
        in_specs=[VECTORS] * (GROUPS + 5),
        out_specs=[VECTORS] * 4,
        out_shape=(
            jax.ShapeDtypeStruct((3, GROUPS * ROWS, 512), bf16),
            jax.ShapeDtypeStruct((GROUPS, 8, PIECE, 128), bf16),
            jax.ShapeDtypeStruct((GROUPS, 8, PIECE, 128), bf16),
            jax.ShapeDtypeStruct((8, 512), f32),
        ),
        compiler_params=pltpu.CompilerParams(vmem_limit_bytes=24 * MIB),
        name="unite",
    )(*blocks, *lengths, weight)


def head_kernel(
    own_ref, other_ref, gain_ref, head_ref,
    logit_ref, scale_ref, united_ref, held, wide, normed, sems,
):
    width = wide.shape[1]
    tile = head_ref.shape[0] // 8
    loads = [
        pltpu.make_async_copy(
            head_ref.at[pl.ds(i * tile, tile)], held.at[pl.ds(i * tile, tile)], sems.at[i]
        )
        for i in range(8)
    ]
    for copy in loads[:3]:
        copy.start()

    first = lax.axis_index("c") == 0
    wide[ROWS:HALF, :] = jnp.zeros((HALF - ROWS, width), f32)
    for g in range(GROUPS):
        for j in range(8):
            column = (g * 8 + j) * 128
            a = own_ref[j, g].astype(f32)
            b = other_ref[j, g].astype(f32)
            wide[0:PIECE, column : column + 128] = jnp.where(first, a, b)
            wide[PIECE:ROWS, column : column + 128] = jnp.where(first, b, a)
    square = jnp.zeros((HALF, 1), f32)
    for g in range(GROUPS):
        values = wide[:, g * 1024 : (g + 1) * 1024]
        square = square + jnp.sum(values * values, axis=1, keepdims=True)
    scale = lax.rsqrt(square / width + NORM_EPS)
    for g in range(GROUPS):
        part = slice(g * 1024, (g + 1) * 1024)
        values = wide[:, part]
        united_ref[:, part] = values[0:ROWS].astype(bf16)
        normed[part, :] = jnp.transpose(values * scale * gain_ref[:, part]).astype(bf16)

    scale_ref[...] = jnp.transpose(jnp.broadcast_to(scale, (HALF, HALF)))[0:8]
    for i in range(0, 8, 2):
        for k in (i, i + 1):
            loads[k].wait()
            if k + 3 < 8:
                loads[k + 3].start()
        part = slice(i * tile, (i + 2) * tile)
        logit_ref[part, :] = jnp.dot(held[part, :], normed[...], preferred_element_type=f32)


def head_forward(own, other, gain, head):
    vocab, width = head.shape
    return pl.pallas_call(
        head_kernel,
        in_specs=[VECTORS] * 3 + [FAR],
        out_specs=[VECTORS] * 4,
        out_shape=(
            jax.ShapeDtypeStruct((vocab, HALF), f32),
            jax.ShapeDtypeStruct((8, HALF), f32),
            jax.ShapeDtypeStruct((ROWS, width), bf16),
            jax.ShapeDtypeStruct((vocab, width), bf16),
        ),
        scratch_shapes=[
            pltpu.VMEM((HALF, width), f32),
            pltpu.VMEM((width, HALF), bf16),
            pltpu.SemaphoreType.DMA((8,)),
        ],
        compiler_params=pltpu.CompilerParams(vmem_limit_bytes=24 * MIB),
        cost_estimate=pl.CostEstimate(
            flops=4 * HALF * vocab * width, bytes_accessed=2 * vocab * width, transcendentals=0
        ),
        name="head_forward",
    )(own, other, gain, head)


def stat_kernel(
    length_ref, logit_ref, scale_ref, target_ref, mask_ref, slot_ref, *refs
):
    spares = refs[:4]
    chosen_ref, stat_ref, side_ref, pool, pool_sems = refs[4:]
    moves = [
        pltpu.make_async_copy(spares[-dx % 4].at[dy], pool.at[k], pool_sems.at[k])
        for k, (dx, dy) in enumerate(PLACES)
    ]
    for copy in moves:
        copy.start()
    for copy in moves:
        copy.wait()
    have = have_here(length_ref[0])
    row = lax.broadcasted_iota(jnp.int32, (HALF, 384), 0)
    pick = (row.astype(f32) == slot_ref[0:1, 0:384]).astype(bf16)
    spare = pool[:, 0:SPARE, :].reshape(384, pool.shape[2])
    moved = jnp.dot(pick, spare, preferred_element_type=f32)
    kept = lax.broadcasted_iota(jnp.int32, moved.shape, 0) < have
    chosen = jnp.transpose(jnp.where(kept, target_ref[...].astype(f32), moved))
    chosen_ref[...] = chosen
    column = lax.broadcasted_iota(jnp.int32, (1, 384), 1)
    mask_pool = seq_pool = jnp.zeros((1, 384), f32)
    counts = []
    for k, place in enumerate(PLACES):
        mine = (column >= SPARE * k) & (column < SPARE * (k + 1))
        facts = pool[k, SPARE : SPARE + 16, :].astype(f32)
        mask_pool = jnp.where(mine, facts[0:1, 0:384], mask_pool)
        seq_pool = jnp.where(mine, (group_at(*place) // 2).astype(f32), seq_pool)
        counts.append(facts[1:2, 0:HALF])
    none = jnp.zeros((6, 384), f32)
    traits = lax.dot_general(
        jnp.concatenate([mask_pool, seq_pool, none], axis=0).astype(bf16), pick, (((1,), (1,)), ((), ())), preferred_element_type=f32
    )
    lane = lax.broadcasted_iota(jnp.int32, (1, HALF), 1)
    masked = (mask_ref[...] == 1).astype(f32)
    valid = jnp.where(lane < have, masked, traits[0:1])
    valid = jnp.where(lane < ROWS, valid, 0.0)
    sequence = jnp.where(lane < have, lax.axis_index("x").astype(f32), traits[1:2])
    nothing = jnp.zeros((1, HALF), f32)
    side_ref[...] = jnp.concatenate(
        [scale_ref[0:1], valid, sequence, sum(counts), counts[0] + counts[1]] + [nothing] * 3, axis=0
    )

    top_t = jnp.max(chosen, axis=0, keepdims=True)
    pow_t = jnp.exp(chosen - top_t)
    sum_t = jnp.sum(pow_t, axis=0, keepdims=True)
    dot_t = jnp.sum(pow_t * chosen, axis=0, keepdims=True)
    logits = logit_ref[...]
    top_d = jnp.max(logits, axis=0, keepdims=True)
    pow_d = jnp.exp(logits - top_d)
    stat_ref[...] = jnp.concatenate(
        [
            top_t,
            sum_t,
            dot_t,
            jnp.sum(pow_t * logits, axis=0, keepdims=True),
            top_d,
            jnp.sum(pow_d, axis=0, keepdims=True),
            jnp.sum(pow_d * logits, axis=0, keepdims=True),
            nothing,
        ],
        axis=0,
    )


def row_stats(lengths, logits, scales, target, loss_mask, slots, spares):
    vocab = logits.shape[0]
    return pl.pallas_call(
        stat_kernel,
        in_specs=[SCALARS] + [VECTORS] * 5 + [FAR] * 4,
        out_specs=[VECTORS] * 3,
        out_shape=(
            jax.ShapeDtypeStruct((vocab, HALF), f32),
            jax.ShapeDtypeStruct((8, HALF), f32),
            jax.ShapeDtypeStruct((8, HALF), f32),
        ),
        scratch_shapes=[
            pltpu.VMEM((GROUPS, SPARE + 16, vocab), bf16),
            pltpu.SemaphoreType.DMA((GROUPS,)),
        ],
        compiler_params=pltpu.CompilerParams(vmem_limit_bytes=16 * MIB),
        name="row_stats",
    )(lengths, logits, scales, target, loss_mask, slots, *spares)


def back_kernel(
    every_ref, logit_ref, chosen_ref, side_ref, gain_ref, united_ref, head_ref,
    mine_ref, other_ref,
):
    width = gain_ref.shape[1]
    every = every_ref[...]
    max_t = jnp.max(every[:, 0:1], axis=0)
    scale_t = jnp.exp(every[:, 0:1] - max_t[None])
    sum_t = jnp.sum(every[:, 1:2] * scale_t, axis=0)
    mean_tt = jnp.sum(every[:, 2:3] * scale_t, axis=0) / sum_t
    mean_tl = jnp.sum(every[:, 3:4] * scale_t, axis=0) / sum_t
    max_d = jnp.max(every[:, 4:5], axis=0)
    scale_d = jnp.exp(every[:, 4:5] - max_d[None])
    sum_d = jnp.sum(every[:, 5:6] * scale_d, axis=0)
    mean_dl = jnp.sum(every[:, 6:7] * scale_d, axis=0) / sum_d
    log_t = max_t + jnp.log(sum_t)
    log_d = max_d + jnp.log(sum_d)
    row_scale, valid, sequence = side_ref[0:1], side_ref[1:2], side_ref[2:3]
    kl = (mean_tt - mean_tl - log_t + log_d) * valid
    row = lax.broadcasted_iota(jnp.int32, (8, HALF), 0)
    sums = jnp.sum(jnp.where(row.astype(f32) == sequence, kl, 0.0), axis=1, keepdims=True)
    sums = jnp.broadcast_to(sums, (8, HALF))
    high = sums.astype(bf16).astype(f32)
    middle = (sums - high).astype(bf16).astype(f32)
    column = lax.broadcasted_iota(jnp.int32, (8, HALF), 1)
    third = jnp.where(column < 96, sums - high - middle, 0.0)
    sums = jnp.where(column < 32, high, jnp.where(column < 64, middle, third))

    weight = valid * row_scale
    grad = weight * (jnp.exp(logit_ref[...] - log_d) - jnp.exp(chosen_ref[...] - log_t))
    grad = jnp.transpose(grad)[0:ROWS].astype(bf16)
    lane = lax.broadcasted_iota(jnp.int32, (1, HALF), 1)
    share = ROWS // 16
    index = lax.axis_index(("z", "yl", "c"))
    mine = (lane >= index * share) & (lane < (index + 1) * share)
    cubic = jnp.where(mine, weight * row_scale * (mean_dl - mean_tl) / width, 0.0)
    cubic = jnp.transpose(jnp.broadcast_to(cubic, (HALF, HALF)))[0:ROWS, 0:1]
    for g in range(GROUPS):
        part = slice(g * 1024, (g + 1) * 1024)
        block = jnp.dot(grad, head_ref[:, part], preferred_element_type=f32)
        block = block * gain_ref[:, part] - cubic * united_ref[:, part].astype(f32)
        split_by_core(
            block, lax.axis_index("c") == 0, mine_ref.at[g], other_ref.at[g], sums
        )


def head_backward(every, logits, chosen, side, gain, united, head):
    return pl.pallas_call(
        back_kernel,
        in_specs=[VECTORS] * 7,
        out_specs=[VECTORS] * 2,
        out_shape=(
            jax.ShapeDtypeStruct((GROUPS, 8, PIECE + 8, 128), bf16),
            jax.ShapeDtypeStruct((GROUPS, 8, PIECE + 8, 128), bf16),
        ),
        compiler_params=pltpu.CompilerParams(vmem_limit_bytes=24 * MIB),
        name="head_backward",
    )(every, logits, chosen, side, gain, united, head)


def grad_kernel(side_ref, own_ref, other_ref, rows_ref, out_ref, wide, grads):
    @pl.when((pl.program_id(0) == 0) & (pl.program_id(1) == 0))
    def _():
        first = lax.axis_index("c") == 0
        for k, place in enumerate(PLACES):
            group = group_at(*place)
            for j in range(8):
                a = own_ref[j, group].astype(f32)
                b = other_ref[j, group].astype(f32)
                base = k * ROWS
                wide[base : base + PIECE, j * 128 : (j + 1) * 128] = jnp.where(first, a, b)
                wide[base + PIECE : base + ROWS, j * 128 : (j + 1) * 128] = jnp.where(first, b, a)
        grads[...] = wide[...].astype(bf16)

    factor = (2 * HALF) / jnp.maximum(side_ref[3:4, 0:1], 1.0)
    out_ref[0] = factor * lax.dot_general(
        rows_ref[0], grads[...], (((0,), (0,)), ((), ())), preferred_element_type=f32
    )


def weight_gradient(side, own, other, rows):
    total = GROUPS * ROWS
    whole = lambda shape: pl.BlockSpec(shape, lambda s, i: (0,) * len(shape))
    return pl.pallas_call(
        grad_kernel,
        grid=(3, 2),
        in_specs=[
            whole((8, HALF)),
            whole((8, GROUPS, PIECE, 128)),
            whole((8, GROUPS, PIECE, 128)),
            pl.BlockSpec((1, total, 256), lambda s, i: (s, 0, i)),
        ],
        out_specs=pl.BlockSpec((1, 256, 1024), lambda s, i: (s, i, 0)),
        out_shape=jax.ShapeDtypeStruct((3, 512, 1024), f32),
        scratch_shapes=[pltpu.VMEM((total, 1024), f32), pltpu.VMEM((total, 1024), bf16)],
        compiler_params=pltpu.CompilerParams(vmem_limit_bytes=40 * MIB),
        name="weight_gradient",
    )(side, own, other, rows)


def sum_kernel(piece_ref, out_ref, extra_ref):
    extra = jnp.zeros((8, 128), f32)
    for g in range(GROUPS):
        total = jnp.zeros((PIECE, 128), f32)
        for j in range(8):
            total = total + piece_ref[g * 8 + j, 0:PIECE, :].astype(f32)
        for k in range(8):
            out_ref[k, g] = total.astype(bf16)
        if piece_ref.shape[1] > PIECE:
            extra = extra + piece_ref[g * 8].astype(f32)[PIECE : PIECE + 8]
    extra_ref[...] = extra


def gather_sum(mine, other):
    pair = (mine.astype(f32) + swap(other, "c", 1, 2).astype(f32)).astype(bf16)
    received = lax.all_to_all(pair.reshape((64,) + pair.shape[2:]), CHIPS, 0, 0, tiled=True)
    copies, extra = pl.pallas_call(
        sum_kernel,
        in_specs=[VECTORS],
        out_specs=[VECTORS] * 2,
        out_shape=(
            jax.ShapeDtypeStruct((8, GROUPS, PIECE, 128), bf16),
            jax.ShapeDtypeStruct((8, 128), f32),
        ),
        compiler_params=pltpu.CompilerParams(vmem_limit_bytes=8 * MIB),
        name="sum_pieces",
    )(received)
    return copies, extra


def route(value, dx, dy):
    pairs = [(p * 2 + q, (p + dx) % 4 * 2 + (q ^ dy)) for p in range(4) for q in range(2)]
    return lax.ppermute(value, GROUP, pairs)


def local(captured, target_logits, unite_weight, norm_gain, head_weight, lengths, loss_mask):
    width = norm_gain.shape[0]
    own = captured.reshape(3, HALF, 512)
    target = target_logits.reshape(HALF, -1)
    far = route(own, 2, 0)
    over = route(own, 0, 1)
    right = route(own, 3, 0)
    left = route(own, 1, 0)
    far, near_target, later = lax.optimization_barrier((far, target, lengths))
    over_far = route(far, 0, 1)
    over_right = route(over, 3, 0)
    over_left = route(over, 1, 0)
    spare = spare_facts(lengths, loss_mask, near_target)
    pair = jnp.stack([spare, route(spare, 0, 1)])
    left, right, weight = lax.optimization_barrier((left, right, unite_weight))
    weight, near = stage(weight, own)
    wide_length = jnp.broadcast_to(later.astype(f32), (8, HALF))
    all_lengths = [wide_length] + [route(wide_length, dx, 0) for dx in range(1, 4)]
    over_far, pair = lax.optimization_barrier((over_far, pair))
    blocks = [near, over, left, right, far, over_left, over_right, over_far]
    rows, mine, other, slots = unite(blocks, all_lengths, weight)

    copies, _ = gather_sum(mine, other)
    copies, pair = lax.optimization_barrier((copies, pair))
    spares = [pair] + [route(pair, dx, 0) for dx in range(1, 4)]
    own_united = lax.all_to_all(copies, RING, 0, 0, tiled=True)
    own_united, spares[1], spares[3] = lax.optimization_barrier(
        (own_united, spares[1], spares[3])
    )
    other_united = swap(own_united, "c", 1, 2)
    gain = norm_gain.reshape(1, width)
    logits, scales, united, held = head_forward(own_united, other_united, gain, head_weight)
    chosen, stats, side = row_stats(
        lengths, logits, scales, target, loss_mask, slots, spares
    )
    every = spread(stats, ("z", "yl", "c"), 16)
    mine, other = head_backward(every, logits, chosen, side, gain, united, held)
    copies, sums = gather_sum(mine, other)
    own_grad = lax.all_to_all(copies, RING, 0, 0, tiled=True)
    seq_sum = jnp.sum(
        jnp.where(lax.iota(jnp.int32, GROUPS)[:, None] == lax.axis_index("x"), sums, 0.0)
    )
    seq_kl = (seq_sum / 32.0 / jnp.maximum(side[4, 0], 1.0)).reshape(1)
    own_grad, seq_kl = lax.optimization_barrier((own_grad, seq_kl))
    other_grad = swap(own_grad, "c", 1, 2)
    unite_grad = weight_gradient(side, own_grad, other_grad, rows)
    return (seq_kl, unite_grad)


def solution(mesh):
    fine = Mesh(mesh.devices.reshape(4, 2, 4, 2, 2), ALL)
    tensor = ("z", "yl", "c")
    placed = (
        P(None, "x", "yh", tensor),
        P("x", "yh", tensor),
        P(None, tensor, GROUP),
        P(),
        P(tensor, None),
        P("x"),
        P("x", "yh"),
    )
    return jax.shard_map(
        local,
        mesh=fine,
        in_specs=placed,
        out_specs=(P("x"), P(None, tensor, GROUP)),
        check_vma=False,
    )
```

time: 175 us -> 157 us (0.90)
  waiting for transfers between devices: 44.7 us -> 27.9 us
  blocking collectives: 43.9 us -> 52.9 us
  Pallas kernels: 31.5 us -> 25.7 us
  other arithmetic: 4.27 us -> 1.08 us
  starting transfers between devices: 42.3 us -> 40.3 us
  local copies, waits for them, and re-layouts: 3.17 us -> 5.02 us
    all_to_all x1 -> x2, blocking collectives: 21 us -> 44 us  [gather_sum(): lax.all_to_all(pair.reshape((64,) + pair.shape[2:]), CHIPS, 0, 0, tiled=T...]
    all_to_all x1 -> x0, blocking collectives: 14.2 us -> none  [local(): own_united = lax.all_to_all(copies, RING, 0, 0, tiled=True)]
    ppermute x11 -> x14, waiting for transfers between devices: 23.8 us -> 11.4 us  [route(): return lax.ppermute(value, GROUP, pairs)]
    all_to_all x1, waiting for transfers between devices: 9.73 us -> 2.37 us  [local(): own_united = lax.all_to_all(copies, RING, 0, 0, tiled=True)]
    all_to_all x1, starting transfers between devices: 10.9 us -> 3.54 us  [local(): own_united = lax.all_to_all(copies, RING, 0, 0, tiled=True)]
    pallas_call x5 -> x7, Pallas kernels: 29.9 us -> 23.9 us  [the longest x1 8.21 us: head_forward(): pl.pallas_call(head_kernel, in_specs=[VECTORS] * 3 + [FAR], out_specs=[VE...]
    ppermute x11 -> x14, starting transfers between devices: 20.4 us -> 24 us  [route(): return lax.ppermute(value, GROUP, pairs)]
    convert_element_type x2, other arithmetic: 2.32 us -> 0.38 us  [gather_sum(): pair = (mine.astype(f32) + swap(other, 'c', 1, 2).astype(f32)).astype(bf16)]
  transfers between devices with their start and end apart: 17 -> 20, of which waited for: 12 -> 11; matrix products, arithmetic and copies ran while one was open for 1% -> 1% of each run, Pallas kernels for 0% -> 6%
where the time goes in v4:
time: 157 us
  blocking collectives  52.9 us (34%)
  starting transfers between devices  40.3 us (26%)
  waiting for transfers between devices  27.9 us (18%)
  Pallas kernels  25.7 us (16%)
  local copies, waits for them, and re-layouts  5.02 us (3%)
  between operations  3.94 us (3%)
    all_to_all x2, blocking collectives, gather_sum(): lax.all_to_all(pair.reshape((64,) + pair.shape[2:]), CHIPS, 0, 0, tiled=T...  44 us
    ppermute x14, starting transfers between devices, route(): return lax.ppermute(value, GROUP, pairs)  24 us
    ppermute x14, waiting for transfers between devices, route(): return lax.ppermute(value, GROUP, pairs)  11.4 us
    ppermute x4, starting transfers between devices, swap(): return lax.ppermute(value, axis, [(i, i ^ bit) for i in range(count)])  9.12 us
    all_to_all x1, blocking collectives, spread(): lax.all_to_all(jnp.broadcast_to(value[None], (count,) + value.shape), axe...  8.91 us
    pallas_call x1, Pallas kernels, head_forward(): pl.pallas_call(head_kernel, in_specs=[VECTORS] * 3 + [FAR], out_specs=[VE...  8.21 us
    all_to_all x1, waiting for transfers between devices, local(): own_grad = lax.all_to_all(copies, RING, 0, 0, tiled=True)  7.25 us
    ppermute x4, waiting for transfers between devices, swap(): return lax.ppermute(value, axis, [(i, i ^ bit) for i in range(count)])  6.86 us
  transfers between devices with their start and end apart: 20, of which 11 were waited for; matrix products, arithmetic and copies ran while one was open for 1% of the time, Pallas kernels for 6%

profile of v4, /device:TPU:1, one launch (start us, length us, event | category | flops | bytes accessed | tf_op | source)
XLA Modules:
  0.0 156.8 jit_solution(10989642198397771030)
XLA Ops:
  0.6 3.7 %collective-permute-start.3 = (bf16[3,128,512]{2,1,0:T(8,128)(2,1)}, bf16[3,128,512]{2,1,0:T(8,128)(2,1)S(1)}, u32[]{:S(2)}, u32[]{:S(2)}) collective-permute-start(bf16[3,128,512]{2,1,0:T(8,128)(2,1)} %bitcast.13), channel_id=1, source_target_pairs={{0,64},{16,80},{32,96},{48,112},{64,0},{80,16},{96,32},{112,48},{1... | collective-permute-start | bytes 1179656 | tf_op jit(solution)/shard_map/ppermute | solution.py:481
  4.3 2.9 %collective-permute-start.2 = (bf16[3,128,512]{2,1,0:T(8,128)(2,1)}, bf16[3,128,512]{2,1,0:T(8,128)(2,1)S(1)}, u32[]{:S(2)}, u32[]{:S(2)}) collective-permute-start(bf16[3,128,512]{2,1,0:T(8,128)(2,1)} %bitcast.14), channel_id=1, source_target_pairs={{0,16},{16,0},{32,48},{48,32},{64,80},{80,64},{96,112},{112,96},{1... | collective-permute-start | bytes 1179656 | tf_op jit(solution)/shard_map/ppermute | solution.py:481
  7.5 2.4 %collective-permute-start.1 = (bf16[3,128,512]{2,1,0:T(8,128)(2,1)}, bf16[3,128,512]{2,1,0:T(8,128)(2,1)S(1)}, u32[]{:S(2)}, u32[]{:S(2)}) collective-permute-start(bf16[3,128,512]{2,1,0:T(8,128)(2,1)} %bitcast.16), channel_id=1, source_target_pairs={{0,96},{16,112},{32,0},{48,16},{64,32},{80,48},{96,64},{112,80},{1... | collective-permute-start | bytes 1179656 | tf_op jit(solution)/shard_map/ppermute | solution.py:481
  9.9 3.0 %collective-permute-done.3.refs_4_ = bf16[3,128,512]{2,1,0:T(8,128)(2,1)S(1)} collective-permute-done((bf16[3,128,512]{2,1,0:T(8,128)(2,1)}, bf16[3,128,512]{2,1,0:T(8,128)(2,1)S(1)}, u32[]{:S(2)}, u32[]{:S(2)}) %collective-permute-start.3) | collective-permute-done | bytes 393248 | tf_op jit(solution)/shard_map/ppermute | solution.py:481
  12.9 3.3 %collective-permute-start.6 = (bf16[3,128,512]{2,1,0:T(8,128)(2,1)S(1)}, bf16[3,128,512]{2,1,0:T(8,128)(2,1)S(1)}, u32[]{:S(2)}, u32[]{:S(2)}) collective-permute-start(bf16[3,128,512]{2,1,0:T(8,128)(2,1)S(1)} %collective-permute-done.3.refs_4_), channel_id=1, source_target_pairs={{0,16},{16,0},{32,48},{48,32},{64,80},{80,64},{96,112},{112,96},{1... | collective-permute-start | bytes 1179656 | tf_op jit(solution)/shard_map/ppermute | solution.py:481
  22.5 3.1 %collective-permute-start.7 = (bf16[64,1024]{1,0:T(8,128)(2,1)S(1)}, bf16[64,1024]{1,0:T(8,128)(2,1)S(1)}, u32[]{:S(2)}, u32[]{:S(2)}) collective-permute-start(bf16[64,1024]{1,0:T(8,128)(2,1)S(1)} %spare_facts.1), channel_id=1, source_target_pairs={{0,16},{16,0},{32,48},{48,32},{64,80},{80,64},{96,112},{112,96},{1... | collective-permute-start | bytes 393224 | tf_op jit(solution)/shard_map/ppermute | solution.py:481
  34.5 3.7 %unite.1 = (bf16[3,640,512]{2,1,0:T(8,128)(2,1)S(1)}, bf16[8,8,40,128]{3,2,1,0:T(8,128)(2,1)S(1)}, bf16[8,8,40,128]{3,2,1,0:T(8,128)(2,1)S(1)}, f32[8,512]{1,0:T(8,128)S(1)}) custom-call(bf16[3,128,512]{2,1,0:T(8,128)(2,1)S(1)} %get-tuple-element.36.refs_0_, bf16[3,128,512]{2,1,0:T(8,128)(2,1)S(1)} %collective-permute-done.2.refs_1_, ...), custom_call_target="tpu_custom_call" | custom-call | tf_op jit(solution)/shard_map/unite/pallas_call | solution.py:178
  38.2 3.2 %collective-permute-start.11 = (bf16[8,8,40,128]{3,2,1,0:T(8,128)(2,1)S(1)}, bf16[8,8,40,128]{3,2,1,0:T(8,128)(2,1)S(1)}, u32[]{:S(2)}, u32[]{:S(2)}) collective-permute-start(bf16[8,8,40,128]{3,2,1,0:T(8,128)(2,1)S(1)} %get-tuple-element.45), channel_id=1, source_target_pairs={{0,1},{1,0},{2,3},{3,2},{4,5},{5,4},{6,7},{7,6},{8,9},{9,8},{10,11... | collective-permute-start | bytes 1966088 | tf_op jit(solution)/shard_map/ppermute | solution.py:43
  43.3 22.5 %all_to_all.25.piece_ref = bf16[64,40,128]{2,1,0:T(8,128)(2,1)S(1)} all-to-all(bf16[64,40,128]{2,1,0:T(8,128)(2,1)S(1)} %bitcast.21), channel_id=1, replica_groups=mesh['x'=4,'yh'=2,'z'=4,'yl'=2,'c'=2] {'x','yh','z','yl'}, dimensions={0} | all-to-all | bytes 1310720 | tf_op jit(solution)/shard_map/all_to_all | solution.py:464
  66.8 3.5 %all-to-all-start.1 = ((bf16[8,8,40,128]{3,2,1,0:T(8,128)(2,1)}), bf16[8,8,40,128]{3,2,1,0:T(8,128)(2,1)S(1)}, u32[]{:S(2)}, u32[]{:S(2)}) async-start(bf16[8,8,40,128]{3,2,1,0:T(8,128)(2,1)} %get-tuple-element.48), calls=%async_computation.1 | async-start | bytes 1310720 | tf_op jit(solution)/shard_map/all_to_all | solution.py:509
  70.8 2.3 %collective-permute-start.13 = (bf16[2,64,1024]{2,1,0:T(8,128)(2,1)S(1)}, bf16[2,64,1024]{2,1,0:T(8,128)(2,1)S(1)}, u32[]{:S(2)}, u32[]{:S(2)}) collective-permute-start(bf16[2,64,1024]{2,1,0:T(8,128)(2,1)S(1)} %pad_maximum_fusion.refs_0_), channel_id=1, source_target_pairs={{0,96},{16,112},{32,0},{48,16},{64,32},{80,48},{96,64},{112,80},{1... | collective-permute-start | bytes 786440 | tf_op jit(solution)/shard_map/ppermute | solution.py:481
  73.1 4.4 %collective-permute-done.12.refs_1_ = bf16[2,64,1024]{2,1,0:T(8,128)(2,1)S(1)} collective-permute-done((bf16[2,64,1024]{2,1,0:T(8,128)(2,1)S(1)}, bf16[2,64,1024]{2,1,0:T(8,128)(2,1)S(1)}, u32[]{:S(2)}, u32[]{:S(2)}) %collective-permute-start.12) | collective-permute-done | bytes 262176 | tf_op jit(solution)/shard_map/ppermute | solution.py:481
  77.5 2.4 %all-to-all-done.1.own_ref = bf16[8,8,40,128]{3,2,1,0:T(8,128)(2,1)S(1)} async-done(((bf16[8,8,40,128]{3,2,1,0:T(8,128)(2,1)}), bf16[8,8,40,128]{3,2,1,0:T(8,128)(2,1)S(1)}, u32[]{:S(2)}, u32[]{:S(2)}) %all-to-all-start.1) | async-done | bytes 655392 | tf_op jit(solution)/shard_map/all_to_all | solution.py:509
  79.8 2.9 %collective-permute-start.14 = (bf16[8,8,40,128]{3,2,1,0:T(8,128)(2,1)S(1)}, bf16[8,8,40,128]{3,2,1,0:T(8,128)(2,1)S(1)}, u32[]{:S(2)}, u32[]{:S(2)}) collective-permute-start(bf16[8,8,40,128]{3,2,1,0:T(8,128)(2,1)S(1)} %all-to-all-done.1.own_ref), channel_id=1, source_target_pairs={{0,1},{1,0},{2,3},{3,2},{4,5},{5,4},{6,7},{7,6},{8,9},{9,8},{10,11... | collective-permute-start | bytes 1966088 | tf_op jit(solution)/shard_map/ppermute | solution.py:43
  84.4 8.2 %head_forward.1 = (f32[1024,128]{1,0:T(8,128)S(1)}, f32[8,128]{1,0:T(8,128)S(1)}, bf16[80,8192]{1,0:T(8,128)(2,1)S(1)}, bf16[1024,8192]{1,0:T(8,128)(2,1)S(1)}) custom-call(bf16[8,8,40,128]{3,2,1,0:T(8,128)(2,1)S(1)} %all-to-all-done.1.own_ref, bf16[8,8,40,128]{3,2,1,0:T(8,128)(2,1)S(1)} %collective-permute-done.14.other_ref, f32[1,8192]{1,0:T(1,128)S(1)} %bitcast.18, ...), custom_call_target="tpu_custom_call" | custom-call | flops 4294967296 | bytes 16777216 | tf_op jit(solution)/shard_map/head_forward/pallas_call | solution.py:240
  92.7 2.2 %row_stats.1 = (f32[1024,128]{1,0:T(8,128)S(1)}, f32[8,128]{1,0:T(8,128)S(1)}, f32[8,128]{1,0:T(8,128)S(1)}) custom-call(s32[1]{0:T(128)S(6)} %copy.9.length_ref, f32[1024,128]{1,0:T(8,128)S(1)} %get-tuple-element.51.logit_ref, f32[8,128]{1,0:T(8,128)S(1)} %get-tuple-element.52.scale_ref, bf16[128,1024]{1,0:T(8,128)(2,1)S(1)} %bitcast.11, ...), custom_call_target="tpu_custom_call" | custom-call | tf_op jit(solution)/shard_map/row_stats/pallas_call | solution.py:331
  94.9 8.9 %all_to_all.26.every_ref = f32[16,8,128]{2,1,0:T(8,128)S(1)} all-to-all(f32[16,8,128]{2,1,0:T(8,128)S(1)} %broadcast_in_dim.25), channel_id=1, replica_groups=mesh['x'=4,'yh'=2,'z'=4,'yl'=2,'c'=2] {'z','yl','c'}, dimensions={0} | all-to-all | bytes 131072 | tf_op jit(solution)/shard_map/all_to_all | solution.py:37
  103.8 3.4 %head_backward.1 = (bf16[8,8,48,128]{3,2,1,0:T(8,128)(2,1)S(1)}, bf16[8,8,48,128]{3,2,1,0:T(8,128)(2,1)S(1)}) custom-call(f32[16,8,128]{2,1,0:T(8,128)S(1)} %all_to_all.26.every_ref, f32[1024,128]{1,0:T(8,128)S(1)} %get-tuple-element.51.logit_ref, f32[1024,128]{1,0:T(8,128)S(1)} %get-tuple-element.57.chosen_ref, f32[8,128]{1,0:T(8,128)S(1)} %get-tuple-element.58.side_ref, ...), custom_call_target="tpu_custom_call" | custom-call | tf_op jit(solution)/shard_map/head_backward/pallas_call | solution.py:396
  107.7 1.9 %collective-permute-done.16 = bf16[8,8,48,128]{3,2,1,0:T(8,128)(2,1)S(1)} collective-permute-done((bf16[8,8,48,128]{3,2,1,0:T(8,128)(2,1)S(1)}, bf16[8,8,48,128]{3,2,1,0:T(8,128)(2,1)S(1)}, u32[]{:S(2)}, u32[]{:S(2)}) %collective-permute-start.16) | collective-permute-done | bytes 786464 | tf_op jit(solution)/shard_map/ppermute | solution.py:43
  109.8 21.4 %all_to_all.27.piece_ref = bf16[64,48,128]{2,1,0:T(8,128)(2,1)S(1)} all-to-all(bf16[64,48,128]{2,1,0:T(8,128)(2,1)S(1)} %bitcast.20), channel_id=1, replica_groups=mesh['x'=4,'yh'=2,'z'=4,'yl'=2,'c'=2] {'x','yh','z','yl'}, dimensions={0} | all-to-all | bytes 1572864 | tf_op jit(solution)/shard_map/all_to_all | solution.py:464
  132.2 3.5 %all-to-all-start.4 = ((bf16[8,8,40,128]{3,2,1,0:T(8,128)(2,1)}), bf16[8,8,40,128]{3,2,1,0:T(8,128)(2,1)S(1)}, u32[]{:S(2)}, u32[]{:S(2)}) async-start(bf16[8,8,40,128]{3,2,1,0:T(8,128)(2,1)} %get-tuple-element.63), calls=%async_computation.4 | async-start | bytes 1310720 | tf_op jit(solution)/shard_map/all_to_all | solution.py:522
  138.3 7.3 %all-to-all-done.4.own_ref = bf16[8,8,40,128]{3,2,1,0:T(8,128)(2,1)S(1)} async-done(((bf16[8,8,40,128]{3,2,1,0:T(8,128)(2,1)}), bf16[8,8,40,128]{3,2,1,0:T(8,128)(2,1)S(1)}, u32[]{:S(2)}, u32[]{:S(2)}) %all-to-all-start.4) | async-done | bytes 655392 | tf_op jit(solution)/shard_map/all_to_all | solution.py:522
  145.5 2.6 %collective-permute-start.17 = (bf16[8,8,40,128]{3,2,1,0:T(8,128)(2,1)S(1)}, bf16[8,8,40,128]{3,2,1,0:T(8,128)(2,1)S(1)}, u32[]{:S(2)}, u32[]{:S(2)}) collective-permute-start(bf16[8,8,40,128]{3,2,1,0:T(8,128)(2,1)S(1)} %all-to-all-done.4.own_ref), channel_id=1, source_target_pairs={{0,1},{1,0},{2,3},{3,2},{4,5},{5,4},{6,7},{7,6},{8,9},{9,8},{10,11... | collective-permute-start | bytes 1966088 | tf_op jit(solution)/shard_map/ppermute | solution.py:43
  149.8 5.8 %weight_gradient.1 = f32[3,512,1024]{2,1,0:T(8,128)} custom-call(f32[8,128]{1,0:T(8,128)S(1)} %get-tuple-element.58.side_ref, bf16[8,8,40,128]{3,2,1,0:T(8,128)(2,1)S(1)} %all-to-all-done.4.own_ref, bf16[8,8,40,128]{3,2,1,0:T(8,128)(2,1)S(1)} %collective-permute-done.17.other_ref, bf16[3,640,512]{2,1,0:T(8,128)(2,1)S(1)} %get-tuple-element.67.rows_ref), custom_call_target="tpu_custom_call" | custom-call | tf_op jit(solution)/shard_map/weight_gradient/pallas_call | solution.py:432
  (50 shorter events, 24.3 us)
Async XLA Ops:
  0.6 12.2 %collective-permute-start.3 = (bf16[3,128,512]{2,1,0:T(8,128)(2,1)}, bf16[3,128,512]{2,1,0:T(8,128)(2,1)S(1)}, u32[]{:S(2)}, u32[]{:S(2)}) collective-permute-start(bf16[3,128,512]{2,1,0:T(8,128)(2,1)} %bitcast.13), channel_id=1, source_target_pairs={{0,64},{16,80},{32,96},{48,112},{64,0},{80,16},{96,32},{112,48},{1... | collective-permute-start | bytes 1179656 | tf_op jit(solution)/shard_map/ppermute | solution.py:481
  4.3 11.9 %collective-permute-start.2 = (bf16[3,128,512]{2,1,0:T(8,128)(2,1)}, bf16[3,128,512]{2,1,0:T(8,128)(2,1)S(1)}, u32[]{:S(2)}, u32[]{:S(2)}) collective-permute-start(bf16[3,128,512]{2,1,0:T(8,128)(2,1)} %bitcast.14), channel_id=1, source_target_pairs={{0,16},{16,0},{32,48},{48,32},{64,80},{80,64},{96,112},{112,96},{1... | collective-permute-start | bytes 1179656 | tf_op jit(solution)/shard_map/ppermute | solution.py:481
  7.2 15.3 %collective-permute-start = (bf16[3,128,512]{2,1,0:T(8,128)(2,1)}, bf16[3,128,512]{2,1,0:T(8,128)(2,1)S(1)}, u32[]{:S(2)}, u32[]{:S(2)}) collective-permute-start(bf16[3,128,512]{2,1,0:T(8,128)(2,1)} %bitcast.15), channel_id=1, source_target_pairs={{0,32},{16,48},{32,64},{48,80},{64,96},{80,112},{96,0},{112,16},{1... | collective-permute-start | bytes 1179656 | tf_op jit(solution)/shard_map/ppermute | solution.py:481
  7.5 18.1 %collective-permute-start.1 = (bf16[3,128,512]{2,1,0:T(8,128)(2,1)}, bf16[3,128,512]{2,1,0:T(8,128)(2,1)S(1)}, u32[]{:S(2)}, u32[]{:S(2)}) collective-permute-start(bf16[3,128,512]{2,1,0:T(8,128)(2,1)} %bitcast.16), channel_id=1, source_target_pairs={{0,96},{16,112},{32,0},{48,16},{64,32},{80,48},{96,64},{112,80},{1... | collective-permute-start | bytes 1179656 | tf_op jit(solution)/shard_map/ppermute | solution.py:481
  12.9 17.6 %collective-permute-start.6 = (bf16[3,128,512]{2,1,0:T(8,128)(2,1)S(1)}, bf16[3,128,512]{2,1,0:T(8,128)(2,1)S(1)}, u32[]{:S(2)}, u32[]{:S(2)}) collective-permute-start(bf16[3,128,512]{2,1,0:T(8,128)(2,1)S(1)} %collective-permute-done.3.refs_4_), channel_id=1, source_target_pairs={{0,16},{16,0},{32,48},{48,32},{64,80},{80,64},{96,112},{112,96},{1... | collective-permute-start | bytes 1179656 | tf_op jit(solution)/shard_map/ppermute | solution.py:481
  16.2 18.3 %collective-permute-start.4 = (bf16[3,128,512]{2,1,0:T(8,128)(2,1)S(1)}, bf16[3,128,512]{2,1,0:T(8,128)(2,1)S(1)}, u32[]{:S(2)}, u32[]{:S(2)}) collective-permute-start(bf16[3,128,512]{2,1,0:T(8,128)(2,1)S(1)} %collective-permute-done.2.refs_1_), channel_id=1, source_target_pairs={{0,32},{16,48},{32,64},{48,80},{64,96},{80,112},{96,0},{112,16},{1... | collective-permute-start | bytes 1179656 | tf_op jit(solution)/shard_map/ppermute | solution.py:481
  17.4 17.1 %collective-permute-start.5 = (bf16[3,128,512]{2,1,0:T(8,128)(2,1)S(1)}, bf16[3,128,512]{2,1,0:T(8,128)(2,1)S(1)}, u32[]{:S(2)}, u32[]{:S(2)}) collective-permute-start(bf16[3,128,512]{2,1,0:T(8,128)(2,1)S(1)} %collective-permute-done.2.refs_1_), channel_id=1, source_target_pairs={{0,96},{16,112},{32,0},{48,16},{64,32},{80,48},{96,64},{112,80},{1... | collective-permute-start | bytes 1179656 | tf_op jit(solution)/shard_map/ppermute | solution.py:481
  22.5 6.5 %collective-permute-start.7 = (bf16[64,1024]{1,0:T(8,128)(2,1)S(1)}, bf16[64,1024]{1,0:T(8,128)(2,1)S(1)}, u32[]{:S(2)}, u32[]{:S(2)}) collective-permute-start(bf16[64,1024]{1,0:T(8,128)(2,1)S(1)} %spare_facts.1), channel_id=1, source_target_pairs={{0,16},{16,0},{32,48},{48,32},{64,80},{80,64},{96,112},{112,96},{1... | collective-permute-start | bytes 393224 | tf_op jit(solution)/shard_map/ppermute | solution.py:481
  25.6 6.1 %collective-permute-start.10 = (f32[8,128]{1,0:T(8,128)S(1)}, f32[8,128]{1,0:T(8,128)S(1)}, u32[]{:S(2)}, u32[]{:S(2)}) collective-permute-start(f32[8,128]{1,0:T(8,128)S(1)} %broadcast_in_dim.24.refs_8_), channel_id=1, source_target_pairs={{0,96},{16,112},{32,0},{48,16},{64,32},{80,48},{96,64},{112,80},{1... | collective-permute-start | bytes 12296 | tf_op jit(solution)/shard_map/ppermute | solution.py:481
  25.6 1.9 %copy-start = (bf16[3,512,1024]{2,1,0:T(8,128)(2,1)S(1)}, bf16[3,512,1024]{2,1,0:T(8,128)(2,1)}, u32[]{:S(2)}) copy-start(bf16[3,512,1024]{2,1,0:T(8,128)(2,1)} %hbm_weight) | copy-start | bytes 9437188
  29.0 3.7 %collective-permute-start.8 = (f32[8,128]{1,0:T(8,128)S(1)}, f32[8,128]{1,0:T(8,128)S(1)}, u32[]{:S(2)}, u32[]{:S(2)}) collective-permute-start(f32[8,128]{1,0:T(8,128)S(1)} %broadcast_in_dim.24.refs_8_), channel_id=1, source_target_pairs={{0,32},{16,48},{32,64},{48,80},{64,96},{80,112},{96,0},{112,16},{1... | collective-permute-start | bytes 12296 | tf_op jit(solution)/shard_map/ppermute | solution.py:481
  30.5 4.0 %collective-permute-start.9 = (f32[8,128]{1,0:T(8,128)S(1)}, f32[8,128]{1,0:T(8,128)S(1)}, u32[]{:S(2)}, u32[]{:S(2)}) collective-permute-start(f32[8,128]{1,0:T(8,128)S(1)} %broadcast_in_dim.24.refs_8_), channel_id=1, source_target_pairs={{0,64},{16,80},{32,96},{48,112},{64,0},{80,16},{96,32},{112,48},{1... | collective-permute-start | bytes 12296 | tf_op jit(solution)/shard_map/ppermute | solution.py:481
  38.2 4.9 %collective-permute-start.11 = (bf16[8,8,40,128]{3,2,1,0:T(8,128)(2,1)S(1)}, bf16[8,8,40,128]{3,2,1,0:T(8,128)(2,1)S(1)}, u32[]{:S(2)}, u32[]{:S(2)}) collective-permute-start(bf16[8,8,40,128]{3,2,1,0:T(8,128)(2,1)S(1)} %get-tuple-element.45), channel_id=1, source_target_pairs={{0,1},{1,0},{2,3},{3,2},{4,5},{5,4},{6,7},{7,6},{8,9},{9,8},{10,11... | collective-permute-start | bytes 1966088 | tf_op jit(solution)/shard_map/ppermute | solution.py:43
  43.3 41.1 %copy-start.4 = (f32[8192]{0:T(1024)S(1)}, f32[8192]{0:T(1024)}, u32[]{:S(2)}) copy-start(f32[8192]{0:T(1024)} %param.10) | copy-start | bytes 98308
  66.8 13.1 %all-to-all-start.1 = ((bf16[8,8,40,128]{3,2,1,0:T(8,128)(2,1)}), bf16[8,8,40,128]{3,2,1,0:T(8,128)(2,1)S(1)}, u32[]{:S(2)}, u32[]{:S(2)}) async-start(bf16[8,8,40,128]{3,2,1,0:T(8,128)(2,1)} %get-tuple-element.48), calls=%async_computation.1 | async-start | bytes 1310720 | tf_op jit(solution)/shard_map/all_to_all | solution.py:509
  70.3 7.1 %collective-permute-start.12 = (bf16[2,64,1024]{2,1,0:T(8,128)(2,1)S(1)}, bf16[2,64,1024]{2,1,0:T(8,128)(2,1)S(1)}, u32[]{:S(2)}, u32[]{:S(2)}) collective-permute-start(bf16[2,64,1024]{2,1,0:T(8,128)(2,1)S(1)} %pad_maximum_fusion.refs_0_), channel_id=1, source_target_pairs={{0,32},{16,48},{32,64},{48,80},{64,96},{80,112},{96,0},{112,16},{1... | collective-permute-start | bytes 786440 | tf_op jit(solution)/shard_map/ppermute | solution.py:481
  70.8 6.7 %collective-permute-start.13 = (bf16[2,64,1024]{2,1,0:T(8,128)(2,1)S(1)}, bf16[2,64,1024]{2,1,0:T(8,128)(2,1)S(1)}, u32[]{:S(2)}, u32[]{:S(2)}) collective-permute-start(bf16[2,64,1024]{2,1,0:T(8,128)(2,1)S(1)} %pad_maximum_fusion.refs_0_), channel_id=1, source_target_pairs={{0,96},{16,112},{32,0},{48,16},{64,32},{80,48},{96,64},{112,80},{1... | collective-permute-start | bytes 786440 | tf_op jit(solution)/shard_map/ppermute | solution.py:481
  79.8 4.6 %collective-permute-start.14 = (bf16[8,8,40,128]{3,2,1,0:T(8,128)(2,1)S(1)}, bf16[8,8,40,128]{3,2,1,0:T(8,128)(2,1)S(1)}, u32[]{:S(2)}, u32[]{:S(2)}) collective-permute-start(bf16[8,8,40,128]{3,2,1,0:T(8,128)(2,1)S(1)} %all-to-all-done.1.own_ref), channel_id=1, source_target_pairs={{0,1},{1,0},{2,3},{3,2},{4,5},{5,4},{6,7},{7,6},{8,9},{9,8},{10,11... | collective-permute-start | bytes 1966088 | tf_op jit(solution)/shard_map/ppermute | solution.py:43
  82.7 10.0 %collective-permute-start.15 = (bf16[2,64,1024]{2,1,0:T(8,128)(2,1)S(1)}, bf16[2,64,1024]{2,1,0:T(8,128)(2,1)S(1)}, u32[]{:S(2)}, u32[]{:S(2)}) collective-permute-start(bf16[2,64,1024]{2,1,0:T(8,128)(2,1)S(1)} %pad_maximum_fusion.refs_0_), channel_id=1, source_target_pairs={{0,64},{16,80},{32,96},{48,112},{64,0},{80,16},{96,32},{112,48},{1... | collective-permute-start | bytes 786440 | tf_op jit(solution)/shard_map/ppermute | solution.py:481
  84.4 8.2 %copy-start.2 = (bf16[1,128,1024]{2,1,0:T(8,128)(2,1)S(1)}, bf16[1,128,1024]{2,1,0:T(8,128)(2,1)}, u32[]{:S(2)}) copy-start(bf16[1,128,1024]{2,1,0:T(8,128)(2,1)} %param.8) | copy-start | bytes 786436
  84.4 8.2 %copy-start.6 = (s32[1,128]{1,0:T(1,128)S(1)}, s32[1,128]{1,0:T(1,128)}, u32[]{:S(2)}) copy-start(s32[1,128]{1,0:T(1,128)} %mask_ref.3) | copy-start | bytes 1540
  107.2 2.4 %collective-permute-start.16 = (bf16[8,8,48,128]{3,2,1,0:T(8,128)(2,1)S(1)}, bf16[8,8,48,128]{3,2,1,0:T(8,128)(2,1)S(1)}, u32[]{:S(2)}, u32[]{:S(2)}) collective-permute-start(bf16[8,8,48,128]{3,2,1,0:T(8,128)(2,1)S(1)} %get-tuple-element.62), channel_id=1, source_target_pairs={{0,1},{1,0},{2,3},{3,2},{4,5},{5,4},{6,7},{7,6},{8,9},{9,8},{10,11... | collective-permute-start | bytes 2359304 | tf_op jit(solution)/shard_map/ppermute | solution.py:43
  132.2 13.3 %all-to-all-start.4 = ((bf16[8,8,40,128]{3,2,1,0:T(8,128)(2,1)}), bf16[8,8,40,128]{3,2,1,0:T(8,128)(2,1)S(1)}, u32[]{:S(2)}, u32[]{:S(2)}) async-start(bf16[8,8,40,128]{3,2,1,0:T(8,128)(2,1)} %get-tuple-element.63), calls=%async_computation.4 | async-start | bytes 1310720 | tf_op jit(solution)/shard_map/all_to_all | solution.py:522
  145.5 4.3 %collective-permute-start.17 = (bf16[8,8,40,128]{3,2,1,0:T(8,128)(2,1)S(1)}, bf16[8,8,40,128]{3,2,1,0:T(8,128)(2,1)S(1)}, u32[]{:S(2)}, u32[]{:S(2)}) collective-permute-start(bf16[8,8,40,128]{3,2,1,0:T(8,128)(2,1)S(1)} %all-to-all-done.4.own_ref), channel_id=1, source_target_pairs={{0,1},{1,0},{2,3},{3,2},{4,5},{5,4},{6,7},{7,6},{8,9},{9,8},{10,11... | collective-permute-start | bytes 1966088 | tf_op jit(solution)/shard_map/ppermute | solution.py:43
  (3 other events, 2.6 us)

commit v5 on v4

--- a/solution.py
+++ b/solution.py
@@ -115,14 +115,16 @@
 
 
 def unite_kernel(*refs):
-    blocks, length_refs = refs[:GROUPS], refs[GROUPS : GROUPS + 4]
-    weight_ref, rows_ref, mine_ref, other_ref, slot_ref = refs[GROUPS + 4 :]
+    blocks, length_refs = refs[:GROUPS], refs[GROUPS : GROUPS + 3]
+    weight_ref, near_rows_ref, far_rows_ref, mine_ref, other_ref, slot_ref = refs[GROUPS + 3 :]
+    lengths = [jnp.broadcast_to(ref[0:1, 0:1], (1, 512)) for ref in length_refs]
+    lengths = {0: lengths[0], 3: lengths[1], 1: lengths[2], 2: GROUPS * ROWS - sum(lengths)}
     first = lax.axis_index("c") == 0
     groups = [group_at(*place) for place in PLACES]
     lane = lax.broadcasted_iota(jnp.int32, (1, 512), 1).astype(f32)
     have = [
         jnp.clip(
-            jnp.broadcast_to(length_refs[-dx % 4][0:1, 0:1], (1, 512))
+            lengths[dx]
             - lax.rem(lax.axis_index("yh") + dy, 2).astype(f32) * HALF,
             0.0,
             float(HALF),
@@ -163,8 +165,12 @@
                 within = lax.broadcasted_iota(jnp.int32, (ROWS, 512), 0).astype(f32) < have[k]
                 base = (k - 4 * half) * ROWS
                 kept.append(jnp.where(within, own, moved[base : base + ROWS]))
+            upper = jnp.concatenate([rows[0:PIECE] for rows in kept], axis=0)
+            lower = jnp.concatenate([rows[PIECE:ROWS] for rows in kept], axis=0)
+            part = pl.ds(half * 4 * PIECE, 4 * PIECE)
+            near_rows_ref[s, part, :] = jnp.where(first, upper, lower).astype(bf16)
+            far_rows_ref[s, part, :] = jnp.where(first, lower, upper).astype(bf16)
             rows = jnp.concatenate(kept, axis=0).astype(bf16)
-            rows_ref[s, pl.ds(half * 4 * ROWS, 4 * ROWS), :] = rows
             term = jnp.dot(rows, weight_ref[s], preferred_element_type=f32)
             total = term if total is None else total + term
         for k in range(4):
@@ -177,10 +183,11 @@
 def unite(blocks, lengths, weight):
     return pl.pallas_call(
         unite_kernel,
-        in_specs=[VECTORS] * (GROUPS + 5),
-        out_specs=[VECTORS] * 4,
+        in_specs=[VECTORS] * (GROUPS + 4),
+        out_specs=[VECTORS] * 5,
         out_shape=(
-            jax.ShapeDtypeStruct((3, GROUPS * ROWS, 512), bf16),
+            jax.ShapeDtypeStruct((3, GROUPS * PIECE, 512), bf16),
+            jax.ShapeDtypeStruct((3, GROUPS * PIECE, 512), bf16),
             jax.ShapeDtypeStruct((GROUPS, 8, PIECE, 128), bf16),
             jax.ShapeDtypeStruct((GROUPS, 8, PIECE, 128), bf16),
             jax.ShapeDtypeStruct((8, 512), f32),
@@ -406,44 +413,73 @@
     )(every, logits, chosen, side, gain, united, head)
 
 
-def grad_kernel(side_ref, own_ref, other_ref, rows_ref, out_ref, wide, grads):
+def assemble(grad_ref, wide, grads):
+    for k, place in enumerate(PLACES):
+        group = group_at(*place)
+        for j in range(8):
+            wide[k * PIECE : (k + 1) * PIECE, j * 128 : (j + 1) * 128] = grad_ref[
+                j, group
+            ].astype(f32)
+    grads[...] = wide[...].astype(bf16)
+
+
+def near_kernel(grad_ref, rows_ref, out_ref, wide, grads):
+    assemble(grad_ref, wide, grads)
+    for s in range(3):
+        out_ref[s] = lax.dot_general(
+            rows_ref[s], grads[...], (((0,), (0,)), ((), ())), preferred_element_type=f32
+        )
+
+
+def far_kernel(side_ref, grad_ref, rows_ref, near_ref, out_ref, wide, grads):
     @pl.when((pl.program_id(0) == 0) & (pl.program_id(1) == 0))
     def _():
-        first = lax.axis_index("c") == 0
-        for k, place in enumerate(PLACES):
-            group = group_at(*place)
-            for j in range(8):
-                a = own_ref[j, group].astype(f32)
-                b = other_ref[j, group].astype(f32)
-                base = k * ROWS
-                wide[base : base + PIECE, j * 128 : (j + 1) * 128] = jnp.where(first, a, b)
-                wide[base + PIECE : base + ROWS, j * 128 : (j + 1) * 128] = jnp.where(first, b, a)
-        grads[...] = wide[...].astype(bf16)
+        assemble(grad_ref, wide, grads)
 
     factor = (2 * HALF) / jnp.maximum(side_ref[3:4, 0:1], 1.0)
-    out_ref[0] = factor * lax.dot_general(
-        rows_ref[0], grads[...], (((0,), (0,)), ((), ())), preferred_element_type=f32
-    )
-
-
-def weight_gradient(side, own, other, rows):
-    total = GROUPS * ROWS
+    here = near_ref[pl.program_id(0), pl.ds(pl.program_id(1) * 256, 256), :]
+    out_ref[0] = factor * (
+        here
+        + lax.dot_general(
+            rows_ref[0], grads[...], (((0,), (0,)), ((), ())), preferred_element_type=f32
+        )
+    )
+
+
+def near_gradient(own, rows):
+    total = GROUPS * PIECE
+    return pl.pallas_call(
+        near_kernel,
+        in_specs=[VECTORS] * 2,
+        out_specs=VECTORS,
+        out_shape=jax.ShapeDtypeStruct((3, 512, 1024), f32),
+        scratch_shapes=[pltpu.VMEM((total, 1024), f32), pltpu.VMEM((total, 1024), bf16)],
+        compiler_params=pltpu.CompilerParams(vmem_limit_bytes=16 * MIB),
+        cost_estimate=pl.CostEstimate(
+            flops=6 * total * 512 * 1024, bytes_accessed=6 * MIB, transcendentals=0
+        ),
+        name="near_gradient",
+    )(own, rows)
+
+
+def weight_gradient(side, other, rows, near):
+    total = GROUPS * PIECE
     whole = lambda shape: pl.BlockSpec(shape, lambda s, i: (0,) * len(shape))
     return pl.pallas_call(
-        grad_kernel,
+        far_kernel,
         grid=(3, 2),
         in_specs=[
             whole((8, HALF)),
             whole((8, GROUPS, PIECE, 128)),
-            whole((8, GROUPS, PIECE, 128)),
             pl.BlockSpec((1, total, 256), lambda s, i: (s, 0, i)),
+            VECTORS,
         ],
         out_specs=pl.BlockSpec((1, 256, 1024), lambda s, i: (s, i, 0)),
         out_shape=jax.ShapeDtypeStruct((3, 512, 1024), f32),
         scratch_shapes=[pltpu.VMEM((total, 1024), f32), pltpu.VMEM((total, 1024), bf16)],
-        compiler_params=pltpu.CompilerParams(vmem_limit_bytes=40 * MIB),
+        compiler_params=pltpu.CompilerParams(vmem_limit_bytes=24 * MIB),
         name="weight_gradient",
-    )(side, own, other, rows)
+    )(side, other, rows, near)
 
 
 def sum_kernel(piece_ref, out_ref, extra_ref):
@@ -498,10 +534,10 @@
     left, right, weight = lax.optimization_barrier((left, right, unite_weight))
     weight, near = stage(weight, own)
     wide_length = jnp.broadcast_to(later.astype(f32), (8, HALF))
-    all_lengths = [wide_length] + [route(wide_length, dx, 0) for dx in range(1, 4)]
+    all_lengths = [wide_length, route(wide_length, 1, 0), route(wide_length, 3, 0)]
     over_far, pair = lax.optimization_barrier((over_far, pair))
     blocks = [near, over, left, right, far, over_left, over_right, over_far]
-    rows, mine, other, slots = unite(blocks, all_lengths, weight)
+    near_rows, far_rows, mine, other, slots = unite(blocks, all_lengths, weight)
 
     copies, _ = gather_sum(mine, other)
     copies, pair = lax.optimization_barrier((copies, pair))
@@ -526,7 +562,8 @@
     seq_kl = (seq_sum / 32.0 / jnp.maximum(side[4, 0], 1.0)).reshape(1)
     own_grad, seq_kl = lax.optimization_barrier((own_grad, seq_kl))
     other_grad = swap(own_grad, "c", 1, 2)
-    unite_grad = weight_gradient(side, own_grad, other_grad, rows)
+    near_part = near_gradient(own_grad, near_rows)
+    unite_grad = weight_gradient(side, other_grad, far_rows, near_part)
     return (seq_kl, unite_grad)
 
 

time: 157 us -> 155 us (0.987)
  waiting for transfers between devices: 27.9 us -> 24.1 us
    ppermute x14 -> x13, waiting for transfers between devices: 11.4 us -> 9.34 us  [route(): return lax.ppermute(value, GROUP, pairs)]
    ppermute x4, waiting for transfers between devices: 6.86 us -> 5.14 us  [swap(): return lax.ppermute(value, axis, [(i, i ^ bit) for i in range(count)])]
    pallas_call x2 -> x3, Pallas kernels: 9.55 us -> 10.6 us  [the longest x1 4.99 us: weight_gradient(): pl.pallas_call(far_kernel, grid=(3, 2), in_specs=[whole((8, HALF)), whole...]
    ppermute x14 -> x13, starting transfers between devices: 24 us -> 24.1 us  [route(): return lax.ppermute(value, GROUP, pairs)]
  transfers between devices with their start and end apart: 20 -> 19, of which waited for: 11 -> 9; matrix products, arithmetic and copies ran while one was open for 1% -> 1% of each run, Pallas kernels for 6% -> 7%
where the time goes in v5:
time: 155 us; the launch traced here: 154 us
  blocking collectives  52.6 us (34%)
  starting transfers between devices  40.8 us (26%)
  Pallas kernels  26.8 us (17%)
  waiting for transfers between devices  24.1 us (16%)
  local copies, waits for them, and re-layouts  5.02 us (3%)
  between operations  3.94 us (3%)
    all_to_all x2, blocking collectives, gather_sum(): lax.all_to_all(pair.reshape((64,) + pair.shape[2:]), CHIPS, 0, 0, tiled=T...  43.6 us
    ppermute x13, starting transfers between devices, route(): return lax.ppermute(value, GROUP, pairs)  24.1 us
    ppermute x4, starting transfers between devices, swap(): return lax.ppermute(value, axis, [(i, i ^ bit) for i in range(count)])  9.65 us
    ppermute x13, waiting for transfers between devices, route(): return lax.ppermute(value, GROUP, pairs)  9.34 us
    all_to_all x1, blocking collectives, spread(): lax.all_to_all(jnp.broadcast_to(value[None], (count,) + value.shape), axe...  8.92 us
    pallas_call x1, Pallas kernels, head_forward(): pl.pallas_call(head_kernel, in_specs=[VECTORS] * 3 + [FAR], out_specs=[VE...  8.2 us
    all_to_all x1, waiting for transfers between devices, local(): own_grad = lax.all_to_all(copies, RING, 0, 0, tiled=True)  7.25 us
    ppermute x4, waiting for transfers between devices, swap(): return lax.ppermute(value, axis, [(i, i ^ bit) for i in range(count)])  5.14 us
  transfers between devices with their start and end apart: 19, of which 9 were waited for; matrix products, arithmetic and copies ran while one was open for 1% of the time, Pallas kernels for 7%

profile of v5, /device:TPU:1, one launch (start us, length us, event | category | flops | bytes accessed | tf_op | source)
XLA Modules:
  0.0 154.4 jit_solution(777424553907560658)
XLA Ops:
  0.6 3.7 %collective-permute-start.3 = (bf16[3,128,512]{2,1,0:T(8,128)(2,1)}, bf16[3,128,512]{2,1,0:T(8,128)(2,1)S(1)}, u32[]{:S(2)}, u32[]{:S(2)}) collective-permute-start(bf16[3,128,512]{2,1,0:T(8,128)(2,1)} %bitcast.13), channel_id=1, source_target_pairs={{0,64},{16,80},{32,96},{48,112},{64,0},{80,16},{96,32},{112,48},{1... | collective-permute-start | bytes 1179656 | tf_op jit(solution)/shard_map/ppermute | solution.py:517
  4.3 2.9 %collective-permute-start.2 = (bf16[3,128,512]{2,1,0:T(8,128)(2,1)}, bf16[3,128,512]{2,1,0:T(8,128)(2,1)S(1)}, u32[]{:S(2)}, u32[]{:S(2)}) collective-permute-start(bf16[3,128,512]{2,1,0:T(8,128)(2,1)} %bitcast.14), channel_id=1, source_target_pairs={{0,16},{16,0},{32,48},{48,32},{64,80},{80,64},{96,112},{112,96},{1... | collective-permute-start | bytes 1179656 | tf_op jit(solution)/shard_map/ppermute | solution.py:517
  7.5 2.4 %collective-permute-start.1 = (bf16[3,128,512]{2,1,0:T(8,128)(2,1)}, bf16[3,128,512]{2,1,0:T(8,128)(2,1)S(1)}, u32[]{:S(2)}, u32[]{:S(2)}) collective-permute-start(bf16[3,128,512]{2,1,0:T(8,128)(2,1)} %bitcast.16), channel_id=1, source_target_pairs={{0,96},{16,112},{32,0},{48,16},{64,32},{80,48},{96,64},{112,80},{1... | collective-permute-start | bytes 1179656 | tf_op jit(solution)/shard_map/ppermute | solution.py:517
  9.9 3.0 %collective-permute-done.3.refs_4_ = bf16[3,128,512]{2,1,0:T(8,128)(2,1)S(1)} collective-permute-done((bf16[3,128,512]{2,1,0:T(8,128)(2,1)}, bf16[3,128,512]{2,1,0:T(8,128)(2,1)S(1)}, u32[]{:S(2)}, u32[]{:S(2)}) %collective-permute-start.3) | collective-permute-done | bytes 393248 | tf_op jit(solution)/shard_map/ppermute | solution.py:517
  12.9 3.3 %collective-permute-start.6 = (bf16[3,128,512]{2,1,0:T(8,128)(2,1)S(1)}, bf16[3,128,512]{2,1,0:T(8,128)(2,1)S(1)}, u32[]{:S(2)}, u32[]{:S(2)}) collective-permute-start(bf16[3,128,512]{2,1,0:T(8,128)(2,1)S(1)} %collective-permute-done.3.refs_4_), channel_id=1, source_target_pairs={{0,16},{16,0},{32,48},{48,32},{64,80},{80,64},{96,112},{112,96},{1... | collective-permute-start | bytes 1179656 | tf_op jit(solution)/shard_map/ppermute | solution.py:517
  22.5 3.1 %collective-permute-start.7 = (bf16[64,1024]{1,0:T(8,128)(2,1)S(1)}, bf16[64,1024]{1,0:T(8,128)(2,1)S(1)}, u32[]{:S(2)}, u32[]{:S(2)}) collective-permute-start(bf16[64,1024]{1,0:T(8,128)(2,1)S(1)} %spare_facts.1), channel_id=1, source_target_pairs={{0,16},{16,0},{32,48},{48,32},{64,80},{80,64},{96,112},{112,96},{1... | collective-permute-start | bytes 393224 | tf_op jit(solution)/shard_map/ppermute | solution.py:517
  29.2 2.5 %collective-permute-start.9 = (f32[8,128]{1,0:T(8,128)S(1)}, f32[8,128]{1,0:T(8,128)S(1)}, u32[]{:S(2)}, u32[]{:S(2)}) collective-permute-start(f32[8,128]{1,0:T(8,128)S(1)} %broadcast_in_dim.24.refs_8_), channel_id=1, source_target_pairs={{0,96},{16,112},{32,0},{48,16},{64,32},{80,48},{96,64},{112,80},{1... | collective-permute-start | bytes 12296 | tf_op jit(solution)/shard_map/ppermute | solution.py:517
  32.5 3.8 %unite.1 = (bf16[3,320,512]{2,1,0:T(8,128)(2,1)S(1)}, bf16[3,320,512]{2,1,0:T(8,128)(2,1)S(1)}, bf16[8,8,40,128]{3,2,1,0:T(8,128)(2,1)S(1)}, bf16[8,8,40,128]{3,2,1,0:T(8,128)(2,1)S(1)}, f32[8,512]{1,0:T(8,128)S(1)}) custom-call(bf16[3,128,512]{2,1,0:T(8,128)(2,1)S(1)} %get-tuple-element.37.refs_0_, bf16[3,128,512]{2,1,0:T(8,128)(2,1)S(1)} %collective-permute-done.2.refs_1_, ...), custom_call_target="tpu_custom_call" | custom-call | tf_op jit(solution)/shard_map/unite/pallas_call | solution.py:184
  36.3 3.7 %collective-permute-start.10 = (bf16[8,8,40,128]{3,2,1,0:T(8,128)(2,1)S(1)}, bf16[8,8,40,128]{3,2,1,0:T(8,128)(2,1)S(1)}, u32[]{:S(2)}, u32[]{:S(2)}) collective-permute-start(bf16[8,8,40,128]{3,2,1,0:T(8,128)(2,1)S(1)} %get-tuple-element.46), channel_id=1, source_target_pairs={{0,1},{1,0},{2,3},{3,2},{4,5},{5,4},{6,7},{7,6},{8,9},{9,8},{10,11... | collective-permute-start | bytes 1966088 | tf_op jit(solution)/shard_map/ppermute | solution.py:43
  41.9 22.2 %all_to_all.25.piece_ref = bf16[64,40,128]{2,1,0:T(8,128)(2,1)S(1)} all-to-all(bf16[64,40,128]{2,1,0:T(8,128)(2,1)S(1)} %bitcast.21), channel_id=1, replica_groups=mesh['x'=4,'yh'=2,'z'=4,'yl'=2,'c'=2] {'x','yh','z','yl'}, dimensions={0} | all-to-all | bytes 1310720 | tf_op jit(solution)/shard_map/all_to_all | solution.py:500
  65.0 3.5 %all-to-all-start.1 = ((bf16[8,8,40,128]{3,2,1,0:T(8,128)(2,1)}), bf16[8,8,40,128]{3,2,1,0:T(8,128)(2,1)S(1)}, u32[]{:S(2)}, u32[]{:S(2)}) async-start(bf16[8,8,40,128]{3,2,1,0:T(8,128)(2,1)} %get-tuple-element.49), calls=%async_computation.1 | async-start | bytes 1310720 | tf_op jit(solution)/shard_map/all_to_all | solution.py:545
  69.1 2.3 %collective-permute-start.12 = (bf16[2,64,1024]{2,1,0:T(8,128)(2,1)S(1)}, bf16[2,64,1024]{2,1,0:T(8,128)(2,1)S(1)}, u32[]{:S(2)}, u32[]{:S(2)}) collective-permute-start(bf16[2,64,1024]{2,1,0:T(8,128)(2,1)S(1)} %pad_maximum_fusion.refs_0_), channel_id=1, source_target_pairs={{0,96},{16,112},{32,0},{48,16},{64,32},{80,48},{96,64},{112,80},{1... | collective-permute-start | bytes 786440 | tf_op jit(solution)/shard_map/ppermute | solution.py:517
  71.3 4.4 %collective-permute-done.11.refs_1_ = bf16[2,64,1024]{2,1,0:T(8,128)(2,1)S(1)} collective-permute-done((bf16[2,64,1024]{2,1,0:T(8,128)(2,1)S(1)}, bf16[2,64,1024]{2,1,0:T(8,128)(2,1)S(1)}, u32[]{:S(2)}, u32[]{:S(2)}) %collective-permute-start.11) | collective-permute-done | bytes 262176 | tf_op jit(solution)/shard_map/ppermute | solution.py:517
  75.7 2.4 %all-to-all-done.1.own_ref = bf16[8,8,40,128]{3,2,1,0:T(8,128)(2,1)S(1)} async-done(((bf16[8,8,40,128]{3,2,1,0:T(8,128)(2,1)}), bf16[8,8,40,128]{3,2,1,0:T(8,128)(2,1)S(1)}, u32[]{:S(2)}, u32[]{:S(2)}) %all-to-all-start.1) | async-done | bytes 655392 | tf_op jit(solution)/shard_map/all_to_all | solution.py:545
  78.1 2.9 %collective-permute-start.13 = (bf16[8,8,40,128]{3,2,1,0:T(8,128)(2,1)S(1)}, bf16[8,8,40,128]{3,2,1,0:T(8,128)(2,1)S(1)}, u32[]{:S(2)}, u32[]{:S(2)}) collective-permute-start(bf16[8,8,40,128]{3,2,1,0:T(8,128)(2,1)S(1)} %all-to-all-done.1.own_ref), channel_id=1, source_target_pairs={{0,1},{1,0},{2,3},{3,2},{4,5},{5,4},{6,7},{7,6},{8,9},{9,8},{10,11... | collective-permute-start | bytes 1966088 | tf_op jit(solution)/shard_map/ppermute | solution.py:43
  82.7 8.2 %head_forward.1 = (f32[1024,128]{1,0:T(8,128)S(1)}, f32[8,128]{1,0:T(8,128)S(1)}, bf16[80,8192]{1,0:T(8,128)(2,1)S(1)}, bf16[1024,8192]{1,0:T(8,128)(2,1)S(1)}) custom-call(bf16[8,8,40,128]{3,2,1,0:T(8,128)(2,1)S(1)} %all-to-all-done.1.own_ref, bf16[8,8,40,128]{3,2,1,0:T(8,128)(2,1)S(1)} %collective-permute-done.13.other_ref, f32[1,8192]{1,0:T(1,128)S(1)} %bitcast.18, ...), custom_call_target="tpu_custom_call" | custom-call | flops 4294967296 | bytes 16777216 | tf_op jit(solution)/shard_map/head_forward/pallas_call | solution.py:247
  90.9 2.2 %row_stats.1 = (f32[1024,128]{1,0:T(8,128)S(1)}, f32[8,128]{1,0:T(8,128)S(1)}, f32[8,128]{1,0:T(8,128)S(1)}) custom-call(s32[1]{0:T(128)S(6)} %copy.9.length_ref, f32[1024,128]{1,0:T(8,128)S(1)} %get-tuple-element.52.logit_ref, f32[8,128]{1,0:T(8,128)S(1)} %get-tuple-element.53.scale_ref, bf16[128,1024]{1,0:T(8,128)(2,1)S(1)} %bitcast.11, ...), custom_call_target="tpu_custom_call" | custom-call | tf_op jit(solution)/shard_map/row_stats/pallas_call | solution.py:338
  93.2 8.9 %all_to_all.26.every_ref = f32[16,8,128]{2,1,0:T(8,128)S(1)} all-to-all(f32[16,8,128]{2,1,0:T(8,128)S(1)} %broadcast_in_dim.25), channel_id=1, replica_groups=mesh['x'=4,'yh'=2,'z'=4,'yl'=2,'c'=2] {'z','yl','c'}, dimensions={0} | all-to-all | bytes 131072 | tf_op jit(solution)/shard_map/all_to_all | solution.py:37
  102.1 3.4 %head_backward.1 = (bf16[8,8,48,128]{3,2,1,0:T(8,128)(2,1)S(1)}, bf16[8,8,48,128]{3,2,1,0:T(8,128)(2,1)S(1)}) custom-call(f32[16,8,128]{2,1,0:T(8,128)S(1)} %all_to_all.26.every_ref, f32[1024,128]{1,0:T(8,128)S(1)} %get-tuple-element.52.logit_ref, f32[1024,128]{1,0:T(8,128)S(1)} %get-tuple-element.58.chosen_ref, f32[8,128]{1,0:T(8,128)S(1)} %get-tuple-element.59.side_ref, ...), custom_call_target="tpu_custom_call" | custom-call | tf_op jit(solution)/shard_map/head_backward/pallas_call | solution.py:403
  108.1 21.4 %all_to_all.27.piece_ref = bf16[64,48,128]{2,1,0:T(8,128)(2,1)S(1)} all-to-all(bf16[64,48,128]{2,1,0:T(8,128)(2,1)S(1)} %bitcast.20), channel_id=1, replica_groups=mesh['x'=4,'yh'=2,'z'=4,'yl'=2,'c'=2] {'x','yh','z','yl'}, dimensions={0} | all-to-all | bytes 1572864 | tf_op jit(solution)/shard_map/all_to_all | solution.py:500
  130.5 3.5 %all-to-all-start.4 = ((bf16[8,8,40,128]{3,2,1,0:T(8,128)(2,1)}), bf16[8,8,40,128]{3,2,1,0:T(8,128)(2,1)S(1)}, u32[]{:S(2)}, u32[]{:S(2)}) async-start(bf16[8,8,40,128]{3,2,1,0:T(8,128)(2,1)} %get-tuple-element.64), calls=%async_computation.4 | async-start | bytes 1310720 | tf_op jit(solution)/shard_map/all_to_all | solution.py:558
  136.6 7.3 %all-to-all-done.4.grad_ref = bf16[8,8,40,128]{3,2,1,0:T(8,128)(2,1)S(1)} async-done(((bf16[8,8,40,128]{3,2,1,0:T(8,128)(2,1)}), bf16[8,8,40,128]{3,2,1,0:T(8,128)(2,1)S(1)}, u32[]{:S(2)}, u32[]{:S(2)}) %all-to-all-start.4) | async-done | bytes 655392 | tf_op jit(solution)/shard_map/all_to_all | solution.py:558
  143.8 2.6 %collective-permute-start.16 = (bf16[8,8,40,128]{3,2,1,0:T(8,128)(2,1)S(1)}, bf16[8,8,40,128]{3,2,1,0:T(8,128)(2,1)S(1)}, u32[]{:S(2)}, u32[]{:S(2)}) collective-permute-start(bf16[8,8,40,128]{3,2,1,0:T(8,128)(2,1)S(1)} %all-to-all-done.4.grad_ref), channel_id=1, source_target_pairs={{0,1},{1,0},{2,3},{3,2},{4,5},{5,4},{6,7},{7,6},{8,9},{9,8},{10,11... | collective-permute-start | bytes 1966088 | tf_op jit(solution)/shard_map/ppermute | solution.py:43
  148.2 5.0 %weight_gradient.1 = f32[3,512,1024]{2,1,0:T(8,128)} custom-call(f32[8,128]{1,0:T(8,128)S(1)} %get-tuple-element.59.side_ref, bf16[8,8,40,128]{3,2,1,0:T(8,128)(2,1)S(1)} %collective-permute-done.16.grad_ref, bf16[3,320,512]{2,1,0:T(8,128)(2,1)S(1)} %get-tuple-element.68.rows_ref, f32[3,512,1024]{2,1,0:T(8,128)S(1)} %near_gradient.1.near_ref), custom_call_target="tpu_custom_call" | custom-call | tf_op jit(solution)/shard_map/weight_gradient/pallas_call | solution.py:468
  (49 shorter events, 21.9 us)
Async XLA Ops:
  0.6 12.2 %collective-permute-start.3 = (bf16[3,128,512]{2,1,0:T(8,128)(2,1)}, bf16[3,128,512]{2,1,0:T(8,128)(2,1)S(1)}, u32[]{:S(2)}, u32[]{:S(2)}) collective-permute-start(bf16[3,128,512]{2,1,0:T(8,128)(2,1)} %bitcast.13), channel_id=1, source_target_pairs={{0,64},{16,80},{32,96},{48,112},{64,0},{80,16},{96,32},{112,48},{1... | collective-permute-start | bytes 1179656 | tf_op jit(solution)/shard_map/ppermute | solution.py:517
  4.3 11.9 %collective-permute-start.2 = (bf16[3,128,512]{2,1,0:T(8,128)(2,1)}, bf16[3,128,512]{2,1,0:T(8,128)(2,1)S(1)}, u32[]{:S(2)}, u32[]{:S(2)}) collective-permute-start(bf16[3,128,512]{2,1,0:T(8,128)(2,1)} %bitcast.14), channel_id=1, source_target_pairs={{0,16},{16,0},{32,48},{48,32},{64,80},{80,64},{96,112},{112,96},{1... | collective-permute-start | bytes 1179656 | tf_op jit(solution)/shard_map/ppermute | solution.py:517
  7.2 15.3 %collective-permute-start = (bf16[3,128,512]{2,1,0:T(8,128)(2,1)}, bf16[3,128,512]{2,1,0:T(8,128)(2,1)S(1)}, u32[]{:S(2)}, u32[]{:S(2)}) collective-permute-start(bf16[3,128,512]{2,1,0:T(8,128)(2,1)} %bitcast.15), channel_id=1, source_target_pairs={{0,32},{16,48},{32,64},{48,80},{64,96},{80,112},{96,0},{112,16},{1... | collective-permute-start | bytes 1179656 | tf_op jit(solution)/shard_map/ppermute | solution.py:517
  7.5 18.1 %collective-permute-start.1 = (bf16[3,128,512]{2,1,0:T(8,128)(2,1)}, bf16[3,128,512]{2,1,0:T(8,128)(2,1)S(1)}, u32[]{:S(2)}, u32[]{:S(2)}) collective-permute-start(bf16[3,128,512]{2,1,0:T(8,128)(2,1)} %bitcast.16), channel_id=1, source_target_pairs={{0,96},{16,112},{32,0},{48,16},{64,32},{80,48},{96,64},{112,80},{1... | collective-permute-start | bytes 1179656 | tf_op jit(solution)/shard_map/ppermute | solution.py:517
  12.9 18.9 %collective-permute-start.6 = (bf16[3,128,512]{2,1,0:T(8,128)(2,1)S(1)}, bf16[3,128,512]{2,1,0:T(8,128)(2,1)S(1)}, u32[]{:S(2)}, u32[]{:S(2)}) collective-permute-start(bf16[3,128,512]{2,1,0:T(8,128)(2,1)S(1)} %collective-permute-done.3.refs_4_), channel_id=1, source_target_pairs={{0,16},{16,0},{32,48},{48,32},{64,80},{80,64},{96,112},{112,96},{1... | collective-permute-start | bytes 1179656 | tf_op jit(solution)/shard_map/ppermute | solution.py:517
  16.2 16.3 %collective-permute-start.4 = (bf16[3,128,512]{2,1,0:T(8,128)(2,1)S(1)}, bf16[3,128,512]{2,1,0:T(8,128)(2,1)S(1)}, u32[]{:S(2)}, u32[]{:S(2)}) collective-permute-start(bf16[3,128,512]{2,1,0:T(8,128)(2,1)S(1)} %collective-permute-done.2.refs_1_), channel_id=1, source_target_pairs={{0,32},{16,48},{32,64},{48,80},{64,96},{80,112},{96,0},{112,16},{1... | collective-permute-start | bytes 1179656 | tf_op jit(solution)/shard_map/ppermute | solution.py:517
  17.4 15.1 %collective-permute-start.5 = (bf16[3,128,512]{2,1,0:T(8,128)(2,1)S(1)}, bf16[3,128,512]{2,1,0:T(8,128)(2,1)S(1)}, u32[]{:S(2)}, u32[]{:S(2)}) collective-permute-start(bf16[3,128,512]{2,1,0:T(8,128)(2,1)S(1)} %collective-permute-done.2.refs_1_), channel_id=1, source_target_pairs={{0,96},{16,112},{32,0},{48,16},{64,32},{80,48},{96,64},{112,80},{1... | collective-permute-start | bytes 1179656 | tf_op jit(solution)/shard_map/ppermute | solution.py:517
  22.5 6.7 %collective-permute-start.7 = (bf16[64,1024]{1,0:T(8,128)(2,1)S(1)}, bf16[64,1024]{1,0:T(8,128)(2,1)S(1)}, u32[]{:S(2)}, u32[]{:S(2)}) collective-permute-start(bf16[64,1024]{1,0:T(8,128)(2,1)S(1)} %spare_facts.1), channel_id=1, source_target_pairs={{0,16},{16,0},{32,48},{48,32},{64,80},{80,64},{96,112},{112,96},{1... | collective-permute-start | bytes 393224 | tf_op jit(solution)/shard_map/ppermute | solution.py:517
  25.6 6.1 %collective-permute-start.8 = (f32[8,128]{1,0:T(8,128)S(1)}, f32[8,128]{1,0:T(8,128)S(1)}, u32[]{:S(2)}, u32[]{:S(2)}) collective-permute-start(f32[8,128]{1,0:T(8,128)S(1)} %broadcast_in_dim.24.refs_8_), channel_id=1, source_target_pairs={{0,32},{16,48},{32,64},{48,80},{64,96},{80,112},{96,0},{112,16},{1... | collective-permute-start | bytes 12296 | tf_op jit(solution)/shard_map/ppermute | solution.py:517
  25.9 1.9 %copy-start = (bf16[3,512,1024]{2,1,0:T(8,128)(2,1)S(1)}, bf16[3,512,1024]{2,1,0:T(8,128)(2,1)}, u32[]{:S(2)}) copy-start(bf16[3,512,1024]{2,1,0:T(8,128)(2,1)} %hbm_weight) | copy-start | bytes 9437188
  27.8 1.0 copy-start.3
  29.2 3.2 %collective-permute-start.9 = (f32[8,128]{1,0:T(8,128)S(1)}, f32[8,128]{1,0:T(8,128)S(1)}, u32[]{:S(2)}, u32[]{:S(2)}) collective-permute-start(f32[8,128]{1,0:T(8,128)S(1)} %broadcast_in_dim.24.refs_8_), channel_id=1, source_target_pairs={{0,96},{16,112},{32,0},{48,16},{64,32},{80,48},{96,64},{112,80},{1... | collective-permute-start | bytes 12296 | tf_op jit(solution)/shard_map/ppermute | solution.py:517
  36.3 5.4 %collective-permute-start.10 = (bf16[8,8,40,128]{3,2,1,0:T(8,128)(2,1)S(1)}, bf16[8,8,40,128]{3,2,1,0:T(8,128)(2,1)S(1)}, u32[]{:S(2)}, u32[]{:S(2)}) collective-permute-start(bf16[8,8,40,128]{3,2,1,0:T(8,128)(2,1)S(1)} %get-tuple-element.46), channel_id=1, source_target_pairs={{0,1},{1,0},{2,3},{3,2},{4,5},{5,4},{6,7},{7,6},{8,9},{9,8},{10,11... | collective-permute-start | bytes 1966088 | tf_op jit(solution)/shard_map/ppermute | solution.py:43
  41.9 40.8 %copy-start.4 = (f32[8192]{0:T(1024)S(1)}, f32[8192]{0:T(1024)}, u32[]{:S(2)}) copy-start(f32[8192]{0:T(1024)} %param.10) | copy-start | bytes 98308
  65.0 13.1 %all-to-all-start.1 = ((bf16[8,8,40,128]{3,2,1,0:T(8,128)(2,1)}), bf16[8,8,40,128]{3,2,1,0:T(8,128)(2,1)S(1)}, u32[]{:S(2)}, u32[]{:S(2)}) async-start(bf16[8,8,40,128]{3,2,1,0:T(8,128)(2,1)} %get-tuple-element.49), calls=%async_computation.1 | async-start | bytes 1310720 | tf_op jit(solution)/shard_map/all_to_all | solution.py:545
  68.6 7.1 %collective-permute-start.11 = (bf16[2,64,1024]{2,1,0:T(8,128)(2,1)S(1)}, bf16[2,64,1024]{2,1,0:T(8,128)(2,1)S(1)}, u32[]{:S(2)}, u32[]{:S(2)}) collective-permute-start(bf16[2,64,1024]{2,1,0:T(8,128)(2,1)S(1)} %pad_maximum_fusion.refs_0_), channel_id=1, source_target_pairs={{0,32},{16,48},{32,64},{48,80},{64,96},{80,112},{96,0},{112,16},{1... | collective-permute-start | bytes 786440 | tf_op jit(solution)/shard_map/ppermute | solution.py:517
  69.1 6.7 %collective-permute-start.12 = (bf16[2,64,1024]{2,1,0:T(8,128)(2,1)S(1)}, bf16[2,64,1024]{2,1,0:T(8,128)(2,1)S(1)}, u32[]{:S(2)}, u32[]{:S(2)}) collective-permute-start(bf16[2,64,1024]{2,1,0:T(8,128)(2,1)S(1)} %pad_maximum_fusion.refs_0_), channel_id=1, source_target_pairs={{0,96},{16,112},{32,0},{48,16},{64,32},{80,48},{96,64},{112,80},{1... | collective-permute-start | bytes 786440 | tf_op jit(solution)/shard_map/ppermute | solution.py:517
  78.1 4.6 %collective-permute-start.13 = (bf16[8,8,40,128]{3,2,1,0:T(8,128)(2,1)S(1)}, bf16[8,8,40,128]{3,2,1,0:T(8,128)(2,1)S(1)}, u32[]{:S(2)}, u32[]{:S(2)}) collective-permute-start(bf16[8,8,40,128]{3,2,1,0:T(8,128)(2,1)S(1)} %all-to-all-done.1.own_ref), channel_id=1, source_target_pairs={{0,1},{1,0},{2,3},{3,2},{4,5},{5,4},{6,7},{7,6},{8,9},{9,8},{10,11... | collective-permute-start | bytes 1966088 | tf_op jit(solution)/shard_map/ppermute | solution.py:43
  81.0 9.9 %collective-permute-start.14 = (bf16[2,64,1024]{2,1,0:T(8,128)(2,1)S(1)}, bf16[2,64,1024]{2,1,0:T(8,128)(2,1)S(1)}, u32[]{:S(2)}, u32[]{:S(2)}) collective-permute-start(bf16[2,64,1024]{2,1,0:T(8,128)(2,1)S(1)} %pad_maximum_fusion.refs_0_), channel_id=1, source_target_pairs={{0,64},{16,80},{32,96},{48,112},{64,0},{80,16},{96,32},{112,48},{1... | collective-permute-start | bytes 786440 | tf_op jit(solution)/shard_map/ppermute | solution.py:517
  82.7 8.2 %copy-start.2 = (bf16[1,128,1024]{2,1,0:T(8,128)(2,1)S(1)}, bf16[1,128,1024]{2,1,0:T(8,128)(2,1)}, u32[]{:S(2)}) copy-start(bf16[1,128,1024]{2,1,0:T(8,128)(2,1)} %param.8) | copy-start | bytes 786436
  82.7 8.2 %copy-start.6 = (s32[1,128]{1,0:T(1,128)S(1)}, s32[1,128]{1,0:T(1,128)}, u32[]{:S(2)}) copy-start(s32[1,128]{1,0:T(1,128)} %mask_ref.3) | copy-start | bytes 1540
  105.5 2.4 %collective-permute-start.15 = (bf16[8,8,48,128]{3,2,1,0:T(8,128)(2,1)S(1)}, bf16[8,8,48,128]{3,2,1,0:T(8,128)(2,1)S(1)}, u32[]{:S(2)}, u32[]{:S(2)}) collective-permute-start(bf16[8,8,48,128]{3,2,1,0:T(8,128)(2,1)S(1)} %get-tuple-element.63), channel_id=1, source_target_pairs={{0,1},{1,0},{2,3},{3,2},{4,5},{5,4},{6,7},{7,6},{8,9},{9,8},{10,11... | collective-permute-start | bytes 2359304 | tf_op jit(solution)/shard_map/ppermute | solution.py:43
  130.5 13.3 %all-to-all-start.4 = ((bf16[8,8,40,128]{3,2,1,0:T(8,128)(2,1)}), bf16[8,8,40,128]{3,2,1,0:T(8,128)(2,1)S(1)}, u32[]{:S(2)}, u32[]{:S(2)}) async-start(bf16[8,8,40,128]{3,2,1,0:T(8,128)(2,1)} %get-tuple-element.64), calls=%async_computation.4 | async-start | bytes 1310720 | tf_op jit(solution)/shard_map/all_to_all | solution.py:558
  143.8 4.4 %collective-permute-start.16 = (bf16[8,8,40,128]{3,2,1,0:T(8,128)(2,1)S(1)}, bf16[8,8,40,128]{3,2,1,0:T(8,128)(2,1)S(1)}, u32[]{:S(2)}, u32[]{:S(2)}) collective-permute-start(bf16[8,8,40,128]{3,2,1,0:T(8,128)(2,1)S(1)} %all-to-all-done.4.grad_ref), channel_id=1, source_target_pairs={{0,1},{1,0},{2,3},{3,2},{4,5},{5,4},{6,7},{7,6},{8,9},{9,8},{10,11... | collective-permute-start | bytes 1966088 | tf_op jit(solution)/shard_map/ppermute | solution.py:43
  (2 other events, 1.6 us)

commit v6 on v5

--- a/solution.py
+++ b/solution.py
@@ -431,19 +431,32 @@
         )
 
 
-def far_kernel(side_ref, grad_ref, rows_ref, near_ref, out_ref, wide, grads):
-    @pl.when((pl.program_id(0) == 0) & (pl.program_id(1) == 0))
-    def _():
-        assemble(grad_ref, wide, grads)
-
+def far_kernel(side_ref, grad_ref, rows_ref, near_ref, out_ref, wide, grads, done, sems):
+    assemble(grad_ref, wide, grads)
     factor = (2 * HALF) / jnp.maximum(side_ref[3:4, 0:1], 1.0)
-    here = near_ref[pl.program_id(0), pl.ds(pl.program_id(1) * 256, 256), :]
-    out_ref[0] = factor * (
-        here
-        + lax.dot_general(
-            rows_ref[0], grads[...], (((0,), (0,)), ((), ())), preferred_element_type=f32
-        )
-    )
+    copies = []
+    for s in range(3):
+        for i in range(2):
+            part = slice(i * 256, (i + 1) * 256)
+            done[s, part, :] = factor * (
+                near_ref[s, part, :]
+                + lax.dot_general(
+                    rows_ref[s, :, part],
+                    grads[...],
+                    (((0,), (0,)), ((), ())),
+                    preferred_element_type=f32,
+                )
+            )
+            copies.append(
+                pltpu.make_async_copy(
+                    done.at[s, pl.ds(i * 256, 256)],
+                    out_ref.at[s, pl.ds(i * 256, 256)],
+                    sems.at[2 * s + i],
+                )
+            )
+            copies[-1].start()
+    for copy in copies:
+        copy.wait()
 
 
 def near_gradient(own, rows):
@@ -464,19 +477,17 @@
 
 def weight_gradient(side, other, rows, near):
     total = GROUPS * PIECE
-    whole = lambda shape: pl.BlockSpec(shape, lambda s, i: (0,) * len(shape))
     return pl.pallas_call(
         far_kernel,
-        grid=(3, 2),
-        in_specs=[
-            whole((8, HALF)),
-            whole((8, GROUPS, PIECE, 128)),
-            pl.BlockSpec((1, total, 256), lambda s, i: (s, 0, i)),
-            VECTORS,
+        in_specs=[VECTORS] * 4,
+        out_specs=FAR,
+        out_shape=jax.ShapeDtypeStruct((3, 512, 1024), f32),
+        scratch_shapes=[
+            pltpu.VMEM((total, 1024), f32),
+            pltpu.VMEM((total, 1024), bf16),
+            pltpu.VMEM((3, 512, 1024), f32),
+            pltpu.SemaphoreType.DMA((6,)),
         ],
-        out_specs=pl.BlockSpec((1, 256, 1024), lambda s, i: (s, i, 0)),
-        out_shape=jax.ShapeDtypeStruct((3, 512, 1024), f32),
-        scratch_shapes=[pltpu.VMEM((total, 1024), f32), pltpu.VMEM((total, 1024), bf16)],
         compiler_params=pltpu.CompilerParams(vmem_limit_bytes=24 * MIB),
         name="weight_gradient",
     )(side, other, rows, near)

time: 155 us -> 153 us (0.987)
  Pallas kernels: 26.8 us -> 25.1 us
    pallas_call x1, Pallas kernels: 4.99 us -> 3.21 us  [weight_gradient(): pl.pallas_call(far_kernel, in_specs=[VECTORS] * 4, out_specs=FAR, out_sha...]
where the time goes in v6:
time: 153 us
  blocking collectives  52.6 us (34%)
  starting transfers between devices  40.8 us (27%)
  Pallas kernels  25.1 us (16%)
  waiting for transfers between devices  24.1 us (16%)
  local copies, waits for them, and re-layouts  5.02 us (3%)
  between operations  3.95 us (3%)
    all_to_all x2, blocking collectives, gather_sum(): lax.all_to_all(pair.reshape((64,) + pair.shape[2:]), CHIPS, 0, 0, tiled=T...  43.6 us
    ppermute x13, starting transfers between devices, route(): return lax.ppermute(value, GROUP, pairs)  24.1 us
    ppermute x4, starting transfers between devices, swap(): return lax.ppermute(value, axis, [(i, i ^ bit) for i in range(count)])  9.65 us
    ppermute x13, waiting for transfers between devices, route(): return lax.ppermute(value, GROUP, pairs)  9.34 us
    all_to_all x1, blocking collectives, spread(): lax.all_to_all(jnp.broadcast_to(value[None], (count,) + value.shape), axe...  8.92 us
    pallas_call x1, Pallas kernels, head_forward(): pl.pallas_call(head_kernel, in_specs=[VECTORS] * 3 + [FAR], out_specs=[VE...  8.2 us
    all_to_all x1, waiting for transfers between devices, local(): own_grad = lax.all_to_all(copies, RING, 0, 0, tiled=True)  7.25 us
    ppermute x4, waiting for transfers between devices, swap(): return lax.ppermute(value, axis, [(i, i ^ bit) for i in range(count)])  5.14 us
  transfers between devices with their start and end apart: 19, of which 9 were waited for; matrix products, arithmetic and copies ran while one was open for 1% of the time, Pallas kernels for 7%

profile of v6, /device:TPU:1, one launch (start us, length us, event | category | flops | bytes accessed | tf_op | source)
XLA Modules:
  0.0 152.6 jit_solution(15774156910851916049)
XLA Ops:
  0.6 3.7 %collective-permute-start.3 = (bf16[3,128,512]{2,1,0:T(8,128)(2,1)}, bf16[3,128,512]{2,1,0:T(8,128)(2,1)S(1)}, u32[]{:S(2)}, u32[]{:S(2)}) collective-permute-start(bf16[3,128,512]{2,1,0:T(8,128)(2,1)} %bitcast.13), channel_id=1, source_target_pairs={{0,64},{16,80},{32,96},{48,112},{64,0},{80,16},{96,32},{112,48},{1... | collective-permute-start | bytes 1179656 | tf_op jit(solution)/shard_map/ppermute | solution.py:528
  4.3 2.9 %collective-permute-start.2 = (bf16[3,128,512]{2,1,0:T(8,128)(2,1)}, bf16[3,128,512]{2,1,0:T(8,128)(2,1)S(1)}, u32[]{:S(2)}, u32[]{:S(2)}) collective-permute-start(bf16[3,128,512]{2,1,0:T(8,128)(2,1)} %bitcast.14), channel_id=1, source_target_pairs={{0,16},{16,0},{32,48},{48,32},{64,80},{80,64},{96,112},{112,96},{1... | collective-permute-start | bytes 1179656 | tf_op jit(solution)/shard_map/ppermute | solution.py:528
  7.5 2.4 %collective-permute-start.1 = (bf16[3,128,512]{2,1,0:T(8,128)(2,1)}, bf16[3,128,512]{2,1,0:T(8,128)(2,1)S(1)}, u32[]{:S(2)}, u32[]{:S(2)}) collective-permute-start(bf16[3,128,512]{2,1,0:T(8,128)(2,1)} %bitcast.16), channel_id=1, source_target_pairs={{0,96},{16,112},{32,0},{48,16},{64,32},{80,48},{96,64},{112,80},{1... | collective-permute-start | bytes 1179656 | tf_op jit(solution)/shard_map/ppermute | solution.py:528
  9.9 3.0 %collective-permute-done.3.refs_4_ = bf16[3,128,512]{2,1,0:T(8,128)(2,1)S(1)} collective-permute-done((bf16[3,128,512]{2,1,0:T(8,128)(2,1)}, bf16[3,128,512]{2,1,0:T(8,128)(2,1)S(1)}, u32[]{:S(2)}, u32[]{:S(2)}) %collective-permute-start.3) | collective-permute-done | bytes 393248 | tf_op jit(solution)/shard_map/ppermute | solution.py:528
  12.9 3.3 %collective-permute-start.6 = (bf16[3,128,512]{2,1,0:T(8,128)(2,1)S(1)}, bf16[3,128,512]{2,1,0:T(8,128)(2,1)S(1)}, u32[]{:S(2)}, u32[]{:S(2)}) collective-permute-start(bf16[3,128,512]{2,1,0:T(8,128)(2,1)S(1)} %collective-permute-done.3.refs_4_), channel_id=1, source_target_pairs={{0,16},{16,0},{32,48},{48,32},{64,80},{80,64},{96,112},{112,96},{1... | collective-permute-start | bytes 1179656 | tf_op jit(solution)/shard_map/ppermute | solution.py:528
  22.5 3.1 %collective-permute-start.7 = (bf16[64,1024]{1,0:T(8,128)(2,1)S(1)}, bf16[64,1024]{1,0:T(8,128)(2,1)S(1)}, u32[]{:S(2)}, u32[]{:S(2)}) collective-permute-start(bf16[64,1024]{1,0:T(8,128)(2,1)S(1)} %spare_facts.1), channel_id=1, source_target_pairs={{0,16},{16,0},{32,48},{48,32},{64,80},{80,64},{96,112},{112,96},{1... | collective-permute-start | bytes 393224 | tf_op jit(solution)/shard_map/ppermute | solution.py:528
  29.2 2.5 %collective-permute-start.9 = (f32[8,128]{1,0:T(8,128)S(1)}, f32[8,128]{1,0:T(8,128)S(1)}, u32[]{:S(2)}, u32[]{:S(2)}) collective-permute-start(f32[8,128]{1,0:T(8,128)S(1)} %broadcast_in_dim.24.refs_8_), channel_id=1, source_target_pairs={{0,96},{16,112},{32,0},{48,16},{64,32},{80,48},{96,64},{112,80},{1... | collective-permute-start | bytes 12296 | tf_op jit(solution)/shard_map/ppermute | solution.py:528
  32.5 3.8 %unite.1 = (bf16[3,320,512]{2,1,0:T(8,128)(2,1)S(1)}, bf16[3,320,512]{2,1,0:T(8,128)(2,1)S(1)}, bf16[8,8,40,128]{3,2,1,0:T(8,128)(2,1)S(1)}, bf16[8,8,40,128]{3,2,1,0:T(8,128)(2,1)S(1)}, f32[8,512]{1,0:T(8,128)S(1)}) custom-call(bf16[3,128,512]{2,1,0:T(8,128)(2,1)S(1)} %get-tuple-element.37.refs_0_, bf16[3,128,512]{2,1,0:T(8,128)(2,1)S(1)} %collective-permute-done.2.refs_1_, ...), custom_call_target="tpu_custom_call" | custom-call | tf_op jit(solution)/shard_map/unite/pallas_call | solution.py:184
  36.3 3.7 %collective-permute-start.10 = (bf16[8,8,40,128]{3,2,1,0:T(8,128)(2,1)S(1)}, bf16[8,8,40,128]{3,2,1,0:T(8,128)(2,1)S(1)}, u32[]{:S(2)}, u32[]{:S(2)}) collective-permute-start(bf16[8,8,40,128]{3,2,1,0:T(8,128)(2,1)S(1)} %get-tuple-element.46), channel_id=1, source_target_pairs={{0,1},{1,0},{2,3},{3,2},{4,5},{5,4},{6,7},{7,6},{8,9},{9,8},{10,11... | collective-permute-start | bytes 1966088 | tf_op jit(solution)/shard_map/ppermute | solution.py:43
  41.9 22.2 %all_to_all.25.piece_ref = bf16[64,40,128]{2,1,0:T(8,128)(2,1)S(1)} all-to-all(bf16[64,40,128]{2,1,0:T(8,128)(2,1)S(1)} %bitcast.21), channel_id=1, replica_groups=mesh['x'=4,'yh'=2,'z'=4,'yl'=2,'c'=2] {'x','yh','z','yl'}, dimensions={0} | all-to-all | bytes 1310720 | tf_op jit(solution)/shard_map/all_to_all | solution.py:511
  65.0 3.5 %all-to-all-start.1 = ((bf16[8,8,40,128]{3,2,1,0:T(8,128)(2,1)}), bf16[8,8,40,128]{3,2,1,0:T(8,128)(2,1)S(1)}, u32[]{:S(2)}, u32[]{:S(2)}) async-start(bf16[8,8,40,128]{3,2,1,0:T(8,128)(2,1)} %get-tuple-element.49), calls=%async_computation.1 | async-start | bytes 1310720 | tf_op jit(solution)/shard_map/all_to_all | solution.py:556
  69.1 2.3 %collective-permute-start.12 = (bf16[2,64,1024]{2,1,0:T(8,128)(2,1)S(1)}, bf16[2,64,1024]{2,1,0:T(8,128)(2,1)S(1)}, u32[]{:S(2)}, u32[]{:S(2)}) collective-permute-start(bf16[2,64,1024]{2,1,0:T(8,128)(2,1)S(1)} %pad_maximum_fusion.refs_0_), channel_id=1, source_target_pairs={{0,96},{16,112},{32,0},{48,16},{64,32},{80,48},{96,64},{112,80},{1... | collective-permute-start | bytes 786440 | tf_op jit(solution)/shard_map/ppermute | solution.py:528
  71.3 4.4 %collective-permute-done.11.refs_1_ = bf16[2,64,1024]{2,1,0:T(8,128)(2,1)S(1)} collective-permute-done((bf16[2,64,1024]{2,1,0:T(8,128)(2,1)S(1)}, bf16[2,64,1024]{2,1,0:T(8,128)(2,1)S(1)}, u32[]{:S(2)}, u32[]{:S(2)}) %collective-permute-start.11) | collective-permute-done | bytes 262176 | tf_op jit(solution)/shard_map/ppermute | solution.py:528
  75.7 2.4 %all-to-all-done.1.own_ref = bf16[8,8,40,128]{3,2,1,0:T(8,128)(2,1)S(1)} async-done(((bf16[8,8,40,128]{3,2,1,0:T(8,128)(2,1)}), bf16[8,8,40,128]{3,2,1,0:T(8,128)(2,1)S(1)}, u32[]{:S(2)}, u32[]{:S(2)}) %all-to-all-start.1) | async-done | bytes 655392 | tf_op jit(solution)/shard_map/all_to_all | solution.py:556
  78.1 2.9 %collective-permute-start.13 = (bf16[8,8,40,128]{3,2,1,0:T(8,128)(2,1)S(1)}, bf16[8,8,40,128]{3,2,1,0:T(8,128)(2,1)S(1)}, u32[]{:S(2)}, u32[]{:S(2)}) collective-permute-start(bf16[8,8,40,128]{3,2,1,0:T(8,128)(2,1)S(1)} %all-to-all-done.1.own_ref), channel_id=1, source_target_pairs={{0,1},{1,0},{2,3},{3,2},{4,5},{5,4},{6,7},{7,6},{8,9},{9,8},{10,11... | collective-permute-start | bytes 1966088 | tf_op jit(solution)/shard_map/ppermute | solution.py:43
  82.7 8.2 %head_forward.1 = (f32[1024,128]{1,0:T(8,128)S(1)}, f32[8,128]{1,0:T(8,128)S(1)}, bf16[80,8192]{1,0:T(8,128)(2,1)S(1)}, bf16[1024,8192]{1,0:T(8,128)(2,1)S(1)}) custom-call(bf16[8,8,40,128]{3,2,1,0:T(8,128)(2,1)S(1)} %all-to-all-done.1.own_ref, bf16[8,8,40,128]{3,2,1,0:T(8,128)(2,1)S(1)} %collective-permute-done.13.other_ref, f32[1,8192]{1,0:T(1,128)S(1)} %bitcast.18, ...), custom_call_target="tpu_custom_call" | custom-call | flops 4294967296 | bytes 16777216 | tf_op jit(solution)/shard_map/head_forward/pallas_call | solution.py:247
  90.9 2.2 %row_stats.1 = (f32[1024,128]{1,0:T(8,128)S(1)}, f32[8,128]{1,0:T(8,128)S(1)}, f32[8,128]{1,0:T(8,128)S(1)}) custom-call(s32[1]{0:T(128)S(6)} %copy.9.length_ref, f32[1024,128]{1,0:T(8,128)S(1)} %get-tuple-element.52.logit_ref, f32[8,128]{1,0:T(8,128)S(1)} %get-tuple-element.53.scale_ref, bf16[128,1024]{1,0:T(8,128)(2,1)S(1)} %bitcast.11, ...), custom_call_target="tpu_custom_call" | custom-call | tf_op jit(solution)/shard_map/row_stats/pallas_call | solution.py:338
  93.2 8.9 %all_to_all.26.every_ref = f32[16,8,128]{2,1,0:T(8,128)S(1)} all-to-all(f32[16,8,128]{2,1,0:T(8,128)S(1)} %broadcast_in_dim.25), channel_id=1, replica_groups=mesh['x'=4,'yh'=2,'z'=4,'yl'=2,'c'=2] {'z','yl','c'}, dimensions={0} | all-to-all | bytes 131072 | tf_op jit(solution)/shard_map/all_to_all | solution.py:37
  102.1 3.4 %head_backward.1 = (bf16[8,8,48,128]{3,2,1,0:T(8,128)(2,1)S(1)}, bf16[8,8,48,128]{3,2,1,0:T(8,128)(2,1)S(1)}) custom-call(f32[16,8,128]{2,1,0:T(8,128)S(1)} %all_to_all.26.every_ref, f32[1024,128]{1,0:T(8,128)S(1)} %get-tuple-element.52.logit_ref, f32[1024,128]{1,0:T(8,128)S(1)} %get-tuple-element.58.chosen_ref, f32[8,128]{1,0:T(8,128)S(1)} %get-tuple-element.59.side_ref, ...), custom_call_target="tpu_custom_call" | custom-call | tf_op jit(solution)/shard_map/head_backward/pallas_call | solution.py:403
  108.1 21.4 %all_to_all.27.piece_ref = bf16[64,48,128]{2,1,0:T(8,128)(2,1)S(1)} all-to-all(bf16[64,48,128]{2,1,0:T(8,128)(2,1)S(1)} %bitcast.20), channel_id=1, replica_groups=mesh['x'=4,'yh'=2,'z'=4,'yl'=2,'c'=2] {'x','yh','z','yl'}, dimensions={0} | all-to-all | bytes 1572864 | tf_op jit(solution)/shard_map/all_to_all | solution.py:511
  130.5 3.5 %all-to-all-start.4 = ((bf16[8,8,40,128]{3,2,1,0:T(8,128)(2,1)}), bf16[8,8,40,128]{3,2,1,0:T(8,128)(2,1)S(1)}, u32[]{:S(2)}, u32[]{:S(2)}) async-start(bf16[8,8,40,128]{3,2,1,0:T(8,128)(2,1)} %get-tuple-element.64), calls=%async_computation.4 | async-start | bytes 1310720 | tf_op jit(solution)/shard_map/all_to_all | solution.py:569
  136.6 7.3 %all-to-all-done.4.grad_ref = bf16[8,8,40,128]{3,2,1,0:T(8,128)(2,1)S(1)} async-done(((bf16[8,8,40,128]{3,2,1,0:T(8,128)(2,1)}), bf16[8,8,40,128]{3,2,1,0:T(8,128)(2,1)S(1)}, u32[]{:S(2)}, u32[]{:S(2)}) %all-to-all-start.4) | async-done | bytes 655392 | tf_op jit(solution)/shard_map/all_to_all | solution.py:569
  143.8 2.6 %collective-permute-start.16 = (bf16[8,8,40,128]{3,2,1,0:T(8,128)(2,1)S(1)}, bf16[8,8,40,128]{3,2,1,0:T(8,128)(2,1)S(1)}, u32[]{:S(2)}, u32[]{:S(2)}) collective-permute-start(bf16[8,8,40,128]{3,2,1,0:T(8,128)(2,1)S(1)} %all-to-all-done.4.grad_ref), channel_id=1, source_target_pairs={{0,1},{1,0},{2,3},{3,2},{4,5},{5,4},{6,7},{7,6},{8,9},{9,8},{10,11... | collective-permute-start | bytes 1966088 | tf_op jit(solution)/shard_map/ppermute | solution.py:43
  148.2 3.2 %weight_gradient.1 = f32[3,512,1024]{2,1,0:T(8,128)} custom-call(f32[8,128]{1,0:T(8,128)S(1)} %get-tuple-element.59.side_ref, bf16[8,8,40,128]{3,2,1,0:T(8,128)(2,1)S(1)} %collective-permute-done.16.grad_ref, bf16[3,320,512]{2,1,0:T(8,128)(2,1)S(1)} %get-tuple-element.68.rows_ref, f32[3,512,1024]{2,1,0:T(8,128)S(1)} %near_gradient.1.near_ref), custom_call_target="tpu_custom_call" | custom-call | tf_op jit(solution)/shard_map/weight_gradient/pallas_call | solution.py:480
  (49 shorter events, 21.9 us)
Async XLA Ops:
  0.6 12.2 %collective-permute-start.3 = (bf16[3,128,512]{2,1,0:T(8,128)(2,1)}, bf16[3,128,512]{2,1,0:T(8,128)(2,1)S(1)}, u32[]{:S(2)}, u32[]{:S(2)}) collective-permute-start(bf16[3,128,512]{2,1,0:T(8,128)(2,1)} %bitcast.13), channel_id=1, source_target_pairs={{0,64},{16,80},{32,96},{48,112},{64,0},{80,16},{96,32},{112,48},{1... | collective-permute-start | bytes 1179656 | tf_op jit(solution)/shard_map/ppermute | solution.py:528
  4.3 11.9 %collective-permute-start.2 = (bf16[3,128,512]{2,1,0:T(8,128)(2,1)}, bf16[3,128,512]{2,1,0:T(8,128)(2,1)S(1)}, u32[]{:S(2)}, u32[]{:S(2)}) collective-permute-start(bf16[3,128,512]{2,1,0:T(8,128)(2,1)} %bitcast.14), channel_id=1, source_target_pairs={{0,16},{16,0},{32,48},{48,32},{64,80},{80,64},{96,112},{112,96},{1... | collective-permute-start | bytes 1179656 | tf_op jit(solution)/shard_map/ppermute | solution.py:528
  7.2 15.3 %collective-permute-start = (bf16[3,128,512]{2,1,0:T(8,128)(2,1)}, bf16[3,128,512]{2,1,0:T(8,128)(2,1)S(1)}, u32[]{:S(2)}, u32[]{:S(2)}) collective-permute-start(bf16[3,128,512]{2,1,0:T(8,128)(2,1)} %bitcast.15), channel_id=1, source_target_pairs={{0,32},{16,48},{32,64},{48,80},{64,96},{80,112},{96,0},{112,16},{1... | collective-permute-start | bytes 1179656 | tf_op jit(solution)/shard_map/ppermute | solution.py:528
  7.5 18.1 %collective-permute-start.1 = (bf16[3,128,512]{2,1,0:T(8,128)(2,1)}, bf16[3,128,512]{2,1,0:T(8,128)(2,1)S(1)}, u32[]{:S(2)}, u32[]{:S(2)}) collective-permute-start(bf16[3,128,512]{2,1,0:T(8,128)(2,1)} %bitcast.16), channel_id=1, source_target_pairs={{0,96},{16,112},{32,0},{48,16},{64,32},{80,48},{96,64},{112,80},{1... | collective-permute-start | bytes 1179656 | tf_op jit(solution)/shard_map/ppermute | solution.py:528
  12.9 18.9 %collective-permute-start.6 = (bf16[3,128,512]{2,1,0:T(8,128)(2,1)S(1)}, bf16[3,128,512]{2,1,0:T(8,128)(2,1)S(1)}, u32[]{:S(2)}, u32[]{:S(2)}) collective-permute-start(bf16[3,128,512]{2,1,0:T(8,128)(2,1)S(1)} %collective-permute-done.3.refs_4_), channel_id=1, source_target_pairs={{0,16},{16,0},{32,48},{48,32},{64,80},{80,64},{96,112},{112,96},{1... | collective-permute-start | bytes 1179656 | tf_op jit(solution)/shard_map/ppermute | solution.py:528
  16.2 16.3 %collective-permute-start.4 = (bf16[3,128,512]{2,1,0:T(8,128)(2,1)S(1)}, bf16[3,128,512]{2,1,0:T(8,128)(2,1)S(1)}, u32[]{:S(2)}, u32[]{:S(2)}) collective-permute-start(bf16[3,128,512]{2,1,0:T(8,128)(2,1)S(1)} %collective-permute-done.2.refs_1_), channel_id=1, source_target_pairs={{0,32},{16,48},{32,64},{48,80},{64,96},{80,112},{96,0},{112,16},{1... | collective-permute-start | bytes 1179656 | tf_op jit(solution)/shard_map/ppermute | solution.py:528
  17.4 15.1 %collective-permute-start.5 = (bf16[3,128,512]{2,1,0:T(8,128)(2,1)S(1)}, bf16[3,128,512]{2,1,0:T(8,128)(2,1)S(1)}, u32[]{:S(2)}, u32[]{:S(2)}) collective-permute-start(bf16[3,128,512]{2,1,0:T(8,128)(2,1)S(1)} %collective-permute-done.2.refs_1_), channel_id=1, source_target_pairs={{0,96},{16,112},{32,0},{48,16},{64,32},{80,48},{96,64},{112,80},{1... | collective-permute-start | bytes 1179656 | tf_op jit(solution)/shard_map/ppermute | solution.py:528
  22.5 6.7 %collective-permute-start.7 = (bf16[64,1024]{1,0:T(8,128)(2,1)S(1)}, bf16[64,1024]{1,0:T(8,128)(2,1)S(1)}, u32[]{:S(2)}, u32[]{:S(2)}) collective-permute-start(bf16[64,1024]{1,0:T(8,128)(2,1)S(1)} %spare_facts.1), channel_id=1, source_target_pairs={{0,16},{16,0},{32,48},{48,32},{64,80},{80,64},{96,112},{112,96},{1... | collective-permute-start | bytes 393224 | tf_op jit(solution)/shard_map/ppermute | solution.py:528
  25.6 6.1 %collective-permute-start.8 = (f32[8,128]{1,0:T(8,128)S(1)}, f32[8,128]{1,0:T(8,128)S(1)}, u32[]{:S(2)}, u32[]{:S(2)}) collective-permute-start(f32[8,128]{1,0:T(8,128)S(1)} %broadcast_in_dim.24.refs_8_), channel_id=1, source_target_pairs={{0,32},{16,48},{32,64},{48,80},{64,96},{80,112},{96,0},{112,16},{1... | collective-permute-start | bytes 12296 | tf_op jit(solution)/shard_map/ppermute | solution.py:528
  25.9 1.9 %copy-start = (bf16[3,512,1024]{2,1,0:T(8,128)(2,1)S(1)}, bf16[3,512,1024]{2,1,0:T(8,128)(2,1)}, u32[]{:S(2)}) copy-start(bf16[3,512,1024]{2,1,0:T(8,128)(2,1)} %hbm_weight) | copy-start | bytes 9437188
  27.8 1.0 copy-start.3
  29.2 3.2 %collective-permute-start.9 = (f32[8,128]{1,0:T(8,128)S(1)}, f32[8,128]{1,0:T(8,128)S(1)}, u32[]{:S(2)}, u32[]{:S(2)}) collective-permute-start(f32[8,128]{1,0:T(8,128)S(1)} %broadcast_in_dim.24.refs_8_), channel_id=1, source_target_pairs={{0,96},{16,112},{32,0},{48,16},{64,32},{80,48},{96,64},{112,80},{1... | collective-permute-start | bytes 12296 | tf_op jit(solution)/shard_map/ppermute | solution.py:528
  36.3 5.4 %collective-permute-start.10 = (bf16[8,8,40,128]{3,2,1,0:T(8,128)(2,1)S(1)}, bf16[8,8,40,128]{3,2,1,0:T(8,128)(2,1)S(1)}, u32[]{:S(2)}, u32[]{:S(2)}) collective-permute-start(bf16[8,8,40,128]{3,2,1,0:T(8,128)(2,1)S(1)} %get-tuple-element.46), channel_id=1, source_target_pairs={{0,1},{1,0},{2,3},{3,2},{4,5},{5,4},{6,7},{7,6},{8,9},{9,8},{10,11... | collective-permute-start | bytes 1966088 | tf_op jit(solution)/shard_map/ppermute | solution.py:43
  41.9 40.8 %copy-start.4 = (f32[8192]{0:T(1024)S(1)}, f32[8192]{0:T(1024)}, u32[]{:S(2)}) copy-start(f32[8192]{0:T(1024)} %param.10) | copy-start | bytes 98308
  65.0 13.1 %all-to-all-start.1 = ((bf16[8,8,40,128]{3,2,1,0:T(8,128)(2,1)}), bf16[8,8,40,128]{3,2,1,0:T(8,128)(2,1)S(1)}, u32[]{:S(2)}, u32[]{:S(2)}) async-start(bf16[8,8,40,128]{3,2,1,0:T(8,128)(2,1)} %get-tuple-element.49), calls=%async_computation.1 | async-start | bytes 1310720 | tf_op jit(solution)/shard_map/all_to_all | solution.py:556
  68.6 7.1 %collective-permute-start.11 = (bf16[2,64,1024]{2,1,0:T(8,128)(2,1)S(1)}, bf16[2,64,1024]{2,1,0:T(8,128)(2,1)S(1)}, u32[]{:S(2)}, u32[]{:S(2)}) collective-permute-start(bf16[2,64,1024]{2,1,0:T(8,128)(2,1)S(1)} %pad_maximum_fusion.refs_0_), channel_id=1, source_target_pairs={{0,32},{16,48},{32,64},{48,80},{64,96},{80,112},{96,0},{112,16},{1... | collective-permute-start | bytes 786440 | tf_op jit(solution)/shard_map/ppermute | solution.py:528
  69.1 6.7 %collective-permute-start.12 = (bf16[2,64,1024]{2,1,0:T(8,128)(2,1)S(1)}, bf16[2,64,1024]{2,1,0:T(8,128)(2,1)S(1)}, u32[]{:S(2)}, u32[]{:S(2)}) collective-permute-start(bf16[2,64,1024]{2,1,0:T(8,128)(2,1)S(1)} %pad_maximum_fusion.refs_0_), channel_id=1, source_target_pairs={{0,96},{16,112},{32,0},{48,16},{64,32},{80,48},{96,64},{112,80},{1... | collective-permute-start | bytes 786440 | tf_op jit(solution)/shard_map/ppermute | solution.py:528
  78.1 4.6 %collective-permute-start.13 = (bf16[8,8,40,128]{3,2,1,0:T(8,128)(2,1)S(1)}, bf16[8,8,40,128]{3,2,1,0:T(8,128)(2,1)S(1)}, u32[]{:S(2)}, u32[]{:S(2)}) collective-permute-start(bf16[8,8,40,128]{3,2,1,0:T(8,128)(2,1)S(1)} %all-to-all-done.1.own_ref), channel_id=1, source_target_pairs={{0,1},{1,0},{2,3},{3,2},{4,5},{5,4},{6,7},{7,6},{8,9},{9,8},{10,11... | collective-permute-start | bytes 1966088 | tf_op jit(solution)/shard_map/ppermute | solution.py:43
  81.0 9.9 %collective-permute-start.14 = (bf16[2,64,1024]{2,1,0:T(8,128)(2,1)S(1)}, bf16[2,64,1024]{2,1,0:T(8,128)(2,1)S(1)}, u32[]{:S(2)}, u32[]{:S(2)}) collective-permute-start(bf16[2,64,1024]{2,1,0:T(8,128)(2,1)S(1)} %pad_maximum_fusion.refs_0_), channel_id=1, source_target_pairs={{0,64},{16,80},{32,96},{48,112},{64,0},{80,16},{96,32},{112,48},{1... | collective-permute-start | bytes 786440 | tf_op jit(solution)/shard_map/ppermute | solution.py:528
  82.7 8.2 %copy-start.2 = (bf16[1,128,1024]{2,1,0:T(8,128)(2,1)S(1)}, bf16[1,128,1024]{2,1,0:T(8,128)(2,1)}, u32[]{:S(2)}) copy-start(bf16[1,128,1024]{2,1,0:T(8,128)(2,1)} %param.8) | copy-start | bytes 786436
  82.7 8.2 %copy-start.6 = (s32[1,128]{1,0:T(1,128)S(1)}, s32[1,128]{1,0:T(1,128)}, u32[]{:S(2)}) copy-start(s32[1,128]{1,0:T(1,128)} %mask_ref.3) | copy-start | bytes 1540
  105.5 2.4 %collective-permute-start.15 = (bf16[8,8,48,128]{3,2,1,0:T(8,128)(2,1)S(1)}, bf16[8,8,48,128]{3,2,1,0:T(8,128)(2,1)S(1)}, u32[]{:S(2)}, u32[]{:S(2)}) collective-permute-start(bf16[8,8,48,128]{3,2,1,0:T(8,128)(2,1)S(1)} %get-tuple-element.63), channel_id=1, source_target_pairs={{0,1},{1,0},{2,3},{3,2},{4,5},{5,4},{6,7},{7,6},{8,9},{9,8},{10,11... | collective-permute-start | bytes 2359304 | tf_op jit(solution)/shard_map/ppermute | solution.py:43
  130.5 13.3 %all-to-all-start.4 = ((bf16[8,8,40,128]{3,2,1,0:T(8,128)(2,1)}), bf16[8,8,40,128]{3,2,1,0:T(8,128)(2,1)S(1)}, u32[]{:S(2)}, u32[]{:S(2)}) async-start(bf16[8,8,40,128]{3,2,1,0:T(8,128)(2,1)} %get-tuple-element.64), calls=%async_computation.4 | async-start | bytes 1310720 | tf_op jit(solution)/shard_map/all_to_all | solution.py:569
  143.8 4.4 %collective-permute-start.16 = (bf16[8,8,40,128]{3,2,1,0:T(8,128)(2,1)S(1)}, bf16[8,8,40,128]{3,2,1,0:T(8,128)(2,1)S(1)}, u32[]{:S(2)}, u32[]{:S(2)}) collective-permute-start(bf16[8,8,40,128]{3,2,1,0:T(8,128)(2,1)S(1)} %all-to-all-done.4.grad_ref), channel_id=1, source_target_pairs={{0,1},{1,0},{2,3},{3,2},{4,5},{5,4},{6,7},{7,6},{8,9},{9,8},{10,11... | collective-permute-start | bytes 1966088 | tf_op jit(solution)/shard_map/ppermute | solution.py:43
  (2 other events, 1.6 us)

commit v7 on v6

--- a/solution.py
+++ b/solution.py
@@ -233,12 +233,11 @@
         normed[part, :] = jnp.transpose(values * scale * gain_ref[:, part]).astype(bf16)
 
     scale_ref[...] = jnp.transpose(jnp.broadcast_to(scale, (HALF, HALF)))[0:8]
-    for i in range(0, 8, 2):
-        for k in (i, i + 1):
-            loads[k].wait()
-            if k + 3 < 8:
-                loads[k + 3].start()
-        part = slice(i * tile, (i + 2) * tile)
+    for i in range(8):
+        loads[i].wait()
+        if i + 3 < 8:
+            loads[i + 3].start()
+        part = slice(i * tile, (i + 1) * tile)
         logit_ref[part, :] = jnp.dot(held[part, :], normed[...], preferred_element_type=f32)
 
 

time: 153 us -> 153 us (level)
  transfers between devices with their start and end apart: 19 -> 19, of which waited for: 9 -> 10; matrix products, arithmetic and copies ran while one was open for 1% -> 1% of each run, Pallas kernels for 7% -> 6%
where the time goes in v7:
time: 153 us; the launch traced here: 152 us
  blocking collectives  53 us (35%)
  starting transfers between devices  40.8 us (27%)
  waiting for transfers between devices  24.3 us (16%)
  Pallas kernels  24.3 us (16%)
  local copies, waits for them, and re-layouts  5.02 us (3%)
  between operations  3.92 us (3%)
    all_to_all x2, blocking collectives, gather_sum(): lax.all_to_all(pair.reshape((64,) + pair.shape[2:]), CHIPS, 0, 0, tiled=T...  43.6 us
    ppermute x13, starting transfers between devices, route(): return lax.ppermute(value, GROUP, pairs)  24.1 us
    ppermute x4, starting transfers between devices, swap(): return lax.ppermute(value, axis, [(i, i ^ bit) for i in range(count)])  9.65 us
    ppermute x13, waiting for transfers between devices, route(): return lax.ppermute(value, GROUP, pairs)  9.54 us
    all_to_all x1, blocking collectives, spread(): lax.all_to_all(jnp.broadcast_to(value[None], (count,) + value.shape), axe...  9.32 us
    pallas_call x1, Pallas kernels, head_forward(): pl.pallas_call(head_kernel, in_specs=[VECTORS] * 3 + [FAR], out_specs=[VE...  7.5 us
    all_to_all x1, waiting for transfers between devices, local(): own_grad = lax.all_to_all(copies, RING, 0, 0, tiled=True)  7.25 us
    ppermute x4, waiting for transfers between devices, swap(): return lax.ppermute(value, axis, [(i, i ^ bit) for i in range(count)])  5.14 us
  transfers between devices with their start and end apart: 19, of which 10 were waited for; matrix products, arithmetic and copies ran while one was open for 1% of the time, Pallas kernels for 6%

profile of v7, /device:TPU:1, one launch (start us, length us, event | category | flops | bytes accessed | tf_op | source)
XLA Modules:
  0.0 152.5 jit_solution(12722140700691887987)
XLA Ops:
  0.6 3.7 %collective-permute-start.3 = (bf16[3,128,512]{2,1,0:T(8,128)(2,1)}, bf16[3,128,512]{2,1,0:T(8,128)(2,1)S(1)}, u32[]{:S(2)}, u32[]{:S(2)}) collective-permute-start(bf16[3,128,512]{2,1,0:T(8,128)(2,1)} %bitcast.13), channel_id=1, source_target_pairs={{0,64},{16,80},{32,96},{48,112},{64,0},{80,16},{96,32},{112,48},{1... | collective-permute-start | bytes 1179656 | tf_op jit(solution)/shard_map/ppermute | solution.py:527
  4.3 2.9 %collective-permute-start.2 = (bf16[3,128,512]{2,1,0:T(8,128)(2,1)}, bf16[3,128,512]{2,1,0:T(8,128)(2,1)S(1)}, u32[]{:S(2)}, u32[]{:S(2)}) collective-permute-start(bf16[3,128,512]{2,1,0:T(8,128)(2,1)} %bitcast.14), channel_id=1, source_target_pairs={{0,16},{16,0},{32,48},{48,32},{64,80},{80,64},{96,112},{112,96},{1... | collective-permute-start | bytes 1179656 | tf_op jit(solution)/shard_map/ppermute | solution.py:527
  7.5 2.4 %collective-permute-start.1 = (bf16[3,128,512]{2,1,0:T(8,128)(2,1)}, bf16[3,128,512]{2,1,0:T(8,128)(2,1)S(1)}, u32[]{:S(2)}, u32[]{:S(2)}) collective-permute-start(bf16[3,128,512]{2,1,0:T(8,128)(2,1)} %bitcast.16), channel_id=1, source_target_pairs={{0,96},{16,112},{32,0},{48,16},{64,32},{80,48},{96,64},{112,80},{1... | collective-permute-start | bytes 1179656 | tf_op jit(solution)/shard_map/ppermute | solution.py:527
  9.9 3.0 %collective-permute-done.3.refs_4_ = bf16[3,128,512]{2,1,0:T(8,128)(2,1)S(1)} collective-permute-done((bf16[3,128,512]{2,1,0:T(8,128)(2,1)}, bf16[3,128,512]{2,1,0:T(8,128)(2,1)S(1)}, u32[]{:S(2)}, u32[]{:S(2)}) %collective-permute-start.3) | collective-permute-done | bytes 393248 | tf_op jit(solution)/shard_map/ppermute | solution.py:527
  12.9 3.3 %collective-permute-start.6 = (bf16[3,128,512]{2,1,0:T(8,128)(2,1)S(1)}, bf16[3,128,512]{2,1,0:T(8,128)(2,1)S(1)}, u32[]{:S(2)}, u32[]{:S(2)}) collective-permute-start(bf16[3,128,512]{2,1,0:T(8,128)(2,1)S(1)} %collective-permute-done.3.refs_4_), channel_id=1, source_target_pairs={{0,16},{16,0},{32,48},{48,32},{64,80},{80,64},{96,112},{112,96},{1... | collective-permute-start | bytes 1179656 | tf_op jit(solution)/shard_map/ppermute | solution.py:527
  22.5 3.1 %collective-permute-start.7 = (bf16[64,1024]{1,0:T(8,128)(2,1)S(1)}, bf16[64,1024]{1,0:T(8,128)(2,1)S(1)}, u32[]{:S(2)}, u32[]{:S(2)}) collective-permute-start(bf16[64,1024]{1,0:T(8,128)(2,1)S(1)} %spare_facts.1), channel_id=1, source_target_pairs={{0,16},{16,0},{32,48},{48,32},{64,80},{80,64},{96,112},{112,96},{1... | collective-permute-start | bytes 393224 | tf_op jit(solution)/shard_map/ppermute | solution.py:527
  29.2 2.5 %collective-permute-start.9 = (f32[8,128]{1,0:T(8,128)S(1)}, f32[8,128]{1,0:T(8,128)S(1)}, u32[]{:S(2)}, u32[]{:S(2)}) collective-permute-start(f32[8,128]{1,0:T(8,128)S(1)} %broadcast_in_dim.24.refs_8_), channel_id=1, source_target_pairs={{0,96},{16,112},{32,0},{48,16},{64,32},{80,48},{96,64},{112,80},{1... | collective-permute-start | bytes 12296 | tf_op jit(solution)/shard_map/ppermute | solution.py:527
  32.5 3.8 %unite.1 = (bf16[3,320,512]{2,1,0:T(8,128)(2,1)S(1)}, bf16[3,320,512]{2,1,0:T(8,128)(2,1)S(1)}, bf16[8,8,40,128]{3,2,1,0:T(8,128)(2,1)S(1)}, bf16[8,8,40,128]{3,2,1,0:T(8,128)(2,1)S(1)}, f32[8,512]{1,0:T(8,128)S(1)}) custom-call(bf16[3,128,512]{2,1,0:T(8,128)(2,1)S(1)} %get-tuple-element.37.refs_0_, bf16[3,128,512]{2,1,0:T(8,128)(2,1)S(1)} %collective-permute-done.2.refs_1_, ...), custom_call_target="tpu_custom_call" | custom-call | tf_op jit(solution)/shard_map/unite/pallas_call | solution.py:184
  36.3 3.7 %collective-permute-start.10 = (bf16[8,8,40,128]{3,2,1,0:T(8,128)(2,1)S(1)}, bf16[8,8,40,128]{3,2,1,0:T(8,128)(2,1)S(1)}, u32[]{:S(2)}, u32[]{:S(2)}) collective-permute-start(bf16[8,8,40,128]{3,2,1,0:T(8,128)(2,1)S(1)} %get-tuple-element.46), channel_id=1, source_target_pairs={{0,1},{1,0},{2,3},{3,2},{4,5},{5,4},{6,7},{7,6},{8,9},{9,8},{10,11... | collective-permute-start | bytes 1966088 | tf_op jit(solution)/shard_map/ppermute | solution.py:43
  41.9 22.2 %all_to_all.25.piece_ref = bf16[64,40,128]{2,1,0:T(8,128)(2,1)S(1)} all-to-all(bf16[64,40,128]{2,1,0:T(8,128)(2,1)S(1)} %bitcast.21), channel_id=1, replica_groups=mesh['x'=4,'yh'=2,'z'=4,'yl'=2,'c'=2] {'x','yh','z','yl'}, dimensions={0} | all-to-all | bytes 1310720 | tf_op jit(solution)/shard_map/all_to_all | solution.py:510
  65.0 3.5 %all-to-all-start.1 = ((bf16[8,8,40,128]{3,2,1,0:T(8,128)(2,1)}), bf16[8,8,40,128]{3,2,1,0:T(8,128)(2,1)S(1)}, u32[]{:S(2)}, u32[]{:S(2)}) async-start(bf16[8,8,40,128]{3,2,1,0:T(8,128)(2,1)} %get-tuple-element.49), calls=%async_computation.1 | async-start | bytes 1310720 | tf_op jit(solution)/shard_map/all_to_all | solution.py:555
  69.1 2.3 %collective-permute-start.12 = (bf16[2,64,1024]{2,1,0:T(8,128)(2,1)S(1)}, bf16[2,64,1024]{2,1,0:T(8,128)(2,1)S(1)}, u32[]{:S(2)}, u32[]{:S(2)}) collective-permute-start(bf16[2,64,1024]{2,1,0:T(8,128)(2,1)S(1)} %pad_maximum_fusion.refs_0_), channel_id=1, source_target_pairs={{0,96},{16,112},{32,0},{48,16},{64,32},{80,48},{96,64},{112,80},{1... | collective-permute-start | bytes 786440 | tf_op jit(solution)/shard_map/ppermute | solution.py:527
  71.3 4.4 %collective-permute-done.11.refs_1_ = bf16[2,64,1024]{2,1,0:T(8,128)(2,1)S(1)} collective-permute-done((bf16[2,64,1024]{2,1,0:T(8,128)(2,1)S(1)}, bf16[2,64,1024]{2,1,0:T(8,128)(2,1)S(1)}, u32[]{:S(2)}, u32[]{:S(2)}) %collective-permute-start.11) | collective-permute-done | bytes 262176 | tf_op jit(solution)/shard_map/ppermute | solution.py:527
  75.7 2.4 %all-to-all-done.1.own_ref = bf16[8,8,40,128]{3,2,1,0:T(8,128)(2,1)S(1)} async-done(((bf16[8,8,40,128]{3,2,1,0:T(8,128)(2,1)}), bf16[8,8,40,128]{3,2,1,0:T(8,128)(2,1)S(1)}, u32[]{:S(2)}, u32[]{:S(2)}) %all-to-all-start.1) | async-done | bytes 655392 | tf_op jit(solution)/shard_map/all_to_all | solution.py:555
  78.1 2.9 %collective-permute-start.13 = (bf16[8,8,40,128]{3,2,1,0:T(8,128)(2,1)S(1)}, bf16[8,8,40,128]{3,2,1,0:T(8,128)(2,1)S(1)}, u32[]{:S(2)}, u32[]{:S(2)}) collective-permute-start(bf16[8,8,40,128]{3,2,1,0:T(8,128)(2,1)S(1)} %all-to-all-done.1.own_ref), channel_id=1, source_target_pairs={{0,1},{1,0},{2,3},{3,2},{4,5},{5,4},{6,7},{7,6},{8,9},{9,8},{10,11... | collective-permute-start | bytes 1966088 | tf_op jit(solution)/shard_map/ppermute | solution.py:43
  82.7 7.5 %head_forward.1 = (f32[1024,128]{1,0:T(8,128)S(1)}, f32[8,128]{1,0:T(8,128)S(1)}, bf16[80,8192]{1,0:T(8,128)(2,1)S(1)}, bf16[1024,8192]{1,0:T(8,128)(2,1)S(1)}) custom-call(bf16[8,8,40,128]{3,2,1,0:T(8,128)(2,1)S(1)} %all-to-all-done.1.own_ref, bf16[8,8,40,128]{3,2,1,0:T(8,128)(2,1)S(1)} %collective-permute-done.13.other_ref, f32[1,8192]{1,0:T(1,128)S(1)} %bitcast.18, ...), custom_call_target="tpu_custom_call" | custom-call | flops 4294967296 | bytes 16777216 | tf_op jit(solution)/shard_map/head_forward/pallas_call | solution.py:246
  90.4 2.2 %row_stats.1 = (f32[1024,128]{1,0:T(8,128)S(1)}, f32[8,128]{1,0:T(8,128)S(1)}, f32[8,128]{1,0:T(8,128)S(1)}) custom-call(s32[1]{0:T(128)S(6)} %copy.9.length_ref, f32[1024,128]{1,0:T(8,128)S(1)} %get-tuple-element.52.logit_ref, f32[8,128]{1,0:T(8,128)S(1)} %get-tuple-element.53.scale_ref, bf16[128,1024]{1,0:T(8,128)(2,1)S(1)} %bitcast.11, ...), custom_call_target="tpu_custom_call" | custom-call | tf_op jit(solution)/shard_map/row_stats/pallas_call | solution.py:337
  92.6 9.3 %all_to_all.26.every_ref = f32[16,8,128]{2,1,0:T(8,128)S(1)} all-to-all(f32[16,8,128]{2,1,0:T(8,128)S(1)} %broadcast_in_dim.25), channel_id=1, replica_groups=mesh['x'=4,'yh'=2,'z'=4,'yl'=2,'c'=2] {'z','yl','c'}, dimensions={0} | all-to-all | bytes 131072 | tf_op jit(solution)/shard_map/all_to_all | solution.py:37
  102.0 3.4 %head_backward.1 = (bf16[8,8,48,128]{3,2,1,0:T(8,128)(2,1)S(1)}, bf16[8,8,48,128]{3,2,1,0:T(8,128)(2,1)S(1)}) custom-call(f32[16,8,128]{2,1,0:T(8,128)S(1)} %all_to_all.26.every_ref, f32[1024,128]{1,0:T(8,128)S(1)} %get-tuple-element.52.logit_ref, f32[1024,128]{1,0:T(8,128)S(1)} %get-tuple-element.58.chosen_ref, f32[8,128]{1,0:T(8,128)S(1)} %get-tuple-element.59.side_ref, ...), custom_call_target="tpu_custom_call" | custom-call | tf_op jit(solution)/shard_map/head_backward/pallas_call | solution.py:402
  108.0 21.4 %all_to_all.27.piece_ref = bf16[64,48,128]{2,1,0:T(8,128)(2,1)S(1)} all-to-all(bf16[64,48,128]{2,1,0:T(8,128)(2,1)S(1)} %bitcast.20), channel_id=1, replica_groups=mesh['x'=4,'yh'=2,'z'=4,'yl'=2,'c'=2] {'x','yh','z','yl'}, dimensions={0} | all-to-all | bytes 1572864 | tf_op jit(solution)/shard_map/all_to_all | solution.py:510
  130.3 3.5 %all-to-all-start.4 = ((bf16[8,8,40,128]{3,2,1,0:T(8,128)(2,1)}), bf16[8,8,40,128]{3,2,1,0:T(8,128)(2,1)S(1)}, u32[]{:S(2)}, u32[]{:S(2)}) async-start(bf16[8,8,40,128]{3,2,1,0:T(8,128)(2,1)} %get-tuple-element.64), calls=%async_computation.4 | async-start | bytes 1310720 | tf_op jit(solution)/shard_map/all_to_all | solution.py:568
  136.4 7.3 %all-to-all-done.4.grad_ref = bf16[8,8,40,128]{3,2,1,0:T(8,128)(2,1)S(1)} async-done(((bf16[8,8,40,128]{3,2,1,0:T(8,128)(2,1)}), bf16[8,8,40,128]{3,2,1,0:T(8,128)(2,1)S(1)}, u32[]{:S(2)}, u32[]{:S(2)}) %all-to-all-start.4) | async-done | bytes 655392 | tf_op jit(solution)/shard_map/all_to_all | solution.py:568
  143.7 2.6 %collective-permute-start.16 = (bf16[8,8,40,128]{3,2,1,0:T(8,128)(2,1)S(1)}, bf16[8,8,40,128]{3,2,1,0:T(8,128)(2,1)S(1)}, u32[]{:S(2)}, u32[]{:S(2)}) collective-permute-start(bf16[8,8,40,128]{3,2,1,0:T(8,128)(2,1)S(1)} %all-to-all-done.4.grad_ref), channel_id=1, source_target_pairs={{0,1},{1,0},{2,3},{3,2},{4,5},{5,4},{6,7},{7,6},{8,9},{9,8},{10,11... | collective-permute-start | bytes 1966088 | tf_op jit(solution)/shard_map/ppermute | solution.py:43
  148.1 3.2 %weight_gradient.1 = f32[3,512,1024]{2,1,0:T(8,128)} custom-call(f32[8,128]{1,0:T(8,128)S(1)} %get-tuple-element.59.side_ref, bf16[8,8,40,128]{3,2,1,0:T(8,128)(2,1)S(1)} %collective-permute-done.16.grad_ref, bf16[3,320,512]{2,1,0:T(8,128)(2,1)S(1)} %get-tuple-element.68.rows_ref, f32[3,512,1024]{2,1,0:T(8,128)S(1)} %near_gradient.1.near_ref), custom_call_target="tpu_custom_call" | custom-call | tf_op jit(solution)/shard_map/weight_gradient/pallas_call | solution.py:479
  (49 shorter events, 22.1 us)
Async XLA Ops:
  0.6 12.2 %collective-permute-start.3 = (bf16[3,128,512]{2,1,0:T(8,128)(2,1)}, bf16[3,128,512]{2,1,0:T(8,128)(2,1)S(1)}, u32[]{:S(2)}, u32[]{:S(2)}) collective-permute-start(bf16[3,128,512]{2,1,0:T(8,128)(2,1)} %bitcast.13), channel_id=1, source_target_pairs={{0,64},{16,80},{32,96},{48,112},{64,0},{80,16},{96,32},{112,48},{1... | collective-permute-start | bytes 1179656 | tf_op jit(solution)/shard_map/ppermute | solution.py:527
  4.3 11.9 %collective-permute-start.2 = (bf16[3,128,512]{2,1,0:T(8,128)(2,1)}, bf16[3,128,512]{2,1,0:T(8,128)(2,1)S(1)}, u32[]{:S(2)}, u32[]{:S(2)}) collective-permute-start(bf16[3,128,512]{2,1,0:T(8,128)(2,1)} %bitcast.14), channel_id=1, source_target_pairs={{0,16},{16,0},{32,48},{48,32},{64,80},{80,64},{96,112},{112,96},{1... | collective-permute-start | bytes 1179656 | tf_op jit(solution)/shard_map/ppermute | solution.py:527
  7.2 15.3 %collective-permute-start = (bf16[3,128,512]{2,1,0:T(8,128)(2,1)}, bf16[3,128,512]{2,1,0:T(8,128)(2,1)S(1)}, u32[]{:S(2)}, u32[]{:S(2)}) collective-permute-start(bf16[3,128,512]{2,1,0:T(8,128)(2,1)} %bitcast.15), channel_id=1, source_target_pairs={{0,32},{16,48},{32,64},{48,80},{64,96},{80,112},{96,0},{112,16},{1... | collective-permute-start | bytes 1179656 | tf_op jit(solution)/shard_map/ppermute | solution.py:527
  7.5 18.1 %collective-permute-start.1 = (bf16[3,128,512]{2,1,0:T(8,128)(2,1)}, bf16[3,128,512]{2,1,0:T(8,128)(2,1)S(1)}, u32[]{:S(2)}, u32[]{:S(2)}) collective-permute-start(bf16[3,128,512]{2,1,0:T(8,128)(2,1)} %bitcast.16), channel_id=1, source_target_pairs={{0,96},{16,112},{32,0},{48,16},{64,32},{80,48},{96,64},{112,80},{1... | collective-permute-start | bytes 1179656 | tf_op jit(solution)/shard_map/ppermute | solution.py:527
  12.9 18.9 %collective-permute-start.6 = (bf16[3,128,512]{2,1,0:T(8,128)(2,1)S(1)}, bf16[3,128,512]{2,1,0:T(8,128)(2,1)S(1)}, u32[]{:S(2)}, u32[]{:S(2)}) collective-permute-start(bf16[3,128,512]{2,1,0:T(8,128)(2,1)S(1)} %collective-permute-done.3.refs_4_), channel_id=1, source_target_pairs={{0,16},{16,0},{32,48},{48,32},{64,80},{80,64},{96,112},{112,96},{1... | collective-permute-start | bytes 1179656 | tf_op jit(solution)/shard_map/ppermute | solution.py:527
  16.2 16.3 %collective-permute-start.4 = (bf16[3,128,512]{2,1,0:T(8,128)(2,1)S(1)}, bf16[3,128,512]{2,1,0:T(8,128)(2,1)S(1)}, u32[]{:S(2)}, u32[]{:S(2)}) collective-permute-start(bf16[3,128,512]{2,1,0:T(8,128)(2,1)S(1)} %collective-permute-done.2.refs_1_), channel_id=1, source_target_pairs={{0,32},{16,48},{32,64},{48,80},{64,96},{80,112},{96,0},{112,16},{1... | collective-permute-start | bytes 1179656 | tf_op jit(solution)/shard_map/ppermute | solution.py:527
  17.4 15.1 %collective-permute-start.5 = (bf16[3,128,512]{2,1,0:T(8,128)(2,1)S(1)}, bf16[3,128,512]{2,1,0:T(8,128)(2,1)S(1)}, u32[]{:S(2)}, u32[]{:S(2)}) collective-permute-start(bf16[3,128,512]{2,1,0:T(8,128)(2,1)S(1)} %collective-permute-done.2.refs_1_), channel_id=1, source_target_pairs={{0,96},{16,112},{32,0},{48,16},{64,32},{80,48},{96,64},{112,80},{1... | collective-permute-start | bytes 1179656 | tf_op jit(solution)/shard_map/ppermute | solution.py:527
  22.5 6.7 %collective-permute-start.7 = (bf16[64,1024]{1,0:T(8,128)(2,1)S(1)}, bf16[64,1024]{1,0:T(8,128)(2,1)S(1)}, u32[]{:S(2)}, u32[]{:S(2)}) collective-permute-start(bf16[64,1024]{1,0:T(8,128)(2,1)S(1)} %spare_facts.1), channel_id=1, source_target_pairs={{0,16},{16,0},{32,48},{48,32},{64,80},{80,64},{96,112},{112,96},{1... | collective-permute-start | bytes 393224 | tf_op jit(solution)/shard_map/ppermute | solution.py:527
  25.6 6.1 %collective-permute-start.8 = (f32[8,128]{1,0:T(8,128)S(1)}, f32[8,128]{1,0:T(8,128)S(1)}, u32[]{:S(2)}, u32[]{:S(2)}) collective-permute-start(f32[8,128]{1,0:T(8,128)S(1)} %broadcast_in_dim.24.refs_8_), channel_id=1, source_target_pairs={{0,32},{16,48},{32,64},{48,80},{64,96},{80,112},{96,0},{112,16},{1... | collective-permute-start | bytes 12296 | tf_op jit(solution)/shard_map/ppermute | solution.py:527
  25.9 1.9 %copy-start = (bf16[3,512,1024]{2,1,0:T(8,128)(2,1)S(1)}, bf16[3,512,1024]{2,1,0:T(8,128)(2,1)}, u32[]{:S(2)}) copy-start(bf16[3,512,1024]{2,1,0:T(8,128)(2,1)} %hbm_weight) | copy-start | bytes 9437188
  27.8 1.0 copy-start.3
  29.2 3.2 %collective-permute-start.9 = (f32[8,128]{1,0:T(8,128)S(1)}, f32[8,128]{1,0:T(8,128)S(1)}, u32[]{:S(2)}, u32[]{:S(2)}) collective-permute-start(f32[8,128]{1,0:T(8,128)S(1)} %broadcast_in_dim.24.refs_8_), channel_id=1, source_target_pairs={{0,96},{16,112},{32,0},{48,16},{64,32},{80,48},{96,64},{112,80},{1... | collective-permute-start | bytes 12296 | tf_op jit(solution)/shard_map/ppermute | solution.py:527
  36.3 5.4 %collective-permute-start.10 = (bf16[8,8,40,128]{3,2,1,0:T(8,128)(2,1)S(1)}, bf16[8,8,40,128]{3,2,1,0:T(8,128)(2,1)S(1)}, u32[]{:S(2)}, u32[]{:S(2)}) collective-permute-start(bf16[8,8,40,128]{3,2,1,0:T(8,128)(2,1)S(1)} %get-tuple-element.46), channel_id=1, source_target_pairs={{0,1},{1,0},{2,3},{3,2},{4,5},{5,4},{6,7},{7,6},{8,9},{9,8},{10,11... | collective-permute-start | bytes 1966088 | tf_op jit(solution)/shard_map/ppermute | solution.py:43
  41.9 40.8 %copy-start.4 = (f32[8192]{0:T(1024)S(1)}, f32[8192]{0:T(1024)}, u32[]{:S(2)}) copy-start(f32[8192]{0:T(1024)} %param.10) | copy-start | bytes 98308
  65.0 13.1 %all-to-all-start.1 = ((bf16[8,8,40,128]{3,2,1,0:T(8,128)(2,1)}), bf16[8,8,40,128]{3,2,1,0:T(8,128)(2,1)S(1)}, u32[]{:S(2)}, u32[]{:S(2)}) async-start(bf16[8,8,40,128]{3,2,1,0:T(8,128)(2,1)} %get-tuple-element.49), calls=%async_computation.1 | async-start | bytes 1310720 | tf_op jit(solution)/shard_map/all_to_all | solution.py:555
  68.6 7.1 %collective-permute-start.11 = (bf16[2,64,1024]{2,1,0:T(8,128)(2,1)S(1)}, bf16[2,64,1024]{2,1,0:T(8,128)(2,1)S(1)}, u32[]{:S(2)}, u32[]{:S(2)}) collective-permute-start(bf16[2,64,1024]{2,1,0:T(8,128)(2,1)S(1)} %pad_maximum_fusion.refs_0_), channel_id=1, source_target_pairs={{0,32},{16,48},{32,64},{48,80},{64,96},{80,112},{96,0},{112,16},{1... | collective-permute-start | bytes 786440 | tf_op jit(solution)/shard_map/ppermute | solution.py:527
  69.1 6.7 %collective-permute-start.12 = (bf16[2,64,1024]{2,1,0:T(8,128)(2,1)S(1)}, bf16[2,64,1024]{2,1,0:T(8,128)(2,1)S(1)}, u32[]{:S(2)}, u32[]{:S(2)}) collective-permute-start(bf16[2,64,1024]{2,1,0:T(8,128)(2,1)S(1)} %pad_maximum_fusion.refs_0_), channel_id=1, source_target_pairs={{0,96},{16,112},{32,0},{48,16},{64,32},{80,48},{96,64},{112,80},{1... | collective-permute-start | bytes 786440 | tf_op jit(solution)/shard_map/ppermute | solution.py:527
  78.1 4.6 %collective-permute-start.13 = (bf16[8,8,40,128]{3,2,1,0:T(8,128)(2,1)S(1)}, bf16[8,8,40,128]{3,2,1,0:T(8,128)(2,1)S(1)}, u32[]{:S(2)}, u32[]{:S(2)}) collective-permute-start(bf16[8,8,40,128]{3,2,1,0:T(8,128)(2,1)S(1)} %all-to-all-done.1.own_ref), channel_id=1, source_target_pairs={{0,1},{1,0},{2,3},{3,2},{4,5},{5,4},{6,7},{7,6},{8,9},{9,8},{10,11... | collective-permute-start | bytes 1966088 | tf_op jit(solution)/shard_map/ppermute | solution.py:43
  81.0 9.4 %collective-permute-start.14 = (bf16[2,64,1024]{2,1,0:T(8,128)(2,1)S(1)}, bf16[2,64,1024]{2,1,0:T(8,128)(2,1)S(1)}, u32[]{:S(2)}, u32[]{:S(2)}) collective-permute-start(bf16[2,64,1024]{2,1,0:T(8,128)(2,1)S(1)} %pad_maximum_fusion.refs_0_), channel_id=1, source_target_pairs={{0,64},{16,80},{32,96},{48,112},{64,0},{80,16},{96,32},{112,48},{1... | collective-permute-start | bytes 786440 | tf_op jit(solution)/shard_map/ppermute | solution.py:527
  82.7 7.7 %copy-start.2 = (bf16[1,128,1024]{2,1,0:T(8,128)(2,1)S(1)}, bf16[1,128,1024]{2,1,0:T(8,128)(2,1)}, u32[]{:S(2)}) copy-start(bf16[1,128,1024]{2,1,0:T(8,128)(2,1)} %param.8) | copy-start | bytes 786436
  82.7 7.7 %copy-start.6 = (s32[1,128]{1,0:T(1,128)S(1)}, s32[1,128]{1,0:T(1,128)}, u32[]{:S(2)}) copy-start(s32[1,128]{1,0:T(1,128)} %mask_ref.3) | copy-start | bytes 1540
  105.3 2.4 %collective-permute-start.15 = (bf16[8,8,48,128]{3,2,1,0:T(8,128)(2,1)S(1)}, bf16[8,8,48,128]{3,2,1,0:T(8,128)(2,1)S(1)}, u32[]{:S(2)}, u32[]{:S(2)}) collective-permute-start(bf16[8,8,48,128]{3,2,1,0:T(8,128)(2,1)S(1)} %get-tuple-element.63), channel_id=1, source_target_pairs={{0,1},{1,0},{2,3},{3,2},{4,5},{5,4},{6,7},{7,6},{8,9},{9,8},{10,11... | collective-permute-start | bytes 2359304 | tf_op jit(solution)/shard_map/ppermute | solution.py:43
  130.3 13.3 %all-to-all-start.4 = ((bf16[8,8,40,128]{3,2,1,0:T(8,128)(2,1)}), bf16[8,8,40,128]{3,2,1,0:T(8,128)(2,1)S(1)}, u32[]{:S(2)}, u32[]{:S(2)}) async-start(bf16[8,8,40,128]{3,2,1,0:T(8,128)(2,1)} %get-tuple-element.64), calls=%async_computation.4 | async-start | bytes 1310720 | tf_op jit(solution)/shard_map/all_to_all | solution.py:568
  143.7 4.4 %collective-permute-start.16 = (bf16[8,8,40,128]{3,2,1,0:T(8,128)(2,1)S(1)}, bf16[8,8,40,128]{3,2,1,0:T(8,128)(2,1)S(1)}, u32[]{:S(2)}, u32[]{:S(2)}) collective-permute-start(bf16[8,8,40,128]{3,2,1,0:T(8,128)(2,1)S(1)} %all-to-all-done.4.grad_ref), channel_id=1, source_target_pairs={{0,1},{1,0},{2,3},{3,2},{4,5},{5,4},{6,7},{7,6},{8,9},{9,8},{10,11... | collective-permute-start | bytes 1966088 | tf_op jit(solution)/shard_map/ppermute | solution.py:43
  (2 other events, 1.6 us)

commit v8 on v7

--- a/solution.py
+++ b/solution.py
@@ -541,10 +541,12 @@
     over_left = route(over, 1, 0)
     spare = spare_facts(lengths, loss_mask, near_target)
     pair = jnp.stack([spare, route(spare, 0, 1)])
-    left, right, weight = lax.optimization_barrier((left, right, unite_weight))
-    weight, near = stage(weight, own)
     wide_length = jnp.broadcast_to(later.astype(f32), (8, HALF))
     all_lengths = [wide_length, route(wide_length, 1, 0), route(wide_length, 3, 0)]
+    left, right, weight, all_lengths[1] = lax.optimization_barrier(
+        (left, right, unite_weight, all_lengths[1])
+    )
+    weight, near = stage(weight, own)
     over_far, pair = lax.optimization_barrier((over_far, pair))
     blocks = [near, over, left, right, far, over_left, over_right, over_far]
     near_rows, far_rows, mine, other, slots = unite(blocks, all_lengths, weight)

time: 153 us -> 154 us (level)
  starting transfers between devices: 40.8 us -> 37.7 us
  waiting for transfers between devices: 24.3 us -> 26.8 us
    ppermute x13, starting transfers between devices: 24.1 us -> 21.5 us  [route(): return lax.ppermute(value, GROUP, pairs)]
    ppermute x13, waiting for transfers between devices: 9.54 us -> 12 us  [route(): return lax.ppermute(value, GROUP, pairs)]
  transfers between devices with their start and end apart: 19 -> 19, of which waited for: 10 -> 9; matrix products, arithmetic and copies ran while one was open for 1% -> 1% of each run, Pallas kernels for 6% -> 6%
where the time goes in v8:
time: 154 us; the launch traced here: 153 us
  blocking collectives  54.2 us (35%)
  starting transfers between devices  37.7 us (24%)
  waiting for transfers between devices  26.8 us (17%)
  Pallas kernels  24.3 us (16%)
  local copies, waits for them, and re-layouts  5.03 us (3%)
  between operations  3.96 us (3%)
    all_to_all x2, blocking collectives, gather_sum(): lax.all_to_all(pair.reshape((64,) + pair.shape[2:]), CHIPS, 0, 0, tiled=T...  44.8 us
    ppermute x13, starting transfers between devices, route(): return lax.ppermute(value, GROUP, pairs)  21.5 us
    ppermute x13, waiting for transfers between devices, route(): return lax.ppermute(value, GROUP, pairs)  12 us
    all_to_all x1, blocking collectives, spread(): lax.all_to_all(jnp.broadcast_to(value[None], (count,) + value.shape), axe...  9.33 us
    ppermute x4, starting transfers between devices, swap(): return lax.ppermute(value, axis, [(i, i ^ bit) for i in range(count)])  9.1 us
    pallas_call x1, Pallas kernels, head_forward(): pl.pallas_call(head_kernel, in_specs=[VECTORS] * 3 + [FAR], out_specs=[VE...  7.5 us
    all_to_all x1, waiting for transfers between devices, local(): own_grad = lax.all_to_all(copies, RING, 0, 0, tiled=True)  7.25 us
    ppermute x4, waiting for transfers between devices, swap(): return lax.ppermute(value, axis, [(i, i ^ bit) for i in range(count)])  5.14 us
  transfers between devices with their start and end apart: 19, of which 9 were waited for; matrix products, arithmetic and copies ran while one was open for 1% of the time, Pallas kernels for 6%

profile of v8, /device:TPU:1, one launch (start us, length us, event | category | flops | bytes accessed | tf_op | source)
XLA Modules:
  0.0 153.0 jit_solution(6740359106477758565)
XLA Ops:
  0.6 3.7 %collective-permute-start.2 = (bf16[3,128,512]{2,1,0:T(8,128)(2,1)}, bf16[3,128,512]{2,1,0:T(8,128)(2,1)S(1)}, u32[]{:S(2)}, u32[]{:S(2)}) collective-permute-start(bf16[3,128,512]{2,1,0:T(8,128)(2,1)} %bitcast.13), channel_id=1, source_target_pairs={{0,64},{16,80},{32,96},{48,112},{64,0},{80,16},{96,32},{112,48},{1... | collective-permute-start | bytes 1179656 | tf_op jit(solution)/shard_map/ppermute | solution.py:527
  4.3 2.9 %collective-permute-start.4 = (bf16[3,128,512]{2,1,0:T(8,128)(2,1)}, bf16[3,128,512]{2,1,0:T(8,128)(2,1)S(1)}, u32[]{:S(2)}, u32[]{:S(2)}) collective-permute-start(bf16[3,128,512]{2,1,0:T(8,128)(2,1)} %bitcast.14), channel_id=1, source_target_pairs={{0,16},{16,0},{32,48},{48,32},{64,80},{80,64},{96,112},{112,96},{1... | collective-permute-start | bytes 1179656 | tf_op jit(solution)/shard_map/ppermute | solution.py:527
  7.5 2.4 %collective-permute-start.1 = (bf16[3,128,512]{2,1,0:T(8,128)(2,1)}, bf16[3,128,512]{2,1,0:T(8,128)(2,1)S(1)}, u32[]{:S(2)}, u32[]{:S(2)}) collective-permute-start(bf16[3,128,512]{2,1,0:T(8,128)(2,1)} %bitcast.16), channel_id=1, source_target_pairs={{0,96},{16,112},{32,0},{48,16},{64,32},{80,48},{96,64},{112,80},{1... | collective-permute-start | bytes 1179656 | tf_op jit(solution)/shard_map/ppermute | solution.py:527
  10.6 2.2 %collective-permute-done.2.refs_4_ = bf16[3,128,512]{2,1,0:T(8,128)(2,1)S(1)} collective-permute-done((bf16[3,128,512]{2,1,0:T(8,128)(2,1)}, bf16[3,128,512]{2,1,0:T(8,128)(2,1)S(1)}, u32[]{:S(2)}, u32[]{:S(2)}) %collective-permute-start.2) | collective-permute-done | bytes 393248 | tf_op jit(solution)/shard_map/ppermute | solution.py:527
  12.9 3.3 %collective-permute-start.7 = (bf16[3,128,512]{2,1,0:T(8,128)(2,1)S(1)}, bf16[3,128,512]{2,1,0:T(8,128)(2,1)S(1)}, u32[]{:S(2)}, u32[]{:S(2)}) collective-permute-start(bf16[3,128,512]{2,1,0:T(8,128)(2,1)S(1)} %collective-permute-done.2.refs_4_), channel_id=1, source_target_pairs={{0,16},{16,0},{32,48},{48,32},{64,80},{80,64},{96,112},{112,96},{1... | collective-permute-start | bytes 1179656 | tf_op jit(solution)/shard_map/ppermute | solution.py:527
  17.4 5.2 %collective-permute-done.3.refs_9_ = f32[8,128]{1,0:T(8,128)S(1)} collective-permute-done((f32[8,128]{1,0:T(8,128)S(1)}, f32[8,128]{1,0:T(8,128)S(1)}, u32[]{:S(2)}, u32[]{:S(2)}) %collective-permute-start.3) | collective-permute-done | bytes 4128 | tf_op jit(solution)/shard_map/ppermute | solution.py:527
  24.3 3.2 %collective-permute-start.8 = (bf16[64,1024]{1,0:T(8,128)(2,1)S(1)}, bf16[64,1024]{1,0:T(8,128)(2,1)S(1)}, u32[]{:S(2)}, u32[]{:S(2)}) collective-permute-start(bf16[64,1024]{1,0:T(8,128)(2,1)S(1)} %spare_facts.1), channel_id=1, source_target_pairs={{0,16},{16,0},{32,48},{48,32},{64,80},{80,64},{96,112},{112,96},{1... | collective-permute-start | bytes 393224 | tf_op jit(solution)/shard_map/ppermute | solution.py:527
  32.4 3.8 %unite.1 = (bf16[3,320,512]{2,1,0:T(8,128)(2,1)S(1)}, bf16[3,320,512]{2,1,0:T(8,128)(2,1)S(1)}, bf16[8,8,40,128]{3,2,1,0:T(8,128)(2,1)S(1)}, bf16[8,8,40,128]{3,2,1,0:T(8,128)(2,1)S(1)}, f32[8,512]{1,0:T(8,128)S(1)}) custom-call(bf16[3,128,512]{2,1,0:T(8,128)(2,1)S(1)} %get-tuple-element.39.refs_0_, bf16[3,128,512]{2,1,0:T(8,128)(2,1)S(1)} %collective-permute-done.4.refs_1_, ...), custom_call_target="tpu_custom_call" | custom-call | tf_op jit(solution)/shard_map/unite/pallas_call | solution.py:184
  36.2 3.1 %collective-permute-start.10 = (bf16[8,8,40,128]{3,2,1,0:T(8,128)(2,1)S(1)}, bf16[8,8,40,128]{3,2,1,0:T(8,128)(2,1)S(1)}, u32[]{:S(2)}, u32[]{:S(2)}) collective-permute-start(bf16[8,8,40,128]{3,2,1,0:T(8,128)(2,1)S(1)} %get-tuple-element.48), channel_id=1, source_target_pairs={{0,1},{1,0},{2,3},{3,2},{4,5},{5,4},{6,7},{7,6},{8,9},{9,8},{10,11... | collective-permute-start | bytes 1966088 | tf_op jit(solution)/shard_map/ppermute | solution.py:43
  41.3 23.4 %all_to_all.25.piece_ref = bf16[64,40,128]{2,1,0:T(8,128)(2,1)S(1)} all-to-all(bf16[64,40,128]{2,1,0:T(8,128)(2,1)S(1)} %bitcast.21), channel_id=1, replica_groups=mesh['x'=4,'yh'=2,'z'=4,'yl'=2,'c'=2] {'x','yh','z','yl'}, dimensions={0} | all-to-all | bytes 1310720 | tf_op jit(solution)/shard_map/all_to_all | solution.py:510
  65.6 3.5 %all-to-all-start.1 = ((bf16[8,8,40,128]{3,2,1,0:T(8,128)(2,1)}), bf16[8,8,40,128]{3,2,1,0:T(8,128)(2,1)S(1)}, u32[]{:S(2)}, u32[]{:S(2)}) async-start(bf16[8,8,40,128]{3,2,1,0:T(8,128)(2,1)} %get-tuple-element.51), calls=%async_computation.1 | async-start | bytes 1310720 | tf_op jit(solution)/shard_map/all_to_all | solution.py:557
  69.6 2.3 %collective-permute-start.12 = (bf16[2,64,1024]{2,1,0:T(8,128)(2,1)S(1)}, bf16[2,64,1024]{2,1,0:T(8,128)(2,1)S(1)}, u32[]{:S(2)}, u32[]{:S(2)}) collective-permute-start(bf16[2,64,1024]{2,1,0:T(8,128)(2,1)S(1)} %pad_maximum_fusion.refs_0_), channel_id=1, source_target_pairs={{0,96},{16,112},{32,0},{48,16},{64,32},{80,48},{96,64},{112,80},{1... | collective-permute-start | bytes 786440 | tf_op jit(solution)/shard_map/ppermute | solution.py:527
  71.9 4.4 %collective-permute-done.11.refs_1_ = bf16[2,64,1024]{2,1,0:T(8,128)(2,1)S(1)} collective-permute-done((bf16[2,64,1024]{2,1,0:T(8,128)(2,1)S(1)}, bf16[2,64,1024]{2,1,0:T(8,128)(2,1)S(1)}, u32[]{:S(2)}, u32[]{:S(2)}) %collective-permute-start.11) | collective-permute-done | bytes 262176 | tf_op jit(solution)/shard_map/ppermute | solution.py:527
  76.3 2.4 %all-to-all-done.1.own_ref = bf16[8,8,40,128]{3,2,1,0:T(8,128)(2,1)S(1)} async-done(((bf16[8,8,40,128]{3,2,1,0:T(8,128)(2,1)}), bf16[8,8,40,128]{3,2,1,0:T(8,128)(2,1)S(1)}, u32[]{:S(2)}, u32[]{:S(2)}) %all-to-all-start.1) | async-done | bytes 655392 | tf_op jit(solution)/shard_map/all_to_all | solution.py:557
  78.7 2.9 %collective-permute-start.13 = (bf16[8,8,40,128]{3,2,1,0:T(8,128)(2,1)S(1)}, bf16[8,8,40,128]{3,2,1,0:T(8,128)(2,1)S(1)}, u32[]{:S(2)}, u32[]{:S(2)}) collective-permute-start(bf16[8,8,40,128]{3,2,1,0:T(8,128)(2,1)S(1)} %all-to-all-done.1.own_ref), channel_id=1, source_target_pairs={{0,1},{1,0},{2,3},{3,2},{4,5},{5,4},{6,7},{7,6},{8,9},{9,8},{10,11... | collective-permute-start | bytes 1966088 | tf_op jit(solution)/shard_map/ppermute | solution.py:43
  83.3 7.5 %head_forward.1 = (f32[1024,128]{1,0:T(8,128)S(1)}, f32[8,128]{1,0:T(8,128)S(1)}, bf16[80,8192]{1,0:T(8,128)(2,1)S(1)}, bf16[1024,8192]{1,0:T(8,128)(2,1)S(1)}) custom-call(bf16[8,8,40,128]{3,2,1,0:T(8,128)(2,1)S(1)} %all-to-all-done.1.own_ref, bf16[8,8,40,128]{3,2,1,0:T(8,128)(2,1)S(1)} %collective-permute-done.13.other_ref, f32[1,8192]{1,0:T(1,128)S(1)} %bitcast.18, ...), custom_call_target="tpu_custom_call" | custom-call | flops 4294967296 | bytes 16777216 | tf_op jit(solution)/shard_map/head_forward/pallas_call | solution.py:246
  91.0 2.2 %row_stats.1 = (f32[1024,128]{1,0:T(8,128)S(1)}, f32[8,128]{1,0:T(8,128)S(1)}, f32[8,128]{1,0:T(8,128)S(1)}) custom-call(s32[1]{0:T(128)S(6)} %copy.9.length_ref, f32[1024,128]{1,0:T(8,128)S(1)} %get-tuple-element.54.logit_ref, f32[8,128]{1,0:T(8,128)S(1)} %get-tuple-element.55.scale_ref, bf16[128,1024]{1,0:T(8,128)(2,1)S(1)} %bitcast.11, ...), custom_call_target="tpu_custom_call" | custom-call | tf_op jit(solution)/shard_map/row_stats/pallas_call | solution.py:337
  93.2 9.3 %all_to_all.26.every_ref = f32[16,8,128]{2,1,0:T(8,128)S(1)} all-to-all(f32[16,8,128]{2,1,0:T(8,128)S(1)} %broadcast_in_dim.25), channel_id=1, replica_groups=mesh['x'=4,'yh'=2,'z'=4,'yl'=2,'c'=2] {'z','yl','c'}, dimensions={0} | all-to-all | bytes 131072 | tf_op jit(solution)/shard_map/all_to_all | solution.py:37
  102.5 3.4 %head_backward.1 = (bf16[8,8,48,128]{3,2,1,0:T(8,128)(2,1)S(1)}, bf16[8,8,48,128]{3,2,1,0:T(8,128)(2,1)S(1)}) custom-call(f32[16,8,128]{2,1,0:T(8,128)S(1)} %all_to_all.26.every_ref, f32[1024,128]{1,0:T(8,128)S(1)} %get-tuple-element.54.logit_ref, f32[1024,128]{1,0:T(8,128)S(1)} %get-tuple-element.60.chosen_ref, f32[8,128]{1,0:T(8,128)S(1)} %get-tuple-element.61.side_ref, ...), custom_call_target="tpu_custom_call" | custom-call | tf_op jit(solution)/shard_map/head_backward/pallas_call | solution.py:402
  108.5 21.4 %all_to_all.27.piece_ref = bf16[64,48,128]{2,1,0:T(8,128)(2,1)S(1)} all-to-all(bf16[64,48,128]{2,1,0:T(8,128)(2,1)S(1)} %bitcast.20), channel_id=1, replica_groups=mesh['x'=4,'yh'=2,'z'=4,'yl'=2,'c'=2] {'x','yh','z','yl'}, dimensions={0} | all-to-all | bytes 1572864 | tf_op jit(solution)/shard_map/all_to_all | solution.py:510
  130.9 3.5 %all-to-all-start.4 = ((bf16[8,8,40,128]{3,2,1,0:T(8,128)(2,1)}), bf16[8,8,40,128]{3,2,1,0:T(8,128)(2,1)S(1)}, u32[]{:S(2)}, u32[]{:S(2)}) async-start(bf16[8,8,40,128]{3,2,1,0:T(8,128)(2,1)} %get-tuple-element.66), calls=%async_computation.4 | async-start | bytes 1310720 | tf_op jit(solution)/shard_map/all_to_all | solution.py:570
  137.0 7.3 %all-to-all-done.4.grad_ref = bf16[8,8,40,128]{3,2,1,0:T(8,128)(2,1)S(1)} async-done(((bf16[8,8,40,128]{3,2,1,0:T(8,128)(2,1)}), bf16[8,8,40,128]{3,2,1,0:T(8,128)(2,1)S(1)}, u32[]{:S(2)}, u32[]{:S(2)}) %all-to-all-start.4) | async-done | bytes 655392 | tf_op jit(solution)/shard_map/all_to_all | solution.py:570
  144.2 2.6 %collective-permute-start.16 = (bf16[8,8,40,128]{3,2,1,0:T(8,128)(2,1)S(1)}, bf16[8,8,40,128]{3,2,1,0:T(8,128)(2,1)S(1)}, u32[]{:S(2)}, u32[]{:S(2)}) collective-permute-start(bf16[8,8,40,128]{3,2,1,0:T(8,128)(2,1)S(1)} %all-to-all-done.4.grad_ref), channel_id=1, source_target_pairs={{0,1},{1,0},{2,3},{3,2},{4,5},{5,4},{6,7},{7,6},{8,9},{9,8},{10,11... | collective-permute-start | bytes 1966088 | tf_op jit(solution)/shard_map/ppermute | solution.py:43
  148.7 3.2 %weight_gradient.1 = f32[3,512,1024]{2,1,0:T(8,128)} custom-call(f32[8,128]{1,0:T(8,128)S(1)} %get-tuple-element.61.side_ref, bf16[8,8,40,128]{3,2,1,0:T(8,128)(2,1)S(1)} %collective-permute-done.16.grad_ref, bf16[3,320,512]{2,1,0:T(8,128)(2,1)S(1)} %get-tuple-element.70.rows_ref, f32[3,512,1024]{2,1,0:T(8,128)S(1)} %near_gradient.1.near_ref), custom_call_target="tpu_custom_call" | custom-call | tf_op jit(solution)/shard_map/weight_gradient/pallas_call | solution.py:479
  (49 shorter events, 20.0 us)
Async XLA Ops:
  0.6 12.2 %collective-permute-start.2 = (bf16[3,128,512]{2,1,0:T(8,128)(2,1)}, bf16[3,128,512]{2,1,0:T(8,128)(2,1)S(1)}, u32[]{:S(2)}, u32[]{:S(2)}) collective-permute-start(bf16[3,128,512]{2,1,0:T(8,128)(2,1)} %bitcast.13), channel_id=1, source_target_pairs={{0,64},{16,80},{32,96},{48,112},{64,0},{80,16},{96,32},{112,48},{1... | collective-permute-start | bytes 1179656 | tf_op jit(solution)/shard_map/ppermute | solution.py:527
  4.3 11.9 %collective-permute-start.4 = (bf16[3,128,512]{2,1,0:T(8,128)(2,1)}, bf16[3,128,512]{2,1,0:T(8,128)(2,1)S(1)}, u32[]{:S(2)}, u32[]{:S(2)}) collective-permute-start(bf16[3,128,512]{2,1,0:T(8,128)(2,1)} %bitcast.14), channel_id=1, source_target_pairs={{0,16},{16,0},{32,48},{48,32},{64,80},{80,64},{96,112},{112,96},{1... | collective-permute-start | bytes 1179656 | tf_op jit(solution)/shard_map/ppermute | solution.py:527
  7.2 17.1 %collective-permute-start = (bf16[3,128,512]{2,1,0:T(8,128)(2,1)}, bf16[3,128,512]{2,1,0:T(8,128)(2,1)S(1)}, u32[]{:S(2)}, u32[]{:S(2)}) collective-permute-start(bf16[3,128,512]{2,1,0:T(8,128)(2,1)} %bitcast.15), channel_id=1, source_target_pairs={{0,32},{16,48},{32,64},{48,80},{64,96},{80,112},{96,0},{112,16},{1... | collective-permute-start | bytes 1179656 | tf_op jit(solution)/shard_map/ppermute | solution.py:527
  7.5 20.1 %collective-permute-start.1 = (bf16[3,128,512]{2,1,0:T(8,128)(2,1)}, bf16[3,128,512]{2,1,0:T(8,128)(2,1)S(1)}, u32[]{:S(2)}, u32[]{:S(2)}) collective-permute-start(bf16[3,128,512]{2,1,0:T(8,128)(2,1)} %bitcast.16), channel_id=1, source_target_pairs={{0,96},{16,112},{32,0},{48,16},{64,32},{80,48},{96,64},{112,80},{1... | collective-permute-start | bytes 1179656 | tf_op jit(solution)/shard_map/ppermute | solution.py:527
  10.5 12.0 %collective-permute-start.3 = (f32[8,128]{1,0:T(8,128)S(1)}, f32[8,128]{1,0:T(8,128)S(1)}, u32[]{:S(2)}, u32[]{:S(2)}) collective-permute-start(f32[8,128]{1,0:T(8,128)S(1)} %broadcast_in_dim.24.refs_8_), channel_id=1, source_target_pairs={{0,32},{16,48},{32,64},{48,80},{64,96},{80,112},{96,0},{112,16},{1... | collective-permute-start | bytes 12296 | tf_op jit(solution)/shard_map/ppermute | solution.py:527
  12.9 19.5 %collective-permute-start.7 = (bf16[3,128,512]{2,1,0:T(8,128)(2,1)S(1)}, bf16[3,128,512]{2,1,0:T(8,128)(2,1)S(1)}, u32[]{:S(2)}, u32[]{:S(2)}) collective-permute-start(bf16[3,128,512]{2,1,0:T(8,128)(2,1)S(1)} %collective-permute-done.2.refs_4_), channel_id=1, source_target_pairs={{0,16},{16,0},{32,48},{48,32},{64,80},{80,64},{96,112},{112,96},{1... | collective-permute-start | bytes 1179656 | tf_op jit(solution)/shard_map/ppermute | solution.py:527
  16.2 16.2 %collective-permute-start.5 = (bf16[3,128,512]{2,1,0:T(8,128)(2,1)S(1)}, bf16[3,128,512]{2,1,0:T(8,128)(2,1)S(1)}, u32[]{:S(2)}, u32[]{:S(2)}) collective-permute-start(bf16[3,128,512]{2,1,0:T(8,128)(2,1)S(1)} %collective-permute-done.4.refs_1_), channel_id=1, source_target_pairs={{0,32},{16,48},{32,64},{48,80},{64,96},{80,112},{96,0},{112,16},{1... | collective-permute-start | bytes 1179656 | tf_op jit(solution)/shard_map/ppermute | solution.py:527
  22.6 9.8 %collective-permute-start.6 = (bf16[3,128,512]{2,1,0:T(8,128)(2,1)S(1)}, bf16[3,128,512]{2,1,0:T(8,128)(2,1)S(1)}, u32[]{:S(2)}, u32[]{:S(2)}) collective-permute-start(bf16[3,128,512]{2,1,0:T(8,128)(2,1)S(1)} %collective-permute-done.4.refs_1_), channel_id=1, source_target_pairs={{0,96},{16,112},{32,0},{48,16},{64,32},{80,48},{96,64},{112,80},{1... | collective-permute-start | bytes 1179656 | tf_op jit(solution)/shard_map/ppermute | solution.py:527
  24.3 8.0 %collective-permute-start.8 = (bf16[64,1024]{1,0:T(8,128)(2,1)S(1)}, bf16[64,1024]{1,0:T(8,128)(2,1)S(1)}, u32[]{:S(2)}, u32[]{:S(2)}) collective-permute-start(bf16[64,1024]{1,0:T(8,128)(2,1)S(1)} %spare_facts.1), channel_id=1, source_target_pairs={{0,16},{16,0},{32,48},{48,32},{64,80},{80,64},{96,112},{112,96},{1... | collective-permute-start | bytes 393224 | tf_op jit(solution)/shard_map/ppermute | solution.py:527
  27.6 4.8 %collective-permute-start.9 = (f32[8,128]{1,0:T(8,128)S(1)}, f32[8,128]{1,0:T(8,128)S(1)}, u32[]{:S(2)}, u32[]{:S(2)}) collective-permute-start(f32[8,128]{1,0:T(8,128)S(1)} %broadcast_in_dim.24.refs_8_), channel_id=1, source_target_pairs={{0,96},{16,112},{32,0},{48,16},{64,32},{80,48},{96,64},{112,80},{1... | collective-permute-start | bytes 12296 | tf_op jit(solution)/shard_map/ppermute | solution.py:527
  29.0 1.9 %copy-start = (bf16[3,512,1024]{2,1,0:T(8,128)(2,1)S(1)}, bf16[3,512,1024]{2,1,0:T(8,128)(2,1)}, u32[]{:S(2)}) copy-start(bf16[3,512,1024]{2,1,0:T(8,128)(2,1)} %hbm_weight) | copy-start | bytes 9437188
  30.9 1.0 copy-start.3
  36.2 4.9 %collective-permute-start.10 = (bf16[8,8,40,128]{3,2,1,0:T(8,128)(2,1)S(1)}, bf16[8,8,40,128]{3,2,1,0:T(8,128)(2,1)S(1)}, u32[]{:S(2)}, u32[]{:S(2)}) collective-permute-start(bf16[8,8,40,128]{3,2,1,0:T(8,128)(2,1)S(1)} %get-tuple-element.48), channel_id=1, source_target_pairs={{0,1},{1,0},{2,3},{3,2},{4,5},{5,4},{6,7},{7,6},{8,9},{9,8},{10,11... | collective-permute-start | bytes 1966088 | tf_op jit(solution)/shard_map/ppermute | solution.py:43
  41.3 42.0 %copy-start.4 = (f32[8192]{0:T(1024)S(1)}, f32[8192]{0:T(1024)}, u32[]{:S(2)}) copy-start(f32[8192]{0:T(1024)} %param.10) | copy-start | bytes 98308
  65.6 13.1 %all-to-all-start.1 = ((bf16[8,8,40,128]{3,2,1,0:T(8,128)(2,1)}), bf16[8,8,40,128]{3,2,1,0:T(8,128)(2,1)S(1)}, u32[]{:S(2)}, u32[]{:S(2)}) async-start(bf16[8,8,40,128]{3,2,1,0:T(8,128)(2,1)} %get-tuple-element.51), calls=%async_computation.1 | async-start | bytes 1310720 | tf_op jit(solution)/shard_map/all_to_all | solution.py:557
  69.2 7.1 %collective-permute-start.11 = (bf16[2,64,1024]{2,1,0:T(8,128)(2,1)S(1)}, bf16[2,64,1024]{2,1,0:T(8,128)(2,1)S(1)}, u32[]{:S(2)}, u32[]{:S(2)}) collective-permute-start(bf16[2,64,1024]{2,1,0:T(8,128)(2,1)S(1)} %pad_maximum_fusion.refs_0_), channel_id=1, source_target_pairs={{0,32},{16,48},{32,64},{48,80},{64,96},{80,112},{96,0},{112,16},{1... | collective-permute-start | bytes 786440 | tf_op jit(solution)/shard_map/ppermute | solution.py:527
  69.6 6.7 %collective-permute-start.12 = (bf16[2,64,1024]{2,1,0:T(8,128)(2,1)S(1)}, bf16[2,64,1024]{2,1,0:T(8,128)(2,1)S(1)}, u32[]{:S(2)}, u32[]{:S(2)}) collective-permute-start(bf16[2,64,1024]{2,1,0:T(8,128)(2,1)S(1)} %pad_maximum_fusion.refs_0_), channel_id=1, source_target_pairs={{0,96},{16,112},{32,0},{48,16},{64,32},{80,48},{96,64},{112,80},{1... | collective-permute-start | bytes 786440 | tf_op jit(solution)/shard_map/ppermute | solution.py:527
  78.7 4.6 %collective-permute-start.13 = (bf16[8,8,40,128]{3,2,1,0:T(8,128)(2,1)S(1)}, bf16[8,8,40,128]{3,2,1,0:T(8,128)(2,1)S(1)}, u32[]{:S(2)}, u32[]{:S(2)}) collective-permute-start(bf16[8,8,40,128]{3,2,1,0:T(8,128)(2,1)S(1)} %all-to-all-done.1.own_ref), channel_id=1, source_target_pairs={{0,1},{1,0},{2,3},{3,2},{4,5},{5,4},{6,7},{7,6},{8,9},{9,8},{10,11... | collective-permute-start | bytes 1966088 | tf_op jit(solution)/shard_map/ppermute | solution.py:43
  81.5 9.4 %collective-permute-start.14 = (bf16[2,64,1024]{2,1,0:T(8,128)(2,1)S(1)}, bf16[2,64,1024]{2,1,0:T(8,128)(2,1)S(1)}, u32[]{:S(2)}, u32[]{:S(2)}) collective-permute-start(bf16[2,64,1024]{2,1,0:T(8,128)(2,1)S(1)} %pad_maximum_fusion.refs_0_), channel_id=1, source_target_pairs={{0,64},{16,80},{32,96},{48,112},{64,0},{80,16},{96,32},{112,48},{1... | collective-permute-start | bytes 786440 | tf_op jit(solution)/shard_map/ppermute | solution.py:527
  83.3 7.7 %copy-start.2 = (bf16[1,128,1024]{2,1,0:T(8,128)(2,1)S(1)}, bf16[1,128,1024]{2,1,0:T(8,128)(2,1)}, u32[]{:S(2)}) copy-start(bf16[1,128,1024]{2,1,0:T(8,128)(2,1)} %param.8) | copy-start | bytes 786436
  83.3 7.7 %copy-start.6 = (s32[1,128]{1,0:T(1,128)S(1)}, s32[1,128]{1,0:T(1,128)}, u32[]{:S(2)}) copy-start(s32[1,128]{1,0:T(1,128)} %mask_ref.3) | copy-start | bytes 1540
  105.9 2.4 %collective-permute-start.15 = (bf16[8,8,48,128]{3,2,1,0:T(8,128)(2,1)S(1)}, bf16[8,8,48,128]{3,2,1,0:T(8,128)(2,1)S(1)}, u32[]{:S(2)}, u32[]{:S(2)}) collective-permute-start(bf16[8,8,48,128]{3,2,1,0:T(8,128)(2,1)S(1)} %get-tuple-element.65), channel_id=1, source_target_pairs={{0,1},{1,0},{2,3},{3,2},{4,5},{5,4},{6,7},{7,6},{8,9},{9,8},{10,11... | collective-permute-start | bytes 2359304 | tf_op jit(solution)/shard_map/ppermute | solution.py:43
  130.9 13.3 %all-to-all-start.4 = ((bf16[8,8,40,128]{3,2,1,0:T(8,128)(2,1)}), bf16[8,8,40,128]{3,2,1,0:T(8,128)(2,1)S(1)}, u32[]{:S(2)}, u32[]{:S(2)}) async-start(bf16[8,8,40,128]{3,2,1,0:T(8,128)(2,1)} %get-tuple-element.66), calls=%async_computation.4 | async-start | bytes 1310720 | tf_op jit(solution)/shard_map/all_to_all | solution.py:570
  144.2 4.4 %collective-permute-start.16 = (bf16[8,8,40,128]{3,2,1,0:T(8,128)(2,1)S(1)}, bf16[8,8,40,128]{3,2,1,0:T(8,128)(2,1)S(1)}, u32[]{:S(2)}, u32[]{:S(2)}) collective-permute-start(bf16[8,8,40,128]{3,2,1,0:T(8,128)(2,1)S(1)} %all-to-all-done.4.grad_ref), channel_id=1, source_target_pairs={{0,1},{1,0},{2,3},{3,2},{4,5},{5,4},{6,7},{7,6},{8,9},{9,8},{10,11... | collective-permute-start | bytes 1966088 | tf_op jit(solution)/shard_map/ppermute | solution.py:43
  (2 other events, 1.6 us)
